TPU v7x, 128 devices: a whole 4x4x4 slice. The times are simulated.
128 devices in a mesh: pp: 8 (over y, core), ep: 16 (over z, x).
Axes of the slice: x: 4, y: 4, z: 4, core: 2. Of those that a mesh axis runs over, the one named last changes fastest.
Arguments:
- forward_acts: bfloat16 [8, 2048, 3584], P('pp', 'ep'), may hold values from -6 to 6
- forward_ids: int32 [8, 2048, 2], P('pp', 'ep'), may hold values from 0 to 15, all different within a row; in each aligned block of 128 rows (0 to 127, 128 to 255, ..., all dimensions but the last counted through in order) at most 24 rows name the same one
- backward_acts: bfloat16 [8, 2048, 3584], P('pp', 'ep'), may hold values from -6 to 6
- backward_ids: int32 [8, 2048, 2], P('pp', 'ep'), may hold values from 0 to 15, all different within a row; in each aligned block of 128 rows (0 to 127, 128 to 255, ..., all dimensions but the last counted through in order) at most 24 rows name the same one
- upstream_grad: bfloat16 [8, 2048, 3584], P('pp', 'ep'), may hold values from -6 to 6
- gate_up_weight: bfloat16 [8, 16, 3584, 2048], P('pp', 'ep'), may hold values from -0.09375 to 0.09375
- down_weight: bfloat16 [8, 16, 1024, 3584], P('pp', 'ep'), may hold values from -0.1875 to 0.1875
- router_weight: bfloat16 [8, 3584, 16], P('pp'), may hold values from -0.09375 to 0.09375
- mirror_grads: float32 [8, 3584, 16], P('pp', 'ep'), may hold values from -6 to 6
Outputs:
- next_acts: bfloat16 [8, 2048, 3584], P('pp', 'ep')
- next_grads: bfloat16 [8, 2048, 3584], P('pp', 'ep')
- router_grads: float32 [8, 3584, 16], P('pp', 'ep')
Inputs may be any that keep to these rules, and one draw needn't show every extreme that they name: `forward_ids`: each token names 2 different experts. Among the 128 tokens of one device, no expert is named more than 24 times. `backward_ids`: as for forward_ids.
All inputs are finite; a program needn't handle non-finite values.
Results may differ from a plain program's by a relative error of at most 0.015.
Values may be sent and summed in bfloat16 or wider, within the bound.
No kernel may reach another device: no remote copies, remote signals or barrier semaphores. Data moves between devices by JAX's collectives and lax.ppermute only.
A program may use at most 128 MiB of HBM per device.

v0:
```python
import jax
import jax.numpy as jnp
from jax import lax
from jax.sharding import PartitionSpec as P


def shifted(value, axis, steps):
    count = lax.axis_size(axis)
    pairs = [(source, (source + steps) % count) for source in range(count)]
    return lax.ppermute(value, axis, pairs)


def partner(x, axis, stride):
    return lax.ppermute(x, axis, [(i, i ^ 1 << stride) for i in range(lax.axis_size(axis))])


def routing(tokens, ids, router_section, capacity):
    row_count, top_count = ids.shape
    expert_count = router_section.shape[1]
    logits = jnp.dot(tokens, router_section, preferred_element_type=jnp.float32)
    expert_hot = ids[:, :, None] == lax.broadcasted_iota(
        jnp.int32, (row_count, top_count, expert_count), 2
    )
    affinity = jax.nn.sigmoid(jnp.sum(jnp.where(expert_hot, logits[:, None, :], 0.0), axis=-1))
    total = jnp.sum(affinity, axis=1, keepdims=True)
    flat_hot = expert_hot.reshape(row_count * top_count, expert_count).astype(jnp.int32)
    before = jnp.sum((jnp.cumsum(flat_hot, axis=0) - 1) * flat_hot, axis=-1).reshape(
        row_count, top_count
    )
    slot_index = ids * capacity + before
    slot_hot = slot_index[:, :, None] == lax.broadcasted_iota(
        jnp.int32, (row_count, top_count, expert_count * capacity), 2
    )
    picker = jnp.any(slot_hot, axis=1).astype(jnp.bfloat16)
    return (affinity, affinity / total, total, expert_hot, slot_hot, picker)


def dispatch(picker, tokens, expert_count, capacity):
    sent = lax.dot_general(
        picker, tokens, (((0,), (0,)), ((), ())), preferred_element_type=jnp.float32
    )
    return sent.astype(jnp.bfloat16).reshape(expert_count, capacity, tokens.shape[1])


def pick_rows(slot_hot_k, flat_rows):
    return jnp.dot(slot_hot_k.astype(jnp.bfloat16), flat_rows, preferred_element_type=jnp.float32)


def on_device(
    forward_acts,
    forward_ids,
    backward_acts,
    backward_ids,
    upstream_grad,
    gate_up_weight,
    down_weight,
    router_weight,
    mirror_grads,
):
    joined_weight = gate_up_weight[0, 0]
    proj_weight = down_weight[0, 0]
    router_section = router_weight[0]
    tokens_fwd = forward_acts[0]
    tokens_bwd = backward_acts[0]
    upstream = upstream_grad[0]
    row_count, width = tokens_fwd.shape
    top_count = forward_ids.shape[2]
    expert_count = router_section.shape[1]
    hidden_units = proj_weight.shape[0]
    capacity = 3 * row_count * top_count // (2 * lax.axis_size("ep"))
    _, gates_fwd, _, _, slots_fwd, picker_fwd = routing(
        tokens_fwd, forward_ids[0], router_section, capacity
    )
    send_fwd = dispatch(picker_fwd, tokens_fwd, expert_count, capacity)
    received = lax.all_to_all(send_fwd, "ep", split_axis=0, concat_axis=0, tiled=True)
    flat = received.reshape(-1, width)
    joined = jnp.dot(flat, joined_weight, preferred_element_type=jnp.float32)
    pre_gate = joined[:, :hidden_units]
    pre_up = joined[:, hidden_units:]
    hidden = (pre_gate * jax.nn.sigmoid(pre_gate) * pre_up).astype(jnp.bfloat16)
    produced = jnp.dot(hidden, proj_weight, preferred_element_type=jnp.float32).astype(jnp.bfloat16)
    returned = lax.all_to_all(
        produced.reshape(received.shape), "ep", split_axis=0, concat_axis=0, tiled=True
    )
    flat_return = returned.reshape(-1, width)
    mixed = tokens_fwd.astype(jnp.float32)
    for k_index in range(top_count):
        mixed = mixed + gates_fwd[:, k_index : k_index + 1] * pick_rows(
            slots_fwd[:, k_index], flat_return
        )
    layer_out = mixed.astype(jnp.bfloat16)
    next_acts = shifted(layer_out, "pp", 1)
    affinity, gates_bwd, total, hot_bwd, slots_bwd, picker_bwd = routing(
        tokens_bwd, backward_ids[0], router_section, capacity
    )
    send_acts = dispatch(picker_bwd, tokens_bwd, expert_count, capacity)
    send_grads = dispatch(picker_bwd, upstream, expert_count, capacity)
    acts_in = lax.all_to_all(send_acts, "ep", split_axis=0, concat_axis=0, tiled=True)
    grads_in = lax.all_to_all(send_grads, "ep", split_axis=0, concat_axis=0, tiled=True)
    flat = acts_in.reshape(-1, width)
    flat_grad = grads_in.reshape(-1, width)
    joined = jnp.dot(flat, joined_weight, preferred_element_type=jnp.float32)
    pre_gate = joined[:, :hidden_units]
    pre_up = joined[:, hidden_units:]
    squash = jax.nn.sigmoid(pre_gate)
    swished = pre_gate * squash
    hidden = (swished * pre_up).astype(jnp.bfloat16)
    produced = jnp.dot(hidden, proj_weight, preferred_element_type=jnp.float32).astype(jnp.bfloat16)
    hidden_grad = lax.dot_general(
        flat_grad, proj_weight, (((1,), (1,)), ((), ())), preferred_element_type=jnp.float32
    )
    gate_part = hidden_grad * pre_up * squash * (1.0 + pre_gate * (1.0 - squash))
    up_part = hidden_grad * swished
    joined_grad = jnp.concatenate([gate_part, up_part], axis=1).astype(jnp.bfloat16)
    row_grad = lax.dot_general(
        joined_grad, joined_weight, (((1,), (1,)), ((), ())), preferred_element_type=jnp.float32
    )
    row_grad = row_grad.astype(jnp.bfloat16).reshape(acts_in.shape)
    back_rows = lax.all_to_all(row_grad, "ep", split_axis=0, concat_axis=0, tiled=True)
    back_extra = lax.all_to_all(
        produced.reshape(acts_in.shape), "ep", split_axis=0, concat_axis=0, tiled=True
    )
    flat_back = back_rows.reshape(-1, width)
    upstream_f = upstream.astype(jnp.float32)
    grad_total = upstream_f
    gate_terms = []
    for k_index in range(top_count):
        grad_total = grad_total + gates_bwd[:, k_index : k_index + 1] * pick_rows(
            slots_bwd[:, k_index], flat_back
        )
        out_rows = pick_rows(slots_bwd[:, k_index], back_extra.reshape(-1, width))
        gate_terms.append(jnp.sum(upstream_f * out_rows, axis=-1))
    gate_grad = jnp.stack(gate_terms, axis=1)
    mean_term = jnp.sum(gates_bwd * gate_grad, axis=1, keepdims=True)
    logit_rows = (gate_grad - mean_term) / total * affinity * (1.0 - affinity)
    logit_grad = jnp.sum(logit_rows[:, :, None] * hot_bwd.astype(jnp.float32), axis=1)
    router_back = lax.dot_general(
        logit_grad,
        router_section.astype(jnp.float32),
        (((1,), (1,)), ((), ())),
        precision=lax.Precision.HIGHEST,
        preferred_element_type=jnp.float32,
    )
    input_grad = (grad_total + router_back).astype(jnp.bfloat16)
    next_grads = shifted(input_grad, "pp", -1)
    router_part = (
        lax.dot_general(
            tokens_bwd.astype(jnp.float32),
            logit_grad,
            (((0,), (0,)), ((), ())),
            precision=lax.Precision.HIGHEST,
            preferred_element_type=jnp.float32,
        )
        / row_count
    )
    summed = lax.psum_scatter(
        router_part.astype(jnp.bfloat16), "ep", scatter_dimension=0, tiled=True
    ).astype(jnp.float32)
    mirrored = mirror_grads[0]
    levels = lax.axis_size("pp").bit_length() - 1
    for bit_index in range(levels):
        mirrored = partner(mirrored, "pp", bit_index)
    router_grads = summed + mirrored
    return (next_acts[None], next_grads[None], router_grads[None])


def solution(mesh):
    placed = (
        P("pp", "ep", None),
        P("pp", "ep", None),
        P("pp", "ep", None),
        P("pp", "ep", None),
        P("pp", "ep", None),
        P("pp", "ep", None, None),
        P("pp", "ep", None, None),
        P("pp", None, None),
        P("pp", "ep", None),
    )
    return jax.shard_map(
        on_device,
        mesh=mesh,
        in_specs=placed,
        out_specs=(P("pp", "ep", None), P("pp", "ep", None), P("pp", "ep", None)),
        check_vma=False,
    )
```

profile of v0, /device:TPU:0, one launch (start us, length us, event | category | flops | bytes accessed | tf_op | source)
XLA Modules:
  0.0 364.5 jit_solution(12463095282167108373)
XLA Ops:
  7.2 0.9 copy.51
  8.3 0.6 reduce-window.16
  9.7 2.5 convolution_convert_fusion
  12.2 8.1 %all-to-all-start.3 = ((bf16[16,24,3584]{2,1,0:T(8,128)(2,1)}), bf16[16,24,3584]{2,1,0:T(8,128)(2,1)}, u32[]{:S(2)}, u32[]{:S(2)}) async-start(bf16[16,24,3584]{2,1,0:T(8,128)(2,1)} %bitcast.142), calls=%async_computation.3 | async-start | bytes 5505024 | tf_op jit(solution)/shard_map/all_to_all | solution.py:98
  20.3 2.5 convolution_convert_fusion.1
  22.8 39.2 %all-to-all-done.3 = bf16[16,24,3584]{2,1,0:T(8,128)(2,1)} async-done(((bf16[16,24,3584]{2,1,0:T(8,128)(2,1)}), bf16[16,24,3584]{2,1,0:T(8,128)(2,1)}, u32[]{:S(2)}, u32[]{:S(2)}) %all-to-all-start.3) | async-done | bytes 2752544 | tf_op jit(solution)/shard_map/all_to_all | solution.py:98
  62.0 4.6 %all-to-all-start.2 = ((bf16[16,24,3584]{2,1,0:T(8,128)(2,1)}), bf16[16,24,3584]{2,1,0:T(8,128)(2,1)}, u32[]{:S(2)}, u32[]{:S(2)}) async-start(bf16[16,24,3584]{2,1,0:T(8,128)(2,1)} %bitcast.140), calls=%async_computation.2 | async-start | bytes 5505024 | tf_op jit(solution)/shard_map/all_to_all | solution.py:99
  67.1 0.6 reduce-window.14
  68.3 0.3 fusion.43
  68.9 0.3 fusion.39
  69.2 2.6 convolution_convert_fusion.2
  71.8 33.8 %all-to-all-done.2 = bf16[16,24,3584]{2,1,0:T(8,128)(2,1)} async-done(((bf16[16,24,3584]{2,1,0:T(8,128)(2,1)}), bf16[16,24,3584]{2,1,0:T(8,128)(2,1)}, u32[]{:S(2)}, u32[]{:S(2)}) %all-to-all-start.2) | async-done | bytes 2752544 | tf_op jit(solution)/shard_map/all_to_all | solution.py:99
  105.6 4.5 %all-to-all-start = ((bf16[16,24,3584]{2,1,0:T(8,128)(2,1)}), bf16[16,24,3584]{2,1,0:T(8,128)(2,1)}, u32[]{:S(2)}, u32[]{:S(2)}) async-start(bf16[16,24,3584]{2,1,0:T(8,128)(2,1)} %bitcast.141), calls=%async_computation | async-start | bytes 5505024 | tf_op jit(solution)/shard_map/all_to_all | solution.py:75
  110.1 9.9 %fusion.2 = f32[384,2048]{1,0:T(8,128)S(1)} fusion(bf16[384,3584]{1,0:T(8,128)(2,1)} %bitcast.24, bf16[1,1,3584,2048]{3,2,1,0:T(8,128)(2,1)} %param.14), kind=kOutput, calls=%fused_computation.2 | convolution fusion | flops 5637144576 | bytes 20578304 | tf_op jit(solution)/shard_map/dot_general | solution.py:102
  120.0 1.7 copy-done.6
  121.7 7.4 %fusion.15 = bf16[384,3584]{1,0:T(8,128)(2,1)} fusion(bf16[1,1,1024,3584]{3,2,1,0:T(8,128)(2,1)} %param.15, f32[384,2048]{1,0:T(8,128)S(1)} %fusion.2), kind=kOutput, calls=%fused_computation.16 | convolution fusion | flops 2822307840 | bytes 13238272 | tf_op jit(solution)/shard_map/dot_general | solution.py:108
  129.1 18.2 %all-to-all-done = bf16[16,24,3584]{2,1,0:T(8,128)(2,1)} async-done(((bf16[16,24,3584]{2,1,0:T(8,128)(2,1)}), bf16[16,24,3584]{2,1,0:T(8,128)(2,1)}, u32[]{:S(2)}, u32[]{:S(2)}) %all-to-all-start) | async-done | bytes 2752544 | tf_op jit(solution)/shard_map/all_to_all | solution.py:75
  147.3 4.6 %all-to-all-start.5 = ((bf16[16,24,3584]{2,1,0:T(8,128)(2,1)}), bf16[16,24,3584]{2,1,0:T(8,128)(2,1)}, u32[]{:S(2)}, u32[]{:S(2)}) async-start(bf16[16,24,3584]{2,1,0:T(8,128)(2,1)} %bitcast.144), calls=%async_computation.5 | async-start | bytes 5505024 | tf_op jit(solution)/shard_map/all_to_all | solution.py:120
  152.0 8.1 %multiply_convert_fusion.2 = (bf16[384,1024]{1,0:T(8,128)(2,1)S(1)}, bf16[384,1024]{1,0:T(8,128)(2,1)S(1)}) fusion(f32[384,2048]{1,0:T(8,128)} %copy-done.6, bf16[384,3584]{1,0:T(8,128)(2,1)} %bitcast.22, bf16[1,1,1024,3584]{3,2,1,0:T(8,128)(2,1)} %param.15), kind=kOutput, calls=%fused_computation.41 | convolution fusion | flops 2823684096 | bytes 14811136 | tf_op jit(solution)/shard_map/dot_general | solution.py:109
  160.1 10.5 %fusion.18 = bf16[384,3584]{1,0:T(8,128)(2,1)} fusion(bf16[1,1,3584,2048]{3,2,1,0:T(8,128)(2,1)} %param.14, bf16[384,1024]{1,0:T(8,128)(2,1)S(1)} %get-tuple-element.8, bf16[384,1024]{1,0:T(8,128)(2,1)S(1)} %get-tuple-element.7), kind=kOutput, calls=%fused_computation.17 | convolution fusion | flops 5641666560 | bytes 19005440 | tf_op jit(solution)/shard_map/dot_general | solution.py:115
  170.6 19.2 %all-to-all-done.5 = bf16[16,24,3584]{2,1,0:T(8,128)(2,1)} async-done(((bf16[16,24,3584]{2,1,0:T(8,128)(2,1)}), bf16[16,24,3584]{2,1,0:T(8,128)(2,1)}, u32[]{:S(2)}, u32[]{:S(2)}) %all-to-all-start.5) | async-done | bytes 2752544 | tf_op jit(solution)/shard_map/all_to_all | solution.py:120
  189.7 4.5 %all-to-all-start.4 = ((bf16[16,24,3584]{2,1,0:T(8,128)(2,1)}), bf16[16,24,3584]{2,1,0:T(8,128)(2,1)}, u32[]{:S(2)}, u32[]{:S(2)}) async-start(bf16[16,24,3584]{2,1,0:T(8,128)(2,1)} %bitcast.145), calls=%async_computation.4 | async-start | bytes 5505024 | tf_op jit(solution)/shard_map/all_to_all | solution.py:119
  194.2 9.9 %fusion.4 = f32[384,2048]{1,0:T(8,128)S(1)} fusion(bf16[384,3584]{1,0:T(8,128)(2,1)} %bitcast.7, bf16[1,1,3584,2048]{3,2,1,0:T(8,128)(2,1)} %param.14), kind=kOutput, calls=%fused_computation.4 | convolution fusion | flops 5637144576 | bytes 20578304 | tf_op jit(solution)/shard_map/dot_general | solution.py:77
  204.2 7.4 %fusion.12 = bf16[384,3584]{1,0:T(8,128)(2,1)} fusion(bf16[1,1,1024,3584]{3,2,1,0:T(8,128)(2,1)} %param.15, f32[384,2048]{1,0:T(8,128)S(1)} %fusion.4), kind=kOutput, calls=%fused_computation.15 | convolution fusion | flops 2822307840 | bytes 13238272 | tf_op jit(solution)/shard_map/dot_general | solution.py:81
  211.6 20.2 %all-to-all-done.4 = bf16[16,24,3584]{2,1,0:T(8,128)(2,1)} async-done(((bf16[16,24,3584]{2,1,0:T(8,128)(2,1)}), bf16[16,24,3584]{2,1,0:T(8,128)(2,1)}, u32[]{:S(2)}, u32[]{:S(2)}) %all-to-all-start.4) | async-done | bytes 2752544 | tf_op jit(solution)/shard_map/all_to_all | solution.py:119
  231.8 4.5 %all-to-all-start.1 = ((bf16[16,24,3584]{2,1,0:T(8,128)(2,1)}), bf16[16,24,3584]{2,1,0:T(8,128)(2,1)}, u32[]{:S(2)}, u32[]{:S(2)}) async-start(bf16[16,24,3584]{2,1,0:T(8,128)(2,1)} %bitcast.143), calls=%async_computation.1 | async-start | bytes 5505024 | tf_op jit(solution)/shard_map/all_to_all | solution.py:82
  236.3 0.3 reduce-scatter.4.cloned.1.call-start
  236.6 2.5 fusion.35
  239.1 2.5 fusion.36
  241.7 0.9 fusion.48
  242.6 2.4 convolution_multiply_fusion.2
  245.1 3.5 fusion.26
  248.6 1.0 collective-permute-start.1
  249.5 25.0 %all-to-all-done.1 = bf16[16,24,3584]{2,1,0:T(8,128)(2,1)} async-done(((bf16[16,24,3584]{2,1,0:T(8,128)(2,1)}), bf16[16,24,3584]{2,1,0:T(8,128)(2,1)}, u32[]{:S(2)}, u32[]{:S(2)}) %all-to-all-start.1) | async-done | bytes 2752544 | tf_op jit(solution)/shard_map/all_to_all | solution.py:82
  274.5 2.4 convolution_multiply_fusion.4
  276.9 2.5 fusion.27
  279.5 0.5 fusion.29
  280.0 1.2 copy.57
  281.3 1.7 collective-permute-start.2
  283.0 0.8 collective-permute-done.2
  283.8 1.6 collective-permute-start.3
  285.4 2.2 collective-permute-done.3
  287.6 2.9 collective-permute-start.4
  290.5 62.6 %reduce-scatter.4.cloned.1.call-done = bf16[224,16]{1,0:T(8,128)(2,1)} async-done(((bf16[3584,16]{1,0:T(8,128)(2,1)}), bf16[224,16]{1,0:T(8,128)(2,1)}) %reduce-scatter.4.cloned.1.call-update) | async-done | bytes 7184
  353.1 0.9 copy.58
  354.0 0.6 add_bitcast_fusion
  354.6 0.9 copy.67
  355.5 2.2 copy.68
  (53 shorter events, 2.5 us)
Async XLA Ops:
  7.2 2.5 copy-start
  12.2 8.1 %copy-start.1 = (bf16[1,128,3584]{2,1,0:T(8,128)(2,1)S(1)}, bf16[1,128,3584]{2,1,0:T(8,128)(2,1)}, u32[]{:S(2)}) copy-start(bf16[1,128,3584]{2,1,0:T(8,128)(2,1)} %param.13) | copy-start | bytes 2752516
  12.2 49.9 %all-to-all-start.3 = ((bf16[16,24,3584]{2,1,0:T(8,128)(2,1)}), bf16[16,24,3584]{2,1,0:T(8,128)(2,1)}, u32[]{:S(2)}, u32[]{:S(2)}) async-start(bf16[16,24,3584]{2,1,0:T(8,128)(2,1)} %bitcast.142), calls=%async_computation.3 | async-start | bytes 5505024 | tf_op jit(solution)/shard_map/all_to_all | solution.py:98
  62.0 4.6 %copy-start.4 = (s32[1,128,2]{1,2,0:T(2,128)S(1)}, s32[1,128,2]{1,2,0:T(2,128)}, u32[]{:S(2)}) copy-start(s32[1,128,2]{1,2,0:T(2,128)} %param.10) | copy-start | bytes 3076
  62.0 6.3 %copy-start.2 = (bf16[1,128,3584]{2,1,0:T(8,128)(2,1)S(1)}, bf16[1,128,3584]{2,1,0:T(8,128)(2,1)}, u32[]{:S(2)}) copy-start(bf16[1,128,3584]{2,1,0:T(8,128)(2,1)} %param.9) | copy-start | bytes 2752516
  62.0 6.3 %copy-start.3 = (bf16[1,3584,16]{1,2,0:T(8,128)(2,1)S(1)}, bf16[1,3584,16]{1,2,0:T(8,128)(2,1)}, u32[]{:S(2)}) copy-start(bf16[1,3584,16]{1,2,0:T(8,128)(2,1)} %param.16) | copy-start | bytes 344068
  62.0 43.6 %all-to-all-start.2 = ((bf16[16,24,3584]{2,1,0:T(8,128)(2,1)}), bf16[16,24,3584]{2,1,0:T(8,128)(2,1)}, u32[]{:S(2)}, u32[]{:S(2)}) async-start(bf16[16,24,3584]{2,1,0:T(8,128)(2,1)} %bitcast.140), calls=%async_computation.2 | async-start | bytes 5505024 | tf_op jit(solution)/shard_map/all_to_all | solution.py:99
  105.6 41.7 %all-to-all-start = ((bf16[16,24,3584]{2,1,0:T(8,128)(2,1)}), bf16[16,24,3584]{2,1,0:T(8,128)(2,1)}, u32[]{:S(2)}, u32[]{:S(2)}) async-start(bf16[16,24,3584]{2,1,0:T(8,128)(2,1)} %bitcast.141), calls=%async_computation | async-start | bytes 5505024 | tf_op jit(solution)/shard_map/all_to_all | solution.py:75
  120.0 1.7 copy-start.6
  147.3 42.5 %all-to-all-start.5 = ((bf16[16,24,3584]{2,1,0:T(8,128)(2,1)}), bf16[16,24,3584]{2,1,0:T(8,128)(2,1)}, u32[]{:S(2)}, u32[]{:S(2)}) async-start(bf16[16,24,3584]{2,1,0:T(8,128)(2,1)} %bitcast.144), calls=%async_computation.5 | async-start | bytes 5505024 | tf_op jit(solution)/shard_map/all_to_all | solution.py:120
  189.7 42.1 %all-to-all-start.4 = ((bf16[16,24,3584]{2,1,0:T(8,128)(2,1)}), bf16[16,24,3584]{2,1,0:T(8,128)(2,1)}, u32[]{:S(2)}, u32[]{:S(2)}) async-start(bf16[16,24,3584]{2,1,0:T(8,128)(2,1)} %bitcast.145), calls=%async_computation.4 | async-start | bytes 5505024 | tf_op jit(solution)/shard_map/all_to_all | solution.py:119
  231.8 42.7 %all-to-all-start.1 = ((bf16[16,24,3584]{2,1,0:T(8,128)(2,1)}), bf16[16,24,3584]{2,1,0:T(8,128)(2,1)}, u32[]{:S(2)}, u32[]{:S(2)}) async-start(bf16[16,24,3584]{2,1,0:T(8,128)(2,1)} %bitcast.143), calls=%async_computation.1 | async-start | bytes 5505024 | tf_op jit(solution)/shard_map/all_to_all | solution.py:82
  236.3 116.8 %reduce-scatter.4.cloned.1.call-start = ((), (), s32[]{:S(2)}) async-start(), calls=%async_computation.7 | async-start | bytes 974848
  248.6 106.0 %collective-permute-start.1 = (bf16[128,3584]{1,0:T(8,128)(2,1)}, bf16[128,3584]{1,0:T(8,128)(2,1)}, u32[]{:S(2)}, u32[]{:S(2)}) collective-permute-start(bf16[128,3584]{1,0:T(8,128)(2,1)} %fusion.26), channel_id=1, source_target_pairs={{0,112},{16,0},{32,16},{48,32},{64,48},{80,64},{96,80},{112,96},{1... | collective-permute-start | bytes 2752520 | tf_op jit(solution)/shard_map/ppermute | solution.py:10
  279.5 1.8 copy-start.5
  279.5 75.1 %collective-permute-start = (bf16[128,3584]{1,0:T(8,128)(2,1)S(1)}, bf16[128,3584]{1,0:T(8,128)(2,1)S(1)}, u32[]{:S(2)}, u32[]{:S(2)}) collective-permute-start(bf16[128,3584]{1,0:T(8,128)(2,1)S(1)} %fusion.27), channel_id=1, source_target_pairs={{0,16},{16,32},{32,48},{48,64},{64,80},{80,96},{96,112},{112,0},{1... | collective-permute-start | bytes 2752520 | tf_op jit(solution)/shard_map/ppermute | solution.py:10
  281.3 2.6 collective-permute-start.2
  283.8 3.7 %collective-permute-start.3 = (f32[224,16]{0,1:T(8,128)S(1)}, f32[224,16]{0,1:T(8,128)S(1)}, u32[]{:S(2)}, u32[]{:S(2)}) collective-permute-start(f32[224,16]{0,1:T(8,128)S(1)} %collective-permute-done.2), channel_id=1, source_target_pairs={{0,32},{16,48},{32,0},{48,16},{64,96},{80,112},{96,64},{112,80},{1... | collective-permute-start | bytes 43016 | tf_op jit(solution)/shard_map/ppermute | solution.py:14
  287.6 66.4 %collective-permute-start.4 = (f32[224,16]{0,1:T(8,128)S(1)}, f32[224,16]{0,1:T(8,128)S(1)}, u32[]{:S(2)}, u32[]{:S(2)}) collective-permute-start(f32[224,16]{0,1:T(8,128)S(1)} %collective-permute-done.3), channel_id=1, source_target_pairs={{0,64},{16,80},{32,96},{48,112},{64,0},{80,16},{96,32},{112,48},{1... | collective-permute-start | bytes 43016 | tf_op jit(solution)/shard_map/ppermute | solution.py:14
Sparse Core Ops, SparseCore 0:
  281.4 71.6 reduce-scatter.3
where the time goes:
time: 365 us
  waiting for transfers between devices  221 us (61%)
  matrix products  78.8 us (22%)
  starting transfers between devices  38.2 us (10%)
  between operations  14.3 us (4%)
  local copies, waits for them, and re-layouts  9.34 us (3%)
    unnamed x2, waiting for transfers between devices  62.6 us
    all_to_all x1, waiting for transfers between devices, on_device(): lax.all_to_all(send_acts, 'ep', split_axis=0, concat_axis=0, tiled=True)  39.2 us
    all_to_all x1, waiting for transfers between devices, on_device(): lax.all_to_all(send_grads, 'ep', split_axis=0, concat_axis=0, tiled=True)  33.8 us
    all_to_all x1, waiting for transfers between devices, on_device(): lax.all_to_all(produced.reshape(received.shape), 'ep', split_axis=0, conc...  25 us
    all_to_all x1, waiting for transfers between devices, on_device(): lax.all_to_all(row_grad, 'ep', split_axis=0, concat_axis=0, tiled=True)  20.2 us
    dot_general x2, matrix products, on_device(): joined = jnp.dot(flat, joined_weight, preferred_element_type=jnp.float32)  19.8 us
    all_to_all x1, waiting for transfers between devices, on_device(): lax.all_to_all(produced.reshape(acts_in.shape), 'ep', split_axis=0, conca...  19.2 us
    all_to_all x1, waiting for transfers between devices, on_device(): lax.all_to_all(send_fwd, 'ep', split_axis=0, concat_axis=0, tiled=True)  18.2 us
  transfers between devices with their start and end apart: 12, of which 9 were waited for; matrix products, arithmetic and copies ran while one was open for 22% of the time, Pallas kernels for 0%

commit v1 on v0

v1 whole, which is shorter than its diff:
```python
import jax
import jax.numpy as jnp
from jax import lax
from jax.sharding import PartitionSpec as P


def shifted(value, axis, steps):
    count = lax.axis_size(axis)
    pairs = [(source, (source + steps) % count) for source in range(count)]
    return lax.ppermute(value, axis, pairs)


def exchange(value):
    return lax.all_to_all(value, "ep", split_axis=0, concat_axis=0, tiled=True)


def after(value, *earlier):
    return lax.optimization_barrier((value, *earlier))[0]


def split_two(value):
    high = value.astype(jnp.bfloat16)
    low = (value - high.astype(jnp.float32)).astype(jnp.bfloat16)
    return high, low


def gating(tokens, ids, router_section):
    row_count, top_count = ids.shape
    expert_count = router_section.shape[1]
    logits = jnp.dot(tokens, router_section, preferred_element_type=jnp.float32)
    expert_hot = ids[:, :, None] == lax.broadcasted_iota(
        jnp.int32, (row_count, top_count, expert_count), 2
    )
    affinity = jax.nn.sigmoid(jnp.sum(jnp.where(expert_hot, logits[:, None, :], 0.0), axis=-1))
    total = jnp.sum(affinity, axis=1, keepdims=True)
    return affinity, affinity / total, total, expert_hot


def slots(ids, expert_count, capacity):
    row_count, top_count = ids.shape
    flat_hot = (
        ids.reshape(-1, 1) == lax.broadcasted_iota(jnp.int32, (row_count * top_count, expert_count), 1)
    ).astype(jnp.bfloat16)
    entries = row_count * top_count
    earlier = (
        lax.broadcasted_iota(jnp.int32, (entries, entries), 1)
        < lax.broadcasted_iota(jnp.int32, (entries, entries), 0)
    ).astype(jnp.bfloat16)
    counts = jnp.dot(earlier, flat_hot, preferred_element_type=jnp.float32)
    before = jnp.sum(counts * flat_hot.astype(jnp.float32), axis=1).astype(jnp.int32)
    slot_index = ids * capacity + before.reshape(row_count, top_count)
    return slot_index[:, :, None] == lax.broadcasted_iota(
        jnp.int32, (row_count, top_count, expert_count * capacity), 2
    )


def pick(slot_hot, values):
    picker = jnp.any(slot_hot, axis=1).astype(jnp.bfloat16)
    return lax.dot_general(
        picker, values, (((0,), (0,)), ((), ())), preferred_element_type=jnp.float32
    ).astype(jnp.bfloat16)


def mixer(slot_hot, gates):
    return jnp.sum(jnp.where(slot_hot, gates[:, :, None], 0.0), axis=1).astype(jnp.bfloat16)


def on_device(
    forward_acts,
    forward_ids,
    backward_acts,
    backward_ids,
    upstream_grad,
    gate_up_weight,
    down_weight,
    router_weight,
    mirror_grads,
):
    joined_weight = gate_up_weight[0, 0]
    proj_weight = down_weight[0, 0]
    router_section = router_weight[0]
    tokens_fwd = forward_acts[0]
    tokens_bwd = backward_acts[0]
    upstream = upstream_grad[0]
    row_count, width = tokens_fwd.shape
    top_count = forward_ids.shape[2]
    expert_count = router_section.shape[1]
    hidden_units = proj_weight.shape[0]
    ranks = lax.axis_size("ep")
    capacity = 3 * row_count * top_count // (2 * ranks)
    shard = width // ranks
    early = (3 * width // 4) // 128 * 128

    slots_bwd = slots(backward_ids[0], expert_count, capacity)
    sent_bwd = pick(slots_bwd, jnp.concatenate([tokens_bwd, upstream], axis=1))
    got_bwd = exchange(sent_bwd)

    slots_fwd = slots(forward_ids[0], expert_count, capacity)
    sent_fwd = pick(slots_fwd, tokens_fwd)
    got_fwd = exchange(after(sent_fwd, got_bwd))

    joined = jnp.dot(got_bwd[:, :width], joined_weight, preferred_element_type=jnp.float32)
    pre_gate = joined[:, :hidden_units]
    pre_up = joined[:, hidden_units:]
    squash = jax.nn.sigmoid(pre_gate)
    swished = pre_gate * squash
    hidden = (swished * pre_up).astype(jnp.bfloat16).astype(jnp.float32)
    hidden_grad = lax.dot_general(
        got_bwd[:, width:], proj_weight, (((1,), (1,)), ((), ())), preferred_element_type=jnp.float32
    )
    gate_high, gate_low = split_two(jnp.sum(hidden * hidden_grad, axis=1, keepdims=True))
    gate_part = hidden_grad * pre_up * squash * (1.0 + pre_gate * (1.0 - squash))
    up_part = hidden_grad * swished
    joined_grad = jnp.concatenate([gate_part, up_part], axis=1).astype(jnp.bfloat16)
    row_grad = lax.dot_general(
        joined_grad, joined_weight, (((1,), (1,)), ((), ())), preferred_element_type=jnp.float32
    ).astype(jnp.bfloat16)
    extra = jnp.concatenate(
        [gate_high, gate_low, jnp.zeros((row_grad.shape[0], 126), jnp.bfloat16)], axis=1
    )
    back = exchange(after(jnp.concatenate([row_grad, extra], axis=1), got_fwd))

    joined = jnp.dot(got_fwd, joined_weight, preferred_element_type=jnp.float32)
    pre_gate = joined[:, :hidden_units]
    pre_up = joined[:, hidden_units:]
    hidden_fwd = (pre_gate * jax.nn.sigmoid(pre_gate) * pre_up).astype(jnp.bfloat16)
    produced = jnp.dot(hidden_fwd, proj_weight, preferred_element_type=jnp.float32).astype(jnp.bfloat16)
    returned_early = exchange(after(produced[:, :early], back))

    affinity, gates_bwd, total, hot_bwd = gating(tokens_bwd, backward_ids[0], router_section)
    gate_rows = [
        jnp.dot(
            slots_bwd[:, k].astype(jnp.bfloat16), back[:, width:], preferred_element_type=jnp.float32
        )
        for k in range(top_count)
    ]
    gate_grad = jnp.stack([rows[:, 0] + rows[:, 1] for rows in gate_rows], axis=1)
    mean_term = jnp.sum(gates_bwd * gate_grad, axis=1, keepdims=True)
    logit_rows = (gate_grad - mean_term) / total * affinity * (1.0 - affinity)
    logit_grad = jnp.sum(jnp.where(hot_bwd, logit_rows[:, :, None], 0.0), axis=1)
    logit_pair = jnp.concatenate(split_two(logit_grad), axis=1)
    router_back = lax.dot_general(
        logit_pair,
        jnp.concatenate([router_section, router_section], axis=1),
        (((1,), (1,)), ((), ())),
        preferred_element_type=jnp.float32,
    )
    grad_mix = jnp.dot(
        mixer(slots_bwd, gates_bwd), back[:, :width], preferred_element_type=jnp.float32
    )
    input_grad = (upstream.astype(jnp.float32) + grad_mix + router_back).astype(jnp.bfloat16)
    next_grads = shifted(input_grad, "pp", -1)

    router_pair = lax.dot_general(
        logit_pair, tokens_bwd, (((0,), (0,)), ((), ())), preferred_element_type=jnp.float32
    )
    router_part = ((router_pair[:expert_count] + router_pair[expert_count:]) / row_count).astype(
        jnp.bfloat16
    )
    wide = -(-shard // 128) * 128
    router_blocks = jnp.pad(
        router_part.reshape(expert_count, ranks, shard).transpose(1, 0, 2),
        ((0, 0), (0, capacity - expert_count), (0, wide - shard)),
    ).reshape(ranks * capacity, wide)

    late = jnp.concatenate([produced[:, early:], router_blocks], axis=1)
    returned_late = exchange(after(late, returned_early))

    _, gates_fwd, _, _ = gating(tokens_fwd, forward_ids[0], router_section)
    mixer_fwd = mixer(slots_fwd, gates_fwd)

    def finish(columns, rows):
        mixed = jnp.dot(mixer_fwd, rows, preferred_element_type=jnp.float32)
        return shifted((columns.astype(jnp.float32) + mixed).astype(jnp.bfloat16), "pp", 1)

    next_acts = jnp.concatenate(
        [
            finish(tokens_fwd[:, :early], returned_early),
            finish(tokens_fwd[:, early:], returned_late[:, : width - early]),
        ],
        axis=1,
    )

    count = lax.axis_size("pp")
    mirrored = lax.ppermute(mirror_grads[0], "pp", [(i, count - 1 - i) for i in range(count)])
    summed = jnp.sum(
        returned_late[:, width - early :]
        .reshape(ranks, capacity, wide)[:, :expert_count, :shard]
        .astype(jnp.float32),
        axis=0,
    )
    router_grads = summed.T + mirrored
    return (next_acts[None], next_grads[None], router_grads[None])


def solution(mesh):
    placed = (
        P("pp", "ep", None),
        P("pp", "ep", None),
        P("pp", "ep", None),
        P("pp", "ep", None),
        P("pp", "ep", None),
        P("pp", "ep", None, None),
        P("pp", "ep", None, None),
        P("pp", None, None),
        P("pp", "ep", None),
    )
    return jax.shard_map(
        on_device,
        mesh=mesh,
        in_specs=placed,
        out_specs=(P("pp", "ep", None), P("pp", "ep", None), P("pp", "ep", None)),
        check_vma=False,
    )
```

time: 365 us -> 265 us (0.73)
  waiting for transfers between devices: 221 us -> 144 us
  between operations: 14.3 us -> 0.99 us
  matrix products: 78.8 us -> 65.8 us
  starting transfers between devices: 38.2 us -> 28.9 us
  other arithmetic: 2.6 us -> 10.1 us
  local copies, waits for them, and re-layouts: 9.34 us -> 14.1 us
    unnamed x2 -> x0, waiting for transfers between devices: 62.6 us -> none
    all_to_all x6 -> x5, waiting for transfers between devices: 156 us -> 138 us  [exchange(): return lax.all_to_all(value, 'ep', split_axis=0, concat_axis=0, tiled=True)]
    dot_general x18 -> x17, matrix products: 68.3 us -> 55.1 us  [the longest x1 11.1 us: on_device(): jnp.dot(got_bwd[:, :width], joined_weight, preferred_element_type=jnp.flo...]
    ppermute x2 -> x3, waiting for transfers between devices: 0.01 us -> 5.99 us  [shifted(): return lax.ppermute(value, axis, pairs)]
    concatenate x0 -> x1, local copies, waits for them, and re-layouts: none -> 5.24 us  [on_device(): back = exchange(after(jnp.concatenate([row_grad, extra], axis=1), got_fwd))]
    all_to_all x6 -> x5, starting transfers between devices: 30.8 us -> 25.5 us  [exchange(): return lax.all_to_all(value, 'ep', split_axis=0, concat_axis=0, tiled=True)]
    unnamed x20 -> x21, local copies, waits for them, and re-layouts: 7.86 us -> 3.44 us
  transfers between devices with their start and end apart: 12 -> 9, of which waited for: 9 -> 6; matrix products, arithmetic and copies ran while one was open for 22% -> 24% of each run, Pallas kernels for 0% -> 0%
where the time goes in v1:
time: 265 us; the launch traced here: 264 us
  waiting for transfers between devices  144 us (54%)
  matrix products  65.8 us (25%)
  starting transfers between devices  28.9 us (11%)
  local copies, waits for them, and re-layouts  14.1 us (5%)
  other arithmetic  10.1 us (4%)
    all_to_all x5, waiting for transfers between devices, exchange(): return lax.all_to_all(value, 'ep', split_axis=0, concat_axis=0, tiled=True)  138 us
    all_to_all x5, starting transfers between devices, exchange(): return lax.all_to_all(value, 'ep', split_axis=0, concat_axis=0, tiled=True)  25.5 us
    dot_general x1, matrix products, on_device(): jnp.dot(got_bwd[:, :width], joined_weight, preferred_element_type=jnp.flo...  11.1 us
    dot_general x1, matrix products, on_device(): lax.dot_general(joined_grad, joined_weight, (((1,), (1,)), ((), ())), pre...  10.7 us
    dot_general x1, matrix products, on_device(): joined = jnp.dot(got_fwd, joined_weight, preferred_element_type=jnp.float32)  9.9 us
    dot_general x1, matrix products, on_device(): lax.dot_general(got_bwd[:, width:], proj_weight, (((1,), (1,)), ((), ()))...  9.43 us
    dot_general x2, matrix products, pick(): lax.dot_general(picker, values, (((0,), (0,)), ((), ())), preferred_eleme...  8.1 us
    dot_general x1, matrix products, on_device(): jnp.dot(hidden_fwd, proj_weight, preferred_element_type=jnp.float32)  6.43 us
  transfers between devices with their start and end apart: 9, of which 6 were waited for; matrix products, arithmetic and copies ran while one was open for 24% of the time, Pallas kernels for 0%

profile of v1, /device:TPU:0, one launch (start us, length us, event | category | flops | bytes accessed | tf_op | source)
XLA Modules:
  0.0 264.0 jit_solution(16096275609503325282)
XLA Ops:
  0.6 0.8 copy.61
  1.6 0.2 fusion.31
  2.0 0.8 fusion.41
  2.8 5.5 %convolution_convert_fusion = bf16[384,7168]{1,0:T(8,128)(2,1)} fusion(pred[128,384]{1,0:T(8,128)(4,1)S(1)} %get-tuple-element.20, bf16[128,3584]{1,0:T(8,128)(2,1)} %bitcast.85, bf16[128,3584]{1,0:T(8,128)(2,1)} %bitcast.81), kind=kOutput, calls=%fused_computation.6 | convolution fusion | flops 711065600 | bytes 7389184 | tf_op jit(solution)/shard_map/dot_general | solution.py:59
  8.4 8.2 %all-to-all-start = ((bf16[16,24,7168]{2,1,0:T(8,128)(2,1)}), bf16[16,24,7168]{2,1,0:T(8,128)(2,1)}, u32[]{:S(2)}, u32[]{:S(2)}) async-start(bf16[16,24,7168]{2,1,0:T(8,128)(2,1)} %bitcast.77), calls=%async_computation | async-start | bytes 11010048 | tf_op jit(solution)/shard_map/all_to_all | solution.py:14
  16.9 0.2 fusion.30
  17.4 0.3 fusion.61
  17.8 0.3 fusion.64
  18.1 0.6 select_reduce_fusion.4
  18.9 2.6 convolution_convert_fusion.1
  21.4 77.1 %all-to-all-done = bf16[16,24,7168]{2,1,0:T(8,128)(2,1)} async-done(((bf16[16,24,7168]{2,1,0:T(8,128)(2,1)}), bf16[16,24,7168]{2,1,0:T(8,128)(2,1)}, u32[]{:S(2)}, u32[]{:S(2)}) %all-to-all-start) | async-done | bytes 5505056 | tf_op jit(solution)/shard_map/all_to_all | solution.py:14
  98.5 11.1 %fusion.2 = f32[384,2048]{1,0:T(8,128)} fusion(bf16[1,1,3584,2048]{3,2,1,0:T(8,128)(2,1)} %param.14, bf16[384,7168]{1,0:T(8,128)(2,1)} %bitcast.7), kind=kOutput, calls=%fused_computation.2 | convolution fusion | flops 5637144576 | bytes 20578304 | tf_op jit(solution)/shard_map/dot_general | solution.py:102
  109.6 5.4 %all-to-all-start.1 = ((bf16[16,24,3584]{2,1,0:T(8,128)(2,1)}), bf16[16,24,3584]{2,1,0:T(8,128)(2,1)S(1)}, u32[]{:S(2)}, u32[]{:S(2)}) async-start(bf16[16,24,3584]{2,1,0:T(8,128)(2,1)} %bitcast.8), calls=%async_computation.1 | async-start | bytes 5505024 | tf_op jit(solution)/shard_map/all_to_all | solution.py:14
  115.0 9.4 %multiply_reduce_fusion = (f32[384]{0:T(512)S(1)}, bf16[384,1024]{1,0:T(8,128)(2,1)}, bf16[384,1024]{1,0:T(8,128)(2,1)}) fusion(f32[384,2048]{1,0:T(8,128)} %fusion.2, bf16[1,1,1024,3584]{3,2,1,0:T(8,128)(2,1)} %param.15, bf16[384,7168]{1,0:T(8,128)(2,1)} %bitcast.7), kind=kOutput, calls=%fused_computation.30 | convolution fusion | flops 2825649664 | bytes 14812672 | tf_op jit(solution)/shard_map/dot_general | solution.py:108
  124.8 10.7 %fusion.13 = bf16[384,3584]{1,0:T(8,128)(2,1)} fusion(bf16[1,1,3584,2048]{3,2,1,0:T(8,128)(2,1)} %param.14, bf16[384,1024]{1,0:T(8,128)(2,1)} %get-tuple-element.16, bf16[384,1024]{1,0:T(8,128)(2,1)} %get-tuple-element.17), kind=kOutput, calls=%fused_computation.13 | convolution fusion | flops 5641666560 | bytes 19005440 | tf_op jit(solution)/shard_map/dot_general | solution.py:115
  135.5 5.2 %concatenate.28 = bf16[384,3712]{1,0:T(8,128)(2,1)} concatenate(bf16[384,3584]{1,0:T(8,128)(2,1)} %fusion.13, bf16[384,1]{1,0:T(8,128)(2,1)S(1)} %copy.64, bf16[384,1]{1,0:T(8,128)(2,1)S(1)} %copy.65, bf16[384,126]{1,0:T(8,128)(2,1)S(1)} %broadcast_in_dim.73), dimensions={1} | concatenate | bytes 5701632 | tf_op jit(solution)/shard_map/concatenate | solution.py:121
  140.8 12.4 %all-to-all-done.1 = bf16[16,24,3584]{2,1,0:T(8,128)(2,1)S(1)} async-done(((bf16[16,24,3584]{2,1,0:T(8,128)(2,1)}), bf16[16,24,3584]{2,1,0:T(8,128)(2,1)S(1)}, u32[]{:S(2)}, u32[]{:S(2)}) %all-to-all-start.1) | async-done | bytes 2752544 | tf_op jit(solution)/shard_map/all_to_all | solution.py:14
  153.2 1.6 copy-done.3
  154.8 3.9 %all-to-all-start.2 = ((bf16[16,24,3712]{2,1,0:T(8,128)(2,1)}), bf16[16,24,3712]{2,1,0:T(8,128)(2,1)S(1)}, u32[]{:S(2)}, u32[]{:S(2)}) async-start(bf16[16,24,3712]{2,1,0:T(8,128)(2,1)} %bitcast.12), calls=%async_computation.2 | async-start | bytes 5701632 | tf_op jit(solution)/shard_map/all_to_all | solution.py:14
  158.7 1.1 fusion.69
  159.8 9.9 %fusion.4 = f32[384,2048]{1,0:T(8,128)S(1)} fusion(bf16[384,3584]{1,0:T(8,128)(2,1)} %bitcast.86, bf16[1,1,3584,2048]{3,2,1,0:T(8,128)(2,1)} %param.14), kind=kOutput, calls=%fused_computation.4 | convolution fusion | flops 5637144576 | bytes 20578304 | tf_op jit(solution)/shard_map/dot_general | solution.py:123
  169.7 6.4 %fusion.10 = bf16[384,3584]{1,0:T(8,128)(2,1)S(1)} fusion(bf16[1,1,1024,3584]{3,2,1,0:T(8,128)(2,1)} %param.15, f32[384,2048]{1,0:T(8,128)S(1)} %fusion.4), kind=kOutput, calls=%fused_computation.12 | convolution fusion | flops 2822307840 | bytes 13238272 | tf_op jit(solution)/shard_map/dot_general | solution.py:127
  176.2 1.5 slice.96
  177.6 21.6 %all-to-all-done.2 = bf16[16,24,3712]{2,1,0:T(8,128)(2,1)S(1)} async-done(((bf16[16,24,3712]{2,1,0:T(8,128)(2,1)}), bf16[16,24,3712]{2,1,0:T(8,128)(2,1)S(1)}, u32[]{:S(2)}, u32[]{:S(2)}) %all-to-all-start.2) | async-done | bytes 2850848 | tf_op jit(solution)/shard_map/all_to_all | solution.py:14
  199.3 1.0 fusion.42
  200.2 1.0 fusion.43
  201.2 1.3 multiply_reduce_fusion.1
  202.5 0.7 fusion.55
  203.2 4.4 %all-to-all-start.3 = ((bf16[16,24,2688]{2,1,0:T(8,128)(2,1)}), bf16[16,24,2688]{2,1,0:T(8,128)(2,1)}, u32[]{:S(2)}, u32[]{:S(2)}) async-start(bf16[16,24,2688]{2,1,0:T(8,128)(2,1)} %bitcast.82), calls=%async_computation.3 | async-start | bytes 4128768 | tf_op jit(solution)/shard_map/all_to_all | solution.py:14
  207.7 1.4 fusion.54
  209.1 0.7 fusion.37
  209.8 1.8 reshape.176
  211.5 0.9 copy.69
  212.5 0.8 select_reduce_fusion
  213.4 1.9 convolution_add_fusion.1
  215.3 1.4 fusion.16
  216.6 0.3 collective-permute-start.2
  217.0 1.0 pad_maximum_fusion
  218.0 17.7 %all-to-all-done.3 = bf16[16,24,2688]{2,1,0:T(8,128)(2,1)} async-done(((bf16[16,24,2688]{2,1,0:T(8,128)(2,1)}), bf16[16,24,2688]{2,1,0:T(8,128)(2,1)}, u32[]{:S(2)}, u32[]{:S(2)}) %all-to-all-start.3) | async-done | bytes 2064416 | tf_op jit(solution)/shard_map/all_to_all | solution.py:14
  235.7 3.6 %all-to-all-start.4 = ((bf16[16,24,1152]{2,1,0:T(8,128)(2,1)}), bf16[16,24,1152]{2,1,0:T(8,128)(2,1)S(1)}, u32[]{:S(2)}, u32[]{:S(2)}) async-start(bf16[16,24,1152]{2,1,0:T(8,128)(2,1)} %bitcast.20), calls=%async_computation.4 | async-start | bytes 1769472 | tf_op jit(solution)/shard_map/all_to_all | solution.py:14
  239.5 2.1 fusion.17
  241.7 2.9 %collective-permute-start.3 = (f32[224,16]{0,1:T(8,128)S(1)}, f32[224,16]{0,1:T(8,128)S(1)}, u32[]{:S(2)}, u32[]{:S(2)}) collective-permute-start(f32[224,16]{0,1:T(8,128)S(1)} %bitcast.96), channel_id=1, source_target_pairs={{0,112},{16,96},{32,80},{48,64},{64,48},{80,32},{96,16},{112,0},{1... | collective-permute-start | bytes 43016 | tf_op jit(solution)/shard_map/ppermute | solution.py:185
  244.6 9.4 %all-to-all-done.4 = bf16[16,24,1152]{2,1,0:T(8,128)(2,1)S(1)} async-done(((bf16[16,24,1152]{2,1,0:T(8,128)(2,1)}), bf16[16,24,1152]{2,1,0:T(8,128)(2,1)S(1)}, u32[]{:S(2)}, u32[]{:S(2)}) %all-to-all-start.4) | async-done | bytes 884768 | tf_op jit(solution)/shard_map/all_to_all | solution.py:14
  254.0 0.3 fusion.29
  254.4 0.6 fusion.49
  255.0 6.0 %collective-permute-done.1 = bf16[128,896]{1,0:T(8,128)(2,1)S(1)} collective-permute-done((bf16[128,896]{1,0:T(8,128)(2,1)S(1)}, bf16[128,896]{1,0:T(8,128)(2,1)S(1)}, u32[]{:S(2)}, u32[]{:S(2)}) %collective-permute-start.1) | collective-permute-done | bytes 229408 | tf_op jit(solution)/shard_map/ppermute | solution.py:10
  261.0 2.1 maximum_bitcast_fusion
  263.1 0.9 copy.72
  (52 shorter events, 1.9 us)
Async XLA Ops:
  8.4 8.2 %copy-start.7 = (s32[1,128,2]{1,2,0:T(2,128)S(1)}, s32[1,128,2]{1,2,0:T(2,128)}, u32[]{:S(2)}) copy-start(s32[1,128,2]{1,2,0:T(2,128)} %param.10) | copy-start | bytes 3076
  8.4 9.0 %copy-start = (bf16[1,128,3584]{2,1,0:T(8,128)(2,1)S(1)}, bf16[1,128,3584]{2,1,0:T(8,128)(2,1)}, u32[]{:S(2)}) copy-start(bf16[1,128,3584]{2,1,0:T(8,128)(2,1)} %param.11) | copy-start | bytes 2752516
  8.4 9.0 %copy-start.4 = (bf16[1,3584,16]{1,2,0:T(8,128)(2,1)S(1)}, bf16[1,3584,16]{1,2,0:T(8,128)(2,1)}, u32[]{:S(2)}) copy-start(bf16[1,3584,16]{1,2,0:T(8,128)(2,1)} %param.16) | copy-start | bytes 344068
  8.4 9.4 %copy-start.1 = (bf16[1,128,3584]{2,1,0:T(8,128)(2,1)S(1)}, bf16[1,128,3584]{2,1,0:T(8,128)(2,1)}, u32[]{:S(2)}) copy-start(bf16[1,128,3584]{2,1,0:T(8,128)(2,1)} %param.9) | copy-start | bytes 2752516
  8.4 90.1 %all-to-all-start = ((bf16[16,24,7168]{2,1,0:T(8,128)(2,1)}), bf16[16,24,7168]{2,1,0:T(8,128)(2,1)}, u32[]{:S(2)}, u32[]{:S(2)}) async-start(bf16[16,24,7168]{2,1,0:T(8,128)(2,1)} %bitcast.77), calls=%async_computation | async-start | bytes 11010048 | tf_op jit(solution)/shard_map/all_to_all | solution.py:14
  109.6 43.6 %all-to-all-start.1 = ((bf16[16,24,3584]{2,1,0:T(8,128)(2,1)}), bf16[16,24,3584]{2,1,0:T(8,128)(2,1)S(1)}, u32[]{:S(2)}, u32[]{:S(2)}) async-start(bf16[16,24,3584]{2,1,0:T(8,128)(2,1)} %bitcast.8), calls=%async_computation.1 | async-start | bytes 5505024 | tf_op jit(solution)/shard_map/all_to_all | solution.py:14
  153.2 1.6 copy-start.3
  154.8 44.5 %all-to-all-start.2 = ((bf16[16,24,3712]{2,1,0:T(8,128)(2,1)}), bf16[16,24,3712]{2,1,0:T(8,128)(2,1)S(1)}, u32[]{:S(2)}, u32[]{:S(2)}) async-start(bf16[16,24,3712]{2,1,0:T(8,128)(2,1)} %bitcast.12), calls=%async_computation.2 | async-start | bytes 5701632 | tf_op jit(solution)/shard_map/all_to_all | solution.py:14
  203.2 32.4 %all-to-all-start.3 = ((bf16[16,24,2688]{2,1,0:T(8,128)(2,1)}), bf16[16,24,2688]{2,1,0:T(8,128)(2,1)}, u32[]{:S(2)}, u32[]{:S(2)}) async-start(bf16[16,24,2688]{2,1,0:T(8,128)(2,1)} %bitcast.82), calls=%async_computation.3 | async-start | bytes 4128768 | tf_op jit(solution)/shard_map/all_to_all | solution.py:14
  213.3 1.9 copy-start.5
  215.3 24.1 %copy-start.6 = (f32[128,2]{0,1:T(2,128)S(1)}, f32[128,2]{0,1:T(2,128)}, u32[]{:S(2)}) copy-start(f32[128,2]{0,1:T(2,128)} %select_reduce_fusion.4) | copy-start | bytes 3076
  215.3 24.2 %copy-start.2 = (bf16[1,128,3584]{2,1,0:T(8,128)(2,1)S(1)}, bf16[1,128,3584]{2,1,0:T(8,128)(2,1)}, u32[]{:S(2)}) copy-start(bf16[1,128,3584]{2,1,0:T(8,128)(2,1)} %param.9) | copy-start | bytes 2752516
  216.6 28.0 %collective-permute-start.2 = (bf16[128,3584]{1,0:T(8,128)(2,1)}, bf16[128,3584]{1,0:T(8,128)(2,1)S(1)}, u32[]{:S(2)}, u32[]{:S(2)}) collective-permute-start(bf16[128,3584]{1,0:T(8,128)(2,1)} %fusion.16), channel_id=1, source_target_pairs={{0,112},{16,0},{32,16},{48,32},{64,48},{80,64},{96,80},{112,96},{1... | collective-permute-start | bytes 2752520 | tf_op jit(solution)/shard_map/ppermute | solution.py:10
  218.0 23.7 %copy-start.8 = (f32[1,224,16]{1,2,0:T(8,128)S(1)}, f32[1,224,16]{1,2,0:T(8,128)}, u32[]{:S(2)}) copy-start(f32[1,224,16]{1,2,0:T(8,128)} %param.17) | copy-start | bytes 43012
  235.7 18.3 %all-to-all-start.4 = ((bf16[16,24,1152]{2,1,0:T(8,128)(2,1)}), bf16[16,24,1152]{2,1,0:T(8,128)(2,1)S(1)}, u32[]{:S(2)}, u32[]{:S(2)}) async-start(bf16[16,24,1152]{2,1,0:T(8,128)(2,1)} %bitcast.20), calls=%async_computation.4 | async-start | bytes 1769472 | tf_op jit(solution)/shard_map/all_to_all | solution.py:14
  241.6 13.3 %collective-permute-start = (bf16[128,2688]{1,0:T(8,128)(2,1)S(1)}, bf16[128,2688]{1,0:T(8,128)(2,1)}, u32[]{:S(2)}, u32[]{:S(2)}) collective-permute-start(bf16[128,2688]{1,0:T(8,128)(2,1)S(1)} %fusion.17), channel_id=1, source_target_pairs={{0,16},{16,32},{32,48},{48,64},{64,80},{80,96},{96,112},{112,0},{1... | collective-permute-start | bytes 2064392 | tf_op jit(solution)/shard_map/ppermute | solution.py:10
  241.7 12.7 %collective-permute-start.3 = (f32[224,16]{0,1:T(8,128)S(1)}, f32[224,16]{0,1:T(8,128)S(1)}, u32[]{:S(2)}, u32[]{:S(2)}) collective-permute-start(f32[224,16]{0,1:T(8,128)S(1)} %bitcast.96), channel_id=1, source_target_pairs={{0,112},{16,96},{32,80},{48,64},{64,48},{80,32},{96,16},{112,0},{1... | collective-permute-start | bytes 43016 | tf_op jit(solution)/shard_map/ppermute | solution.py:185
  254.3 6.7 %collective-permute-start.1 = (bf16[128,896]{1,0:T(8,128)(2,1)S(1)}, bf16[128,896]{1,0:T(8,128)(2,1)S(1)}, u32[]{:S(2)}, u32[]{:S(2)}) collective-permute-start(bf16[128,896]{1,0:T(8,128)(2,1)S(1)} %fusion.29), channel_id=1, source_target_pairs={{0,16},{16,32},{32,48},{48,64},{64,80},{80,96},{96,112},{112,0},{1... | collective-permute-start | bytes 688136 | tf_op jit(solution)/shard_map/ppermute | solution.py:10

commit v2 on v1

v2 whole, which is shorter than its diff:
```python
import functools

import jax
import jax.numpy as jnp
from jax import lax
from jax.experimental import pallas as pl
from jax.experimental.pallas import tpu as pltpu
from jax.sharding import PartitionSpec as P

LANES = 128
BF16 = jnp.bfloat16
F32 = jnp.float32


def shifted(value, steps):
    count = lax.axis_size("pp")
    pairs = [(source, (source + steps) % count) for source in range(count)]
    return lax.ppermute(value, "pp", pairs)


def exchange(value):
    return lax.all_to_all(value, "ep", split_axis=0, concat_axis=0, tiled=True)


def split_two(value):
    high = value.astype(BF16)
    low = (value - high.astype(F32)).astype(BF16)
    return high, low


def call(kernel, grid, in_specs, out_specs, out_shape, scratch=(), aliases=None):
    return pl.pallas_call(
        kernel,
        grid=grid,
        in_specs=in_specs,
        out_specs=out_specs,
        out_shape=out_shape,
        scratch_shapes=scratch,
        input_output_aliases=aliases or {},
        compiler_params=pltpu.CompilerParams(vmem_limit_bytes=48 * 1024 * 1024),
        cost_estimate=pl.CostEstimate(flops=1000, bytes_accessed=1000, transcendentals=0),
    )


def slot_rows(ids, expert_count, capacity):
    top_count, tokens = ids.shape
    earlier = (
        lax.broadcasted_iota(jnp.int32, (tokens, tokens), 0)
        < lax.broadcasted_iota(jnp.int32, (tokens, tokens), 1)
    ).astype(F32)
    experts = lax.broadcasted_iota(jnp.int32, (expert_count, tokens), 0)
    taken = jnp.zeros((expert_count, 1), F32)
    rows = []
    for k in range(top_count):
        row = ids[k : k + 1]
        hot = (experts == row).astype(F32)
        before = jnp.dot(hot, earlier, preferred_element_type=F32) + taken
        taken = taken + jnp.sum(hot, axis=1, keepdims=True)
        place = jnp.sum(before * hot, axis=0, keepdims=True)
        rows.append(row * capacity + place.astype(jnp.int32))
    return rows


def picker_of(rows, slot_count):
    tokens = rows[0].shape[1]
    places = lax.broadcasted_iota(jnp.int32, (slot_count, tokens), 0)
    chosen = functools.reduce(jnp.logical_or, [places == row for row in rows])
    return chosen.astype(F32).astype(BF16)


def dispatch_kernel(
    sizes, ids_bwd, ids_fwd, acts_bwd, upstream, acts_fwd, sent_bwd, sent_fwd, slots, picker
):
    steps, expert_count, capacity = sizes
    step = pl.program_id(0)
    slot_count = expert_count * capacity

    @pl.when(step == 0)
    def _():
        rows_bwd = slot_rows(ids_bwd[...], expert_count, capacity)
        rows_fwd = slot_rows(ids_fwd[...], expert_count, capacity)
        picker[0] = picker_of(rows_bwd, slot_count)
        picker[1] = picker_of(rows_fwd, slot_count)
        slots[...] = jnp.concatenate(rows_bwd + rows_fwd, axis=0)

    @pl.when(step < steps)
    def _():
        sent_bwd[...] = jnp.dot(picker[0], acts_bwd[...], preferred_element_type=F32).astype(BF16)

    @pl.when(jnp.logical_and(step >= steps, step < 2 * steps))
    def _():
        sent_bwd[...] = jnp.dot(picker[0], upstream[...], preferred_element_type=F32).astype(BF16)

    @pl.when(step >= 2 * steps)
    def _():
        sent_fwd[...] = jnp.dot(picker[1], acts_fwd[...], preferred_element_type=F32).astype(BF16)


def dispatch(ids_bwd, ids_fwd, acts_bwd, upstream, acts_fwd, expert_count, capacity):
    tokens, width = acts_bwd.shape
    top_count = ids_bwd.shape[0]
    slot_count = expert_count * capacity
    steps = 2
    block = width // steps

    def part(number):
        return pl.BlockSpec(
            (tokens, block), lambda i: (0, jnp.clip(i - number * steps, 0, steps - 1))
        )

    whole = pl.BlockSpec((top_count, tokens), lambda i: (0, 0))
    return call(
        functools.partial(dispatch_kernel, (steps, expert_count, capacity)),
        (3 * steps,),
        [whole, whole, part(0), part(1), part(2)],
        [
            pl.BlockSpec((slot_count, block), lambda i: (0, jnp.minimum(i, 2 * steps - 1))),
            pl.BlockSpec((slot_count, block), lambda i: (0, jnp.clip(i - 2 * steps, 0, steps - 1))),
            pl.BlockSpec((2 * top_count, tokens), lambda i: (0, 0)),
        ],
        [
            jax.ShapeDtypeStruct((slot_count, 2 * width), BF16),
            jax.ShapeDtypeStruct((slot_count, width), BF16),
            jax.ShapeDtypeStruct((2 * top_count, tokens), jnp.int32),
        ],
        [pltpu.VMEM((2, slot_count, tokens), BF16)],
    )(ids_bwd, ids_fwd, acts_bwd, upstream, acts_fwd)


def backward_hidden_kernel(acts, grads, gate_w, up_w, down_w, gate_out, up_out, dots):
    pre_gate = jnp.dot(acts[...], gate_w[...], preferred_element_type=F32)
    pre_up = jnp.dot(acts[...], up_w[...], preferred_element_type=F32)
    hidden_grad = lax.dot_general(
        grads[...], down_w[...], (((1,), (1,)), ((), ())), preferred_element_type=F32
    )
    squash = jax.nn.sigmoid(pre_gate)
    swished = pre_gate * squash
    hidden = (swished * pre_up).astype(BF16).astype(F32)
    gate_out[...] = (
        hidden_grad * pre_up * squash * (1.0 + pre_gate * (1.0 - squash))
    ).astype(BF16)
    up_out[...] = (hidden_grad * swished).astype(BF16)

    @pl.when(pl.program_id(0) == 0)
    def _():
        dots[...] = jnp.zeros_like(dots)

    dots[...] += jnp.sum(hidden * hidden_grad, axis=1, keepdims=True)


def backward_hidden(got, joined_weight, proj_weight):
    slot_count = got.shape[0]
    width = got.shape[1] // 2
    hidden_units = proj_weight.shape[0]
    block = 256
    count = hidden_units // block
    return call(
        backward_hidden_kernel,
        (count,),
        [
            pl.BlockSpec((slot_count, width), lambda j: (0, 0), pipeline_mode=pl.Buffered(1)),
            pl.BlockSpec((slot_count, width), lambda j: (0, 1), pipeline_mode=pl.Buffered(1)),
            pl.BlockSpec((width, block), lambda j: (0, j)),
            pl.BlockSpec((width, block), lambda j: (0, count + j)),
            pl.BlockSpec((block, width), lambda j: (j, 0)),
        ],
        [
            pl.BlockSpec((slot_count, block), lambda j: (0, j)),
            pl.BlockSpec((slot_count, block), lambda j: (0, j)),
            pl.BlockSpec((slot_count, LANES), lambda j: (0, 0)),
        ],
        [
            jax.ShapeDtypeStruct((slot_count, hidden_units), BF16),
            jax.ShapeDtypeStruct((slot_count, hidden_units), BF16),
            jax.ShapeDtypeStruct((slot_count, LANES), F32),
        ],
    )(got, got, joined_weight, joined_weight, proj_weight)


def row_grad_kernel(block, gate_grad, up_grad, weight, dots, out):
    step = pl.program_id(0)
    units = gate_grad.shape[1]
    contract = (((1,), (1,)), ((), ()))
    rows = lax.dot_general(
        gate_grad[...], weight[:, :units], contract, preferred_element_type=F32
    ) + lax.dot_general(up_grad[...], weight[:, units:], contract, preferred_element_type=F32)
    out[:, pl.ds(pl.multiple_of(step * block, block), block)] = rows.astype(BF16)

    @pl.when(step == 0)
    def _():
        high, low = split_two(dots[...])
        lane = lax.broadcasted_iota(jnp.int32, dots.shape, 1)
        extra = jnp.where(lane == 0, high.astype(F32), jnp.where(lane == 1, low.astype(F32), 0.0))
        out[:, out.shape[1] - LANES :] = extra.astype(BF16)


def row_gradient(gate_grad, up_grad, joined_weight, dots):
    slot_count, units = gate_grad.shape
    width = joined_weight.shape[0]
    block = 512
    whole = pl.BlockSpec((slot_count, units), lambda j: (0, 0))
    return call(
        functools.partial(row_grad_kernel, block),
        (width // block,),
        [
            whole,
            whole,
            pl.BlockSpec((block, 2 * units), lambda j: (j, 0)),
            pl.BlockSpec((slot_count, LANES), lambda j: (0, 0)),
        ],
        pl.BlockSpec((slot_count, width + LANES), lambda j: (0, 0)),
        jax.ShapeDtypeStruct((slot_count, width + LANES), BF16),
    )(gate_grad, up_grad, joined_weight, dots)


def forward_hidden_kernel(acts, gate_w, up_w, out):
    pre_gate = jnp.dot(acts[...], gate_w[...], preferred_element_type=F32)
    pre_up = jnp.dot(acts[...], up_w[...], preferred_element_type=F32)
    out[...] = (pre_gate * jax.nn.sigmoid(pre_gate) * pre_up).astype(BF16)


def forward_hidden(got, joined_weight):
    slot_count, width = got.shape
    hidden_units = joined_weight.shape[1] // 2
    block = 256
    count = hidden_units // block
    return call(
        forward_hidden_kernel,
        (count,),
        [
            pl.BlockSpec((slot_count, width), lambda j: (0, 0), pipeline_mode=pl.Buffered(1)),
            pl.BlockSpec((width, block), lambda j: (0, j)),
            pl.BlockSpec((width, block), lambda j: (0, count + j)),
        ],
        pl.BlockSpec((slot_count, block), lambda j: (0, j)),
        jax.ShapeDtypeStruct((slot_count, hidden_units), BF16),
    )(got, joined_weight, joined_weight)


def produce_kernel(hidden, weight, out):
    out[...] = jnp.dot(hidden[...], weight[...], preferred_element_type=F32).astype(BF16)


def produce(hidden, proj_weight, first, columns):
    slot_count, units = hidden.shape
    block = 896
    return call(
        produce_kernel,
        (columns // block,),
        [
            pl.BlockSpec((slot_count, units), lambda j: (0, 0)),
            pl.BlockSpec((units, block), lambda j: (0, first // block + j)),
        ],
        pl.BlockSpec((slot_count, block), lambda j: (0, j)),
        jax.ShapeDtypeStruct((slot_count, columns), BF16),
    )(hidden, proj_weight)


def mix_kernel(mixer, rows, residual, *refs):
    out = refs[-1]
    mixed = lax.dot_general(
        mixer[...], rows[...], (((0,), (0,)), ((), ())), preferred_element_type=F32
    )
    out[...] = (residual[...].astype(F32) + mixed).astype(BF16)


def mix(mixer, rows, residual, first, columns, earlier=None):
    slot_count, tokens = mixer.shape
    block = 896
    in_specs = [
        pl.BlockSpec((slot_count, tokens), lambda j: (0, 0)),
        pl.BlockSpec((slot_count, block), lambda j: (0, j)),
        pl.BlockSpec((tokens, block), lambda j: (0, first // block + j)),
    ]
    operands = [mixer, rows, residual]
    aliases = None
    if earlier is not None:
        in_specs.append(pl.BlockSpec(memory_space=pl.ANY))
        operands.append(earlier)
        aliases = {3: 0}
    return call(
        mix_kernel,
        (columns // block,),
        in_specs,
        pl.BlockSpec((tokens, block), lambda j: (0, first // block + j)),
        jax.ShapeDtypeStruct(residual.shape, BF16),
        aliases=aliases,
    )(*operands)


def gating(tokens, ids, router_section):
    expert_count = router_section.shape[1]
    logits = lax.dot_general(
        router_section, tokens, (((0,), (1,)), ((), ())), preferred_element_type=F32
    )
    hot = ids[:, None, :] == lax.broadcasted_iota(
        jnp.int32, (ids.shape[0], expert_count, ids.shape[1]), 1
    )
    affinity = jax.nn.sigmoid(jnp.sum(jnp.where(hot, logits[None], 0.0), axis=1))
    total = jnp.sum(affinity, axis=0, keepdims=True)
    return affinity, affinity / total, total, hot


def slot_hot(slots, slot_count):
    return slots[:, None, :] == lax.broadcasted_iota(
        jnp.int32, (slots.shape[0], slot_count, slots.shape[1]), 1
    )


def weighted(hot, values):
    return jnp.sum(jnp.where(hot, values[:, None, :], 0.0), axis=0)


def on_device(
    forward_acts,
    forward_ids,
    backward_acts,
    backward_ids,
    upstream_grad,
    gate_up_weight,
    down_weight,
    router_weight,
    mirror_grads,
):
    joined_weight = gate_up_weight[0, 0]
    proj_weight = down_weight[0, 0]
    router_section = router_weight[0]
    tokens_fwd = forward_acts[0]
    tokens_bwd = backward_acts[0]
    upstream = upstream_grad[0]
    ids_fwd = forward_ids[0].T
    ids_bwd = backward_ids[0].T
    mirrored = mirror_grads[0]
    row_count, width = tokens_fwd.shape
    top_count = ids_fwd.shape[0]
    expert_count = router_section.shape[1]
    ranks = lax.axis_size("ep")
    capacity = 3 * row_count * top_count // (2 * ranks)
    slot_count = expert_count * capacity
    shard = width // ranks
    early = width // 2

    sent_bwd, sent_fwd, slots = dispatch(
        ids_bwd, ids_fwd, tokens_bwd, upstream, tokens_fwd, expert_count, capacity
    )
    got_bwd = exchange(sent_bwd)
    (got_bwd, sent_fwd, slots, tokens_fwd, tokens_bwd, upstream, mirrored, router_section) = (
        lax.optimization_barrier(
            (got_bwd, sent_fwd, slots, tokens_fwd, tokens_bwd, upstream, mirrored, router_section)
        )
    )
    got_fwd = exchange(sent_fwd)

    gate_part, up_part, dots = backward_hidden(got_bwd, joined_weight, proj_weight)
    back = exchange(row_gradient(gate_part, up_part, joined_weight, dots))

    hidden = forward_hidden(got_fwd, joined_weight)
    produced_early = shifted(produce(hidden, proj_weight, 0, early), 1)
    produced_late = shifted(produce(hidden, proj_weight, early, width - early), 1)
    residual = shifted(tokens_fwd, 1)
    _, gates_fwd, _, _ = gating(tokens_fwd, ids_fwd, router_section)
    hot_fwd = slot_hot(slots[top_count:], slot_count)
    mixer_fwd = shifted(weighted(hot_fwd, gates_fwd).astype(BF16), 1)
    returned_early = exchange(produced_early)
    next_early = mix(mixer_fwd, returned_early, residual, 0, early)

    affinity, gates_bwd, total, hot_bwd = gating(tokens_bwd, ids_bwd, router_section)
    slots_bwd = slot_hot(slots[:top_count], slot_count)
    gate_rows = back[:, width].astype(F32) + back[:, width + 1].astype(F32)
    gate_grad = jnp.sum(jnp.where(slots_bwd, gate_rows[None, :, None], 0.0), axis=1)
    mean_term = jnp.sum(gates_bwd * gate_grad, axis=0, keepdims=True)
    logit_rows = (gate_grad - mean_term) / total * affinity * (1.0 - affinity)
    logit_grad = weighted(hot_bwd, logit_rows)
    logit_pair = jnp.concatenate(split_two(logit_grad), axis=0)
    router_back = lax.dot_general(
        logit_pair,
        jnp.concatenate([router_section, router_section], axis=1),
        (((0,), (1,)), ((), ())),
        preferred_element_type=F32,
    )
    grad_mix = lax.dot_general(
        weighted(slots_bwd, gates_bwd).astype(BF16),
        back[:, :width],
        (((0,), (0,)), ((), ())),
        preferred_element_type=F32,
    )
    next_grads = shifted((upstream.astype(F32) + grad_mix + router_back).astype(BF16), -1)

    router_pair = jnp.dot(logit_pair, tokens_bwd, preferred_element_type=F32)
    router_part = ((router_pair[:expert_count] + router_pair[expert_count:]) / row_count).astype(
        BF16
    )
    wide = -(-shard // LANES) * LANES
    router_blocks = jnp.pad(
        router_part.reshape(expert_count, ranks, shard).transpose(1, 0, 2),
        ((0, 0), (0, capacity - expert_count), (0, wide - shard)),
    ).reshape(slot_count, wide)
    returned_late = exchange(jnp.concatenate([produced_late, router_blocks], axis=1))
    next_acts = mix(mixer_fwd, returned_late, residual, early, width - early, next_early)

    count = lax.axis_size("pp")
    mirrored = lax.ppermute(mirrored, "pp", [(i, count - 1 - i) for i in range(count)])
    summed = jnp.sum(
        returned_late[:, width - early :]
        .reshape(ranks, capacity, wide)[:, :expert_count, :shard]
        .astype(F32),
        axis=0,
    )
    router_grads = summed.T + mirrored
    return (next_acts[None], next_grads[None], router_grads[None])


def solution(mesh):
    placed = (
        P("pp", "ep", None),
        P("pp", "ep", None),
        P("pp", "ep", None),
        P("pp", "ep", None),
        P("pp", "ep", None),
        P("pp", "ep", None, None),
        P("pp", "ep", None, None),
        P("pp", None, None),
        P("pp", "ep", None),
    )
    return jax.shard_map(
        on_device,
        mesh=mesh,
        in_specs=placed,
        out_specs=(P("pp", "ep", None), P("pp", "ep", None), P("pp", "ep", None)),
        check_vma=False,
    )
```

time: 265 us -> 229 us (0.86)
  waiting for transfers between devices: 144 us -> 58.3 us
  blocking collectives: 0 us -> 73 us
  matrix products: 65.8 us -> 6.34 us
  Pallas kernels: 0 us -> 56.6 us
  local copies, waits for them, and re-layouts: 14.1 us -> 5.86 us
  starting transfers between devices: 28.9 us -> 22.1 us
  other arithmetic: 10.1 us -> 4.94 us
    all_to_all x5 -> x4, waiting for transfers between devices: 138 us -> 38 us  [exchange(): return lax.all_to_all(value, 'ep', split_axis=0, concat_axis=0, tiled=True)]
    all_to_all x0 -> x1, blocking collectives: none -> 73 us  [exchange(): return lax.all_to_all(value, 'ep', split_axis=0, concat_axis=0, tiled=True)]
    dot_general x17 -> x4, matrix products: 64.4 us -> 5.93 us  [the longest x2 3 us: gating(): lax.dot_general(router_section, tokens, (((0,), (1,)), ((), ())), preferr...]
    pallas_call x0 -> x8, Pallas kernels: none -> 56.6 us  [the longest x1 15.1 us: backward_hidden(): call(backward_hidden_kernel, (count,), [pl.BlockSpec((slot_count, width),...]
    ppermute x4 -> x6, waiting for transfers between devices: 5.99 us -> 20.3 us  [the longest x5 20.3 us: shifted(): return lax.ppermute(value, 'pp', pairs)]
    all_to_all x5 -> x4, starting transfers between devices: 25.5 us -> 15.8 us  [exchange(): return lax.all_to_all(value, 'ep', split_axis=0, concat_axis=0, tiled=True)]
    concatenate x1 -> x0, local copies, waits for them, and re-layouts: 5.24 us -> none  [on_device(): back = exchange(after(jnp.concatenate([row_grad, extra], axis=1), got_fwd))]
    reduce_sum x8, other arithmetic: 4.04 us -> 0.36 us  [the longest x3 0.22 us: weighted(): return jnp.sum(jnp.where(hot, values[:, None, :], 0.0), axis=0)]
  transfers between devices with their start and end apart: 9 -> 10, of which waited for: 6 -> 6; matrix products, arithmetic and copies ran while one was open for 24% -> 5% of each run, Pallas kernels for 0% -> 22%
where the time goes in v2:
time: 229 us; the launch traced here: 228 us
  blocking collectives  73 us (32%)
  waiting for transfers between devices  58.3 us (25%)
  Pallas kernels  56.6 us (25%)
  starting transfers between devices  22.1 us (10%)
  matrix products  6.34 us (3%)
  local copies, waits for them, and re-layouts  5.86 us (3%)
  other arithmetic  4.94 us (2%)
    all_to_all x1, blocking collectives, exchange(): return lax.all_to_all(value, 'ep', split_axis=0, concat_axis=0, tiled=True)  73 us
    all_to_all x4, waiting for transfers between devices, exchange(): return lax.all_to_all(value, 'ep', split_axis=0, concat_axis=0, tiled=True)  38 us
    ppermute x5, waiting for transfers between devices, shifted(): return lax.ppermute(value, 'pp', pairs)  20.3 us
    all_to_all x4, starting transfers between devices, exchange(): return lax.all_to_all(value, 'ep', split_axis=0, concat_axis=0, tiled=True)  15.8 us
    pallas_call x1, Pallas kernels, backward_hidden(): call(backward_hidden_kernel, (count,), [pl.BlockSpec((slot_count, width),...  15.1 us
    pallas_call x1, Pallas kernels, row_gradient(): call(functools.partial(row_grad_kernel, block), (width // block,), [whole...  12.2 us
    pallas_call x1, Pallas kernels, forward_hidden(): call(forward_hidden_kernel, (count,), [pl.BlockSpec((slot_count, width),...  9.15 us
    pallas_call x2, Pallas kernels, produce(): call(produce_kernel, (columns // block,), [pl.BlockSpec((slot_count, unit...  7.99 us
  transfers between devices with their start and end apart: 10, of which 6 were waited for; matrix products, arithmetic and copies ran while one was open for 5% of the time, Pallas kernels for 22%

profile of v2, /device:TPU:0, one launch (start us, length us, event | category | flops | bytes accessed | tf_op | source)
XLA Modules:
  0.0 228.0 jit_solution(9674894145235001958)
XLA Ops:
  0.6 0.0 copy-start
  0.6 1.2 copy-done
  1.8 1.2 copy-done.2
  3.0 0.7 copy-done.4
  3.7 0.7 copy-done.6
  4.3 7.3 %shard_map.112 = (bf16[384,7168]{1,0:T(8,128)(2,1)}, bf16[384,3584]{1,0:T(8,128)(2,1)S(1)}, s32[4,128]{1,0:T(4,128)S(1)}) custom-call(s32[2,128]{1,0:T(2,128)S(1)} %bitcast.51, s32[2,128]{1,0:T(2,128)S(1)} %bitcast.54, bf16[128,3584]{1,0:T(8,128)(2,1)S(1)} %bitcast.43, bf16[128,3584]{1,0:T(8,128)(2,1)S(1)} %bitcast.49, bf16[128,3584]{1,0:T(8,128)(2,1)} %bitcast.6.acts_fwd), custom_call_target="tpu_custom_call" | custom-call | flops 1000 | bytes 1000 | tf_op jit(solution)/shard_map/pallas_call | solution.py:112
  11.6 73.0 %all_to_all.54 = bf16[16,24,7168]{2,1,0:T(8,128)(2,1)} all-to-all(bf16[16,24,7168]{2,1,0:T(8,128)(2,1)} %bitcast.66), channel_id=1, replica_groups=mesh['pp'=8,'ep'=16] {'ep'}, dimensions={0} | all-to-all | bytes 11010048 | tf_op jit(solution)/shard_map/all_to_all | solution.py:22
  84.6 3.7 %all-to-all-start.1 = ((bf16[16,24,3584]{2,1,0:T(8,128)(2,1)}), bf16[16,24,3584]{2,1,0:T(8,128)(2,1)S(1)}, u32[]{:S(2)}, u32[]{:S(2)}) async-start(bf16[16,24,3584]{2,1,0:T(8,128)(2,1)} %bitcast.50), calls=%async_computation.1 | async-start | bytes 5505024 | tf_op jit(solution)/shard_map/all_to_all | solution.py:22
  88.4 15.1 %shard_map.115 = (bf16[384,1024]{1,0:T(8,128)(2,1)S(1)}, bf16[384,1024]{1,0:T(8,128)(2,1)S(1)}, f32[384,128]{1,0:T(8,128)S(1)}) custom-call(bf16[384,7168]{1,0:T(8,128)(2,1)} %bitcast.64, bf16[384,7168]{1,0:T(8,128)(2,1)} %bitcast.65, bf16[3584,2048]{1,0:T(8,128)(2,1)} %bitcast.56, bf16[3584,2048]{1,0:T(8,128)(2,1)} %bitcast.57, bf16[1024,3584]{1,0:T(8,128)(2,1)} %bitcast.61), custom_call_target="tpu_custom_call" | custom-call | flops 1000 | bytes 1000 | tf_op jit(solution)/shard_map/pallas_call | solution.py:157
  103.4 12.2 %shard_map.116 = bf16[384,3712]{1,0:T(8,128)(2,1)} custom-call(bf16[384,1024]{1,0:T(8,128)(2,1)S(1)} %get-tuple-element.25.gate_grad, bf16[384,1024]{1,0:T(8,128)(2,1)S(1)} %get-tuple-element.26.up_grad, bf16[3584,2048]{1,0:T(8,128)(2,1)} %bitcast.58, f32[384,128]{1,0:T(8,128)S(1)} %get-tuple-element.27.dots), custom_call_target="tpu_custom_call" | custom-call | flops 1000 | bytes 1000 | tf_op jit(solution)/shard_map/pallas_call | solution.py:202
  115.6 11.8 %all-to-all-done.1 = bf16[16,24,3584]{2,1,0:T(8,128)(2,1)S(1)} async-done(((bf16[16,24,3584]{2,1,0:T(8,128)(2,1)}), bf16[16,24,3584]{2,1,0:T(8,128)(2,1)S(1)}, u32[]{:S(2)}, u32[]{:S(2)}) %all-to-all-start.1) | async-done | bytes 2752544 | tf_op jit(solution)/shard_map/all_to_all | solution.py:22
  127.4 4.6 %all-to-all-start.2 = ((bf16[16,24,3712]{2,1,0:T(8,128)(2,1)}), bf16[16,24,3712]{2,1,0:T(8,128)(2,1)}, u32[]{:S(2)}, u32[]{:S(2)}) async-start(bf16[16,24,3712]{2,1,0:T(8,128)(2,1)} %bitcast.18), calls=%async_computation.2 | async-start | bytes 5701632 | tf_op jit(solution)/shard_map/all_to_all | solution.py:22
  132.0 1.5 fusion.19
  133.5 9.2 %shard_map.113.hidden = bf16[384,1024]{1,0:T(8,128)(2,1)S(1)} custom-call(bf16[384,3584]{1,0:T(8,128)(2,1)S(1)} %bitcast.41, bf16[3584,2048]{1,0:T(8,128)(2,1)} %bitcast.59, bf16[3584,2048]{1,0:T(8,128)(2,1)} %bitcast.60), custom_call_target="tpu_custom_call" | custom-call | flops 1000 | bytes 1000 | tf_op jit(solution)/shard_map/pallas_call | solution.py:227
  142.7 3.6 %shard_map.117 = bf16[384,1792]{1,0:T(8,128)(2,1)S(1)} custom-call(bf16[384,1024]{1,0:T(8,128)(2,1)S(1)} %shard_map.113.hidden, bf16[1024,3584]{1,0:T(8,128)(2,1)} %bitcast.62), custom_call_target="tpu_custom_call" | custom-call | flops 1000 | bytes 1000 | tf_op jit(solution)/shard_map/pallas_call | solution.py:247
  146.3 0.0 collective-permute-start.3
  146.3 1.7 collective-permute-start.2
  148.0 4.4 %shard_map.114 = bf16[384,1792]{1,0:T(8,128)(2,1)} custom-call(bf16[384,1024]{1,0:T(8,128)(2,1)S(1)} %shard_map.113.hidden, bf16[1024,3584]{1,0:T(8,128)(2,1)} %bitcast.63), custom_call_target="tpu_custom_call" | custom-call | flops 1000 | bytes 1000 | tf_op jit(solution)/shard_map/pallas_call | solution.py:247
  152.5 0.0 collective-permute-start.1
  152.5 17.9 %all-to-all-done.2 = bf16[16,24,3712]{2,1,0:T(8,128)(2,1)} async-done(((bf16[16,24,3712]{2,1,0:T(8,128)(2,1)}), bf16[16,24,3712]{2,1,0:T(8,128)(2,1)}, u32[]{:S(2)}, u32[]{:S(2)}) %all-to-all-start.2) | async-done | bytes 2850848 | tf_op jit(solution)/shard_map/all_to_all | solution.py:22
  170.4 1.2 add_reduce_fusion
  171.6 0.1 select_reduce_fusion
  171.8 0.0 collective-permute-done.3
  171.8 3.7 %all-to-all-start.4 = ((bf16[16,24,1792]{2,1,0:T(8,128)(2,1)}), bf16[16,24,1792]{2,1,0:T(8,128)(2,1)S(1)}, u32[]{:S(2)}, u32[]{:S(2)}) async-start(bf16[16,24,1792]{2,1,0:T(8,128)(2,1)} %bitcast.22), calls=%async_computation.4 | async-start | bytes 2752512 | tf_op jit(solution)/shard_map/all_to_all | solution.py:22
  175.6 0.3 fusion.11
  175.9 0.2 reshape.111
  176.1 13.8 %collective-permute-done.1 = bf16[384,1792]{1,0:T(8,128)(2,1)} collective-permute-done((bf16[384,1792]{1,0:T(8,128)(2,1)}, bf16[384,1792]{1,0:T(8,128)(2,1)}, u32[]{:S(2)}, u32[]{:S(2)}) %collective-permute-start.1) | collective-permute-done | bytes 1376288 | tf_op jit(solution)/shard_map/ppermute | solution.py:18
  189.9 2.7 %fusion.3 = bf16[16,24,2048]{2,1,0:T(8,128)(2,1)} fusion(bf16[16,16,224]{2,1,0:T(8,128)(2,1)S(1)} %bitcast.73, bf16[16,24,1792]{2,1,0:T(8,128)(2,1)} %bitcast.16), kind=kLoop, calls=%fused_computation.6 | loop fusion | flops 4718592 | bytes 3063808 | tf_op jit(solution)/shard_map/concatenate | solution.py:398
  192.6 4.0 %all-to-all-done.4 = bf16[16,24,1792]{2,1,0:T(8,128)(2,1)S(1)} async-done(((bf16[16,24,1792]{2,1,0:T(8,128)(2,1)}), bf16[16,24,1792]{2,1,0:T(8,128)(2,1)S(1)}, u32[]{:S(2)}, u32[]{:S(2)}) %all-to-all-start.4) | async-done | bytes 1376288 | tf_op jit(solution)/shard_map/all_to_all | solution.py:22
  196.6 3.7 %all-to-all-start.3 = ((bf16[16,24,2048]{2,1,0:T(8,128)(2,1)}), bf16[16,24,2048]{2,1,0:T(8,128)(2,1)S(1)}, u32[]{:S(2)}, u32[]{:S(2)}) async-start(bf16[16,24,2048]{2,1,0:T(8,128)(2,1)} %fusion.3), calls=%async_computation.3 | async-start | bytes 3145728 | tf_op jit(solution)/shard_map/all_to_all | solution.py:22
  200.3 2.7 %convolution_add_fusion.1 = f32[128,3584]{1,0:T(8,128)S(1)} fusion(bf16[384,3712]{1,0:T(8,128)(2,1)} %bitcast.19, bf16[128,3584]{1,0:T(8,128)(2,1)} %bitcast.48, bf16[384,128]{1,0:T(8,128)(2,1)S(1)} %get-tuple-element.31), kind=kOutput, calls=%fused_computation.1 | convolution fusion | flops 353239040 | bytes 5603328 | tf_op jit(solution)/shard_map/dot_general | solution.py:381
  203.0 0.0 copy-start.7
  203.0 0.0 copy-start.11
  203.0 0.4 fusion
  203.5 1.7 collective-permute-start.4
  205.2 1.5 fusion.18
  206.8 0.1 select_reduce_fusion.2
  206.8 0.0 collective-permute-start
  206.9 2.9 %collective-permute-start.5 = (f32[224,16]{0,1:T(8,128)S(1)}, f32[224,16]{0,1:T(8,128)S(1)}, u32[]{:S(2)}, u32[]{:S(2)}) collective-permute-start(f32[224,16]{0,1:T(8,128)S(1)} %bitcast.74), channel_id=1, source_target_pairs={{0,112},{16,96},{32,80},{48,64},{64,48},{80,32},{96,16},{112,0},{1... | collective-permute-start | bytes 43016 | tf_op jit(solution)/shard_map/ppermute | solution.py:402
  209.8 6.5 %collective-permute-done.4 = bf16[128,3584]{1,0:T(8,128)(2,1)S(1)} collective-permute-done((bf16[128,3584]{1,0:T(8,128)(2,1)S(1)}, bf16[128,3584]{1,0:T(8,128)(2,1)S(1)}, u32[]{:S(2)}, u32[]{:S(2)}) %collective-permute-start.4) | collective-permute-done | bytes 917536 | tf_op jit(solution)/shard_map/ppermute | solution.py:18
  216.3 0.0 collective-permute-done.mixer
  216.3 0.9 copy-done.9
  217.2 2.4 %shard_map.118.refs_0_ = bf16[128,3584]{1,0:T(8,128)(2,1)} custom-call(bf16[384,128]{1,0:T(8,128)(2,1)S(1)} %collective-permute-done.mixer, bf16[384,1792]{1,0:T(8,128)(2,1)S(1)} %bitcast.47, bf16[128,3584]{1,0:T(8,128)(2,1)} %collective-permute-done.2.residual), custom_call_target="tpu_custom_call" | custom-call | flops 1000 | bytes 1000 | tf_op jit(solution)/shard_map/pallas_call | solution.py:281
  219.6 4.3 %all-to-all-done.3 = bf16[16,24,2048]{2,1,0:T(8,128)(2,1)S(1)} async-done(((bf16[16,24,2048]{2,1,0:T(8,128)(2,1)}), bf16[16,24,2048]{2,1,0:T(8,128)(2,1)S(1)}, u32[]{:S(2)}, u32[]{:S(2)}) %all-to-all-start.3) | async-done | bytes 1572896 | tf_op jit(solution)/shard_map/all_to_all | solution.py:22
  223.9 0.0 copy-start.10
  223.9 2.5 %shard_map.119 = bf16[128,3584]{1,0:T(8,128)(2,1)} custom-call(bf16[384,128]{1,0:T(8,128)(2,1)S(1)} %collective-permute-done.mixer, bf16[384,2048]{1,0:T(8,128)(2,1)S(1)} %bitcast.46, bf16[128,3584]{1,0:T(8,128)(2,1)} %collective-permute-done.2.residual, bf16[128,3584]{1,0:T(8,128)(2,1)} %shard_map.118.refs_0_), custom_call_target="tpu_custom_call", output_to_operand_aliasing={{}: (3, {})} | custom-call | flops 1000 | bytes 1000 | tf_op jit(solution)/shard_map/pallas_call | solution.py:281
  226.4 0.6 fusion.10
  227.0 0.9 copy.22
  (32 shorter events, 0.4 us)
Async XLA Ops:
  0.6 1.2 copy-start
  1.8 1.2 copy-start.2
  3.0 0.7 copy-start.4
  3.7 0.7 copy-start.6
  11.6 73.0 %copy-start.3 = (bf16[384,3584]{1,0:T(8,128)(2,1)}, bf16[384,3584]{1,0:T(8,128)(2,1)S(1)}, u32[]{:S(2)}) copy-start(bf16[384,3584]{1,0:T(8,128)(2,1)S(1)} %get-tuple-element.23) | copy-start | bytes 8257540
  84.6 42.8 %all-to-all-start.1 = ((bf16[16,24,3584]{2,1,0:T(8,128)(2,1)}), bf16[16,24,3584]{2,1,0:T(8,128)(2,1)S(1)}, u32[]{:S(2)}, u32[]{:S(2)}) async-start(bf16[16,24,3584]{2,1,0:T(8,128)(2,1)} %bitcast.50), calls=%async_computation.1 | async-start | bytes 5505024 | tf_op jit(solution)/shard_map/all_to_all | solution.py:22
  127.4 4.6 %copy-start.8 = (bf16[1,3584,16]{1,2,0:T(8,128)(2,1)S(1)}, bf16[1,3584,16]{1,2,0:T(8,128)(2,1)}, u32[]{:S(2)}) copy-start(bf16[1,3584,16]{1,2,0:T(8,128)(2,1)} %param.16) | copy-start | bytes 344068
  127.4 43.0 %all-to-all-start.2 = ((bf16[16,24,3712]{2,1,0:T(8,128)(2,1)}), bf16[16,24,3712]{2,1,0:T(8,128)(2,1)}, u32[]{:S(2)}, u32[]{:S(2)}) async-start(bf16[16,24,3712]{2,1,0:T(8,128)(2,1)} %bitcast.18), calls=%async_computation.2 | async-start | bytes 5701632 | tf_op jit(solution)/shard_map/all_to_all | solution.py:22
  133.5 9.2 %copy-start.5 = (s32[1,128,2]{1,2,0:T(2,128)S(1)}, s32[1,128,2]{1,2,0:T(2,128)}, u32[]{:S(2)}) copy-start(s32[1,128,2]{1,2,0:T(2,128)} %param.12) | copy-start | bytes 3076
  146.3 25.6 %collective-permute-start.3 = (bf16[384,1792]{1,0:T(8,128)(2,1)S(1)}, bf16[384,1792]{1,0:T(8,128)(2,1)}, u32[]{:S(2)}, u32[]{:S(2)}) collective-permute-start(bf16[384,1792]{1,0:T(8,128)(2,1)S(1)} %shard_map.117), channel_id=1, source_target_pairs={{0,16},{16,32},{32,48},{48,64},{64,80},{80,96},{96,112},{112,0},{1... | collective-permute-start | bytes 4128776 | tf_op jit(solution)/shard_map/ppermute | solution.py:18
  146.3 70.9 %collective-permute-start.2 = (bf16[128,3584]{1,0:T(8,128)(2,1)}, bf16[128,3584]{1,0:T(8,128)(2,1)}, u32[]{:S(2)}, u32[]{:S(2)}) collective-permute-start(bf16[128,3584]{1,0:T(8,128)(2,1)} %bitcast.6.acts_fwd), channel_id=1, source_target_pairs={{0,16},{16,32},{32,48},{48,64},{64,80},{80,96},{96,112},{112,0},{1... | collective-permute-start | bytes 2752520 | tf_op jit(solution)/shard_map/ppermute | solution.py:18
  152.4 23.1 %copy-start.1 = (bf16[1,128,3584]{2,1,0:T(8,128)(2,1)S(1)}, bf16[1,128,3584]{2,1,0:T(8,128)(2,1)}, u32[]{:S(2)}) copy-start(bf16[1,128,3584]{2,1,0:T(8,128)(2,1)} %param.11) | copy-start | bytes 2752516
  152.5 37.5 %collective-permute-start.1 = (bf16[384,1792]{1,0:T(8,128)(2,1)}, bf16[384,1792]{1,0:T(8,128)(2,1)}, u32[]{:S(2)}, u32[]{:S(2)}) collective-permute-start(bf16[384,1792]{1,0:T(8,128)(2,1)} %shard_map.114), channel_id=1, source_target_pairs={{0,16},{16,32},{32,48},{48,64},{64,80},{80,96},{96,112},{112,0},{1... | collective-permute-start | bytes 4128776 | tf_op jit(solution)/shard_map/ppermute | solution.py:18
  171.8 24.8 %all-to-all-start.4 = ((bf16[16,24,1792]{2,1,0:T(8,128)(2,1)}), bf16[16,24,1792]{2,1,0:T(8,128)(2,1)S(1)}, u32[]{:S(2)}, u32[]{:S(2)}) async-start(bf16[16,24,1792]{2,1,0:T(8,128)(2,1)} %bitcast.22), calls=%async_computation.4 | async-start | bytes 2752512 | tf_op jit(solution)/shard_map/all_to_all | solution.py:22
  196.6 27.2 %all-to-all-start.3 = ((bf16[16,24,2048]{2,1,0:T(8,128)(2,1)}), bf16[16,24,2048]{2,1,0:T(8,128)(2,1)S(1)}, u32[]{:S(2)}, u32[]{:S(2)}) async-start(bf16[16,24,2048]{2,1,0:T(8,128)(2,1)} %fusion.3), calls=%async_computation.3 | async-start | bytes 3145728 | tf_op jit(solution)/shard_map/all_to_all | solution.py:22
  203.0 3.7 %copy-start.7 = (s32[1,128,2]{1,2,0:T(2,128)S(1)}, s32[1,128,2]{1,2,0:T(2,128)}, u32[]{:S(2)}) copy-start(s32[1,128,2]{1,2,0:T(2,128)} %param.10) | copy-start | bytes 3076
  203.0 3.8 %copy-start.11 = (f32[1,224,16]{1,2,0:T(8,128)S(1)}, f32[1,224,16]{1,2,0:T(8,128)}, u32[]{:S(2)}) copy-start(f32[1,224,16]{1,2,0:T(8,128)} %param.17) | copy-start | bytes 43012
  203.5 12.8 %collective-permute-start.4 = (bf16[128,3584]{1,0:T(8,128)(2,1)S(1)}, bf16[128,3584]{1,0:T(8,128)(2,1)S(1)}, u32[]{:S(2)}, u32[]{:S(2)}) collective-permute-start(bf16[128,3584]{1,0:T(8,128)(2,1)S(1)} %fusion), channel_id=1, source_target_pairs={{0,112},{16,0},{32,16},{48,32},{64,48},{80,64},{96,80},{112,96},{1... | collective-permute-start | bytes 2752520 | tf_op jit(solution)/shard_map/ppermute | solution.py:18
  206.8 9.4 %collective-permute-start = (bf16[384,128]{1,0:T(8,128)(2,1)S(1)}, bf16[384,128]{1,0:T(8,128)(2,1)S(1)}, u32[]{:S(2)}, u32[]{:S(2)}) collective-permute-start(bf16[384,128]{1,0:T(8,128)(2,1)S(1)} %select_reduce_fusion.2), channel_id=1, source_target_pairs={{0,16},{16,32},{32,48},{48,64},{64,80},{80,96},{96,112},{112,0},{1... | collective-permute-start | bytes 294920 | tf_op jit(solution)/shard_map/ppermute | solution.py:18
  206.9 19.6 %collective-permute-start.5 = (f32[224,16]{0,1:T(8,128)S(1)}, f32[224,16]{0,1:T(8,128)S(1)}, u32[]{:S(2)}, u32[]{:S(2)}) collective-permute-start(f32[224,16]{0,1:T(8,128)S(1)} %bitcast.74), channel_id=1, source_target_pairs={{0,112},{16,96},{32,80},{48,64},{64,48},{80,32},{96,16},{112,0},{1... | collective-permute-start | bytes 43016 | tf_op jit(solution)/shard_map/ppermute | solution.py:402
  216.3 0.9 copy-start.9
  223.9 3.1 %copy-start.10 = (bf16[128,3584]{1,0:T(8,128)(2,1)S(1)}, bf16[128,3584]{1,0:T(8,128)(2,1)}, u32[]{:S(2)}) copy-start(bf16[128,3584]{1,0:T(8,128)(2,1)} %copy-done.9) | copy-start | bytes 2752516

commit v3 on v2

--- a/solution.py
+++ b/solution.py
@@ -28,7 +28,7 @@
     return high, low
 
 
-def call(kernel, grid, in_specs, out_specs, out_shape, scratch=(), aliases=None):
+def call(kernel, grid, in_specs, out_specs, out_shape, scratch=(), aliases=None, limit=48 << 20):
     return pl.pallas_call(
         kernel,
         grid=grid,
@@ -37,28 +37,33 @@
         out_shape=out_shape,
         scratch_shapes=scratch,
         input_output_aliases=aliases or {},
-        compiler_params=pltpu.CompilerParams(vmem_limit_bytes=48 * 1024 * 1024),
+        compiler_params=pltpu.CompilerParams(vmem_limit_bytes=limit),
         cost_estimate=pl.CostEstimate(flops=1000, bytes_accessed=1000, transcendentals=0),
     )
 
 
 def slot_rows(ids, expert_count, capacity):
-    top_count, tokens = ids.shape
+    top_count, tokens = ids[0].shape
     earlier = (
         lax.broadcasted_iota(jnp.int32, (tokens, tokens), 0)
         < lax.broadcasted_iota(jnp.int32, (tokens, tokens), 1)
     ).astype(F32)
     experts = lax.broadcasted_iota(jnp.int32, (expert_count, tokens), 0)
-    taken = jnp.zeros((expert_count, 1), F32)
+    named = [batch[k : k + 1] for batch in ids for k in range(top_count)]
+    hot = [(experts == row).astype(F32) for row in named]
+    counts = jnp.dot(
+        jnp.concatenate(hot, axis=0).astype(BF16),
+        earlier.astype(BF16),
+        preferred_element_type=F32,
+    )
     rows = []
-    for k in range(top_count):
-        row = ids[k : k + 1]
-        hot = (experts == row).astype(F32)
-        before = jnp.dot(hot, earlier, preferred_element_type=F32) + taken
-        taken = taken + jnp.sum(hot, axis=1, keepdims=True)
-        place = jnp.sum(before * hot, axis=0, keepdims=True)
+    for index, row in enumerate(named):
+        before = counts[index * expert_count : (index + 1) * expert_count]
+        for other in range(index // top_count * top_count, index):
+            before = before + jnp.sum(hot[other], axis=1, keepdims=True)
+        place = jnp.sum(before * hot[index], axis=0, keepdims=True)
         rows.append(row * capacity + place.astype(jnp.int32))
-    return rows
+    return [rows[first : first + top_count] for first in range(0, len(rows), top_count)]
 
 
 def picker_of(rows, slot_count):
@@ -69,61 +74,74 @@
 
 
 def dispatch_kernel(
-    sizes, ids_bwd, ids_fwd, acts_bwd, upstream, acts_fwd, sent_bwd, sent_fwd, slots, picker
+    sizes,
+    ids_bwd,
+    ids_fwd,
+    acts_bwd,
+    upstream,
+    acts_fwd,
+    sent_bwd,
+    sent_fwd,
+    slots,
+    loaded,
+    built,
+    picker,
+    arrived,
+    left,
 ):
-    steps, expert_count, capacity = sizes
-    step = pl.program_id(0)
+    expert_count, capacity = sizes
     slot_count = expert_count * capacity
-
-    @pl.when(step == 0)
-    def _():
-        rows_bwd = slot_rows(ids_bwd[...], expert_count, capacity)
-        rows_fwd = slot_rows(ids_fwd[...], expert_count, capacity)
-        picker[0] = picker_of(rows_bwd, slot_count)
-        picker[1] = picker_of(rows_fwd, slot_count)
-        slots[...] = jnp.concatenate(rows_bwd + rows_fwd, axis=0)
-
-    @pl.when(step < steps)
-    def _():
-        sent_bwd[...] = jnp.dot(picker[0], acts_bwd[...], preferred_element_type=F32).astype(BF16)
-
-    @pl.when(jnp.logical_and(step >= steps, step < 2 * steps))
-    def _():
-        sent_bwd[...] = jnp.dot(picker[0], upstream[...], preferred_element_type=F32).astype(BF16)
-
-    @pl.when(step >= 2 * steps)
-    def _():
-        sent_fwd[...] = jnp.dot(picker[1], acts_fwd[...], preferred_element_type=F32).astype(BF16)
+    width = acts_bwd.shape[1]
+    loads = [
+        pltpu.make_async_copy(source, loaded.at[number], arrived.at[number])
+        for number, source in enumerate((acts_fwd, acts_bwd, upstream))
+    ]
+    for load in loads:
+        load.start()
+    rows_bwd, rows_fwd = slot_rows([ids_bwd[...], ids_fwd[...]], expert_count, capacity)
+    slots[...] = jnp.concatenate(rows_bwd + rows_fwd, axis=0)
+    picker[0] = picker_of(rows_fwd, slot_count)
+    picker[1] = picker_of(rows_bwd, slot_count)
+    loads[0].wait()
+    built[...] = jnp.dot(picker[0], loaded[0], preferred_element_type=F32).astype(BF16)
+    store = pltpu.make_async_copy(built, sent_fwd, left)
+    store.start()
+    for number in (1, 2):
+        loads[number].wait()
+        sent_bwd[:, (number - 1) * width : number * width] = jnp.dot(
+            picker[1], loaded[number], preferred_element_type=F32
+        ).astype(BF16)
+    store.wait()
 
 
 def dispatch(ids_bwd, ids_fwd, acts_bwd, upstream, acts_fwd, expert_count, capacity):
     tokens, width = acts_bwd.shape
     top_count = ids_bwd.shape[0]
     slot_count = expert_count * capacity
-    steps = 2
-    block = width // steps
-
-    def part(number):
-        return pl.BlockSpec(
-            (tokens, block), lambda i: (0, jnp.clip(i - number * steps, 0, steps - 1))
-        )
-
-    whole = pl.BlockSpec((top_count, tokens), lambda i: (0, 0))
-    return call(
-        functools.partial(dispatch_kernel, (steps, expert_count, capacity)),
-        (3 * steps,),
-        [whole, whole, part(0), part(1), part(2)],
-        [
-            pl.BlockSpec((slot_count, block), lambda i: (0, jnp.minimum(i, 2 * steps - 1))),
-            pl.BlockSpec((slot_count, block), lambda i: (0, jnp.clip(i - 2 * steps, 0, steps - 1))),
-            pl.BlockSpec((2 * top_count, tokens), lambda i: (0, 0)),
-        ],
-        [
-            jax.ShapeDtypeStruct((slot_count, 2 * width), BF16),
+    whole = pl.BlockSpec((top_count, tokens), lambda: (0, 0))
+    stays = pl.BlockSpec(memory_space=pl.ANY)
+    return call(
+        functools.partial(dispatch_kernel, (expert_count, capacity)),
+        (),
+        [whole, whole, stays, stays, stays],
+        [
+            pl.BlockSpec(memory_space=pltpu.VMEM),
+            stays,
+            pl.BlockSpec((2 * top_count, tokens), lambda: (0, 0)),
+        ],
+        [
+            pltpu.VMEM((slot_count, 2 * width), BF16),
             jax.ShapeDtypeStruct((slot_count, width), BF16),
             jax.ShapeDtypeStruct((2 * top_count, tokens), jnp.int32),
         ],
-        [pltpu.VMEM((2, slot_count, tokens), BF16)],
+        [
+            pltpu.VMEM((3, tokens, width), BF16),
+            pltpu.VMEM((slot_count, width), BF16),
+            pltpu.VMEM((2, slot_count, tokens), BF16),
+            pltpu.SemaphoreType.DMA((3,)),
+            pltpu.SemaphoreType.DMA,
+        ],
+        limit=57982000,
     )(ids_bwd, ids_fwd, acts_bwd, upstream, acts_fwd)
 
 
@@ -256,36 +274,154 @@
     )(hidden, proj_weight)
 
 
-def mix_kernel(mixer, rows, residual, *refs):
-    out = refs[-1]
+def mix_rows(mixer, rows, residual):
     mixed = lax.dot_general(
         mixer[...], rows[...], (((0,), (0,)), ((), ())), preferred_element_type=F32
     )
-    out[...] = (residual[...].astype(F32) + mixed).astype(BF16)
-
-
-def mix(mixer, rows, residual, first, columns, earlier=None):
+    return residual[...].astype(F32) + mixed
+
+
+def mix_early_kernel(mixer, rows, residual, out):
+    out[...] = mix_rows(mixer, rows, residual).astype(BF16)
+
+
+def mix_early(mixer, rows, residual, block=896):
     slot_count, tokens = mixer.shape
-    block = 896
-    in_specs = [
-        pl.BlockSpec((slot_count, tokens), lambda j: (0, 0)),
-        pl.BlockSpec((slot_count, block), lambda j: (0, j)),
-        pl.BlockSpec((tokens, block), lambda j: (0, first // block + j)),
+    return call(
+        mix_early_kernel,
+        (rows.shape[1] // block,),
+        [
+            pl.BlockSpec((slot_count, tokens), lambda j: (0, 0)),
+            pl.BlockSpec((slot_count, block), lambda j: (0, j)),
+            pl.BlockSpec((tokens, block), lambda j: (0, j)),
+        ],
+        pl.BlockSpec((tokens, block), lambda j: (0, j)),
+        jax.ShapeDtypeStruct(residual.shape, BF16),
+    )(mixer, rows, residual)
+
+
+def mix_late_kernel(
+    capacity, mixer, rows, residual, parts, mirrored, early, grads, out, summed
+):
+    del early, grads
+    out[...] = mix_rows(mixer, rows, residual).astype(BF16)
+
+    @pl.when(pl.program_id(0) == 0)
+    def _():
+        shape = (mirrored.shape[0], parts.shape[0])
+        ahead = lax.broadcasted_iota(jnp.int32, shape, 1) - lax.broadcasted_iota(
+            jnp.int32, shape, 0
+        )
+        chosen = functools.reduce(
+            jnp.logical_or, [ahead == place for place in range(0, shape[1], capacity)]
+        )
+        total = jnp.dot(
+            chosen.astype(F32).astype(BF16), parts[...], preferred_element_type=F32
+        )
+        summed[...] = total[:, : mirrored.shape[1]] + mirrored[...]
+
+
+def mix_late(mixer, returned, residual, mirrored, early, grads, capacity, wide, block=896):
+    slot_count, tokens = mixer.shape
+    columns = returned.shape[1] - wide
+    first = residual.shape[1] - columns
+    stays = pl.BlockSpec(memory_space=pl.ANY)
+    whole = pl.BlockSpec(mirrored.shape, lambda j: (0, 0))
+    return call(
+        functools.partial(mix_late_kernel, capacity),
+        (columns // block,),
+        [
+            pl.BlockSpec((slot_count, tokens), lambda j: (0, 0)),
+            pl.BlockSpec((slot_count, block), lambda j: (0, j)),
+            pl.BlockSpec((tokens, block), lambda j: (0, first // block + j)),
+            pl.BlockSpec((slot_count, wide), lambda j: (0, columns // wide)),
+            whole,
+            stays,
+            stays,
+        ],
+        [pl.BlockSpec((tokens, block), lambda j: (0, first // block + j)), whole],
+        [
+            jax.ShapeDtypeStruct(residual.shape, BF16),
+            jax.ShapeDtypeStruct(mirrored.shape, F32),
+        ],
+        aliases={5: 0},
+    )(mixer, returned, residual, returned, mirrored, early, grads)
+
+
+def logit_kernel(extra, slots, ids, affinity, out):
+    top_count, tokens = ids.shape
+    slot_count = extra.shape[0]
+    expert_count = out.shape[0] // 2
+    dots = extra[:, 0:1].astype(F32) + extra[:, 1:2].astype(F32)
+    places = lax.broadcasted_iota(jnp.int32, (slot_count, tokens), 0)
+    experts = lax.broadcasted_iota(jnp.int32, (expert_count, tokens), 0)
+    gate_grads = [
+        jnp.sum(jnp.where(places == slots[k : k + 1], dots, 0.0), axis=0, keepdims=True)
+        for k in range(top_count)
     ]
-    operands = [mixer, rows, residual]
-    aliases = None
-    if earlier is not None:
-        in_specs.append(pl.BlockSpec(memory_space=pl.ANY))
-        operands.append(earlier)
-        aliases = {3: 0}
-    return call(
-        mix_kernel,
-        (columns // block,),
-        in_specs,
-        pl.BlockSpec((tokens, block), lambda j: (0, first // block + j)),
+    rows = [affinity[k : k + 1] for k in range(top_count)]
+    total = sum(rows)
+    mean_term = sum(row / total * grad for row, grad in zip(rows, gate_grads))
+    logit = jnp.zeros((expert_count, tokens), F32)
+    for k in range(top_count):
+        value = (gate_grads[k] - mean_term) / total * rows[k] * (1.0 - rows[k])
+        logit = logit + jnp.where(experts == ids[k : k + 1], value, 0.0)
+    out[...] = jnp.concatenate(split_two(logit), axis=0)
+
+
+def logit_gradient(back, slots, ids, affinity, expert_count):
+    slot_count = back.shape[0]
+    top_count, tokens = ids.shape
+    last = back.shape[1] // LANES - 1
+    whole = pl.BlockSpec((top_count, tokens), lambda j: (0, 0))
+    return call(
+        logit_kernel,
+        (1,),
+        [
+            pl.BlockSpec((slot_count, LANES), lambda j: (0, last)),
+            pl.BlockSpec(slots.shape, lambda j: (0, 0)),
+            whole,
+            whole,
+        ],
+        pl.BlockSpec((2 * expert_count, tokens), lambda j: (0, 0)),
+        jax.ShapeDtypeStruct((2 * expert_count, tokens), BF16),
+    )(back, slots, ids, affinity)
+
+
+def input_grad_kernel(mixer, rows, residual, logit_pair, router, out):
+    contract = (((0,), (0,)), ((), ()))
+    both = jnp.concatenate([router[...], router[...]], axis=0)
+    through = lax.dot_general(logit_pair[...], both, contract, preferred_element_type=F32)
+    out[...] = (mix_rows(mixer, rows, residual) + through).astype(BF16)
+
+
+def input_gradient(mixer, back, residual, logit_pair, router, block=896):
+    slot_count, tokens = mixer.shape
+    return call(
+        input_grad_kernel,
+        (residual.shape[1] // block,),
+        [
+            pl.BlockSpec((slot_count, tokens), lambda j: (0, 0)),
+            pl.BlockSpec((slot_count, block), lambda j: (0, j)),
+            pl.BlockSpec((tokens, block), lambda j: (0, j)),
+            pl.BlockSpec(logit_pair.shape, lambda j: (0, 0)),
+            pl.BlockSpec((router.shape[0], block), lambda j: (0, j)),
+        ],
+        pl.BlockSpec((tokens, block), lambda j: (0, j)),
         jax.ShapeDtypeStruct(residual.shape, BF16),
-        aliases=aliases,
-    )(*operands)
+    )(mixer, back, residual, logit_pair, router)
+
+
+def settle_kernel(rows, out):
+    out[...] = rows[...]
+
+
+def settled(rows, block=1792):
+    tokens, width = rows.shape
+    spec = pl.BlockSpec((tokens, block), lambda j: (0, j))
+    return call(
+        settle_kernel, (width // block,), [spec], spec, jax.ShapeDtypeStruct(rows.shape, BF16)
+    )(rows)
 
 
 def gating(tokens, ids, router_section):
@@ -298,7 +434,7 @@
     )
     affinity = jax.nn.sigmoid(jnp.sum(jnp.where(hot, logits[None], 0.0), axis=1))
     total = jnp.sum(affinity, axis=0, keepdims=True)
-    return affinity, affinity / total, total, hot
+    return affinity, affinity / total
 
 
 def slot_hot(slots, slot_count):
@@ -344,10 +480,8 @@
         ids_bwd, ids_fwd, tokens_bwd, upstream, tokens_fwd, expert_count, capacity
     )
     got_bwd = exchange(sent_bwd)
-    (got_bwd, sent_fwd, slots, tokens_fwd, tokens_bwd, upstream, mirrored, router_section) = (
-        lax.optimization_barrier(
-            (got_bwd, sent_fwd, slots, tokens_fwd, tokens_bwd, upstream, mirrored, router_section)
-        )
+    got_bwd, sent_fwd, slots, mirrored, router_section, here = lax.optimization_barrier(
+        (got_bwd, sent_fwd, slots, mirrored, router_section, jnp.ones((), jnp.bool_))
     )
     got_fwd = exchange(sent_fwd)
 
@@ -357,34 +491,20 @@
     hidden = forward_hidden(got_fwd, joined_weight)
     produced_early = shifted(produce(hidden, proj_weight, 0, early), 1)
     produced_late = shifted(produce(hidden, proj_weight, early, width - early), 1)
-    residual = shifted(tokens_fwd, 1)
-    _, gates_fwd, _, _ = gating(tokens_fwd, ids_fwd, router_section)
+    residual = shifted(jnp.where(here, tokens_fwd, 0), 1)
+    _, gates_fwd = gating(tokens_fwd, ids_fwd, router_section)
     hot_fwd = slot_hot(slots[top_count:], slot_count)
     mixer_fwd = shifted(weighted(hot_fwd, gates_fwd).astype(BF16), 1)
     returned_early = exchange(produced_early)
-    next_early = mix(mixer_fwd, returned_early, residual, 0, early)
-
-    affinity, gates_bwd, total, hot_bwd = gating(tokens_bwd, ids_bwd, router_section)
-    slots_bwd = slot_hot(slots[:top_count], slot_count)
-    gate_rows = back[:, width].astype(F32) + back[:, width + 1].astype(F32)
-    gate_grad = jnp.sum(jnp.where(slots_bwd, gate_rows[None, :, None], 0.0), axis=1)
-    mean_term = jnp.sum(gates_bwd * gate_grad, axis=0, keepdims=True)
-    logit_rows = (gate_grad - mean_term) / total * affinity * (1.0 - affinity)
-    logit_grad = weighted(hot_bwd, logit_rows)
-    logit_pair = jnp.concatenate(split_two(logit_grad), axis=0)
-    router_back = lax.dot_general(
-        logit_pair,
-        jnp.concatenate([router_section, router_section], axis=1),
-        (((0,), (1,)), ((), ())),
-        preferred_element_type=F32,
-    )
-    grad_mix = lax.dot_general(
-        weighted(slots_bwd, gates_bwd).astype(BF16),
-        back[:, :width],
-        (((0,), (0,)), ((), ())),
-        preferred_element_type=F32,
-    )
-    next_grads = shifted((upstream.astype(F32) + grad_mix + router_back).astype(BF16), -1)
+    next_early = mix_early(mixer_fwd, returned_early, residual)
+
+    affinity, gates_bwd = gating(tokens_bwd, ids_bwd, router_section)
+    hot_bwd = slot_hot(slots[:top_count], slot_count)
+    mixer_bwd = weighted(hot_bwd, gates_bwd).astype(BF16)
+    logit_pair = logit_gradient(back, slots, ids_bwd, affinity, expert_count)
+    next_grads = settled(
+        shifted(input_gradient(mixer_bwd, back, upstream, logit_pair, router_section.T), -1)
+    )
 
     router_pair = jnp.dot(logit_pair, tokens_bwd, preferred_element_type=F32)
     router_part = ((router_pair[:expert_count] + router_pair[expert_count:]) / row_count).astype(
@@ -396,18 +516,12 @@
         ((0, 0), (0, capacity - expert_count), (0, wide - shard)),
     ).reshape(slot_count, wide)
     returned_late = exchange(jnp.concatenate([produced_late, router_blocks], axis=1))
-    next_acts = mix(mixer_fwd, returned_late, residual, early, width - early, next_early)
-
     count = lax.axis_size("pp")
     mirrored = lax.ppermute(mirrored, "pp", [(i, count - 1 - i) for i in range(count)])
-    summed = jnp.sum(
-        returned_late[:, width - early :]
-        .reshape(ranks, capacity, wide)[:, :expert_count, :shard]
-        .astype(F32),
-        axis=0,
-    )
-    router_grads = summed.T + mirrored
-    return (next_acts[None], next_grads[None], router_grads[None])
+    next_acts, router_grads = mix_late(
+        mixer_fwd, returned_late, residual, mirrored.T, next_early, next_grads, capacity, wide
+    )
+    return (next_acts[None], next_grads[None], router_grads.T[None])
 
 
 def solution(mesh):

time: 229 us -> 221 us (0.965)
  matrix products: 6.34 us -> 2.08 us
  waiting for transfers between devices: 58.3 us -> 55.8 us
    dot_general x2 -> x0, matrix products: 3.09 us -> none  [the longest x1 2.67 us: on_device(): lax.dot_general(weighted(slots_bwd, gates_bwd).astype(BF16), back[:, :wid...]
    dot_general x2, matrix products: 3 us -> 0.64 us  [gating(): lax.dot_general(router_section, tokens, (((0,), (1,)), ((), ())), preferr...]
    all_to_all x4, waiting for transfers between devices: 38 us -> 35.7 us  [exchange(): return lax.all_to_all(value, 'ep', split_axis=0, concat_axis=0, tiled=True)]
    pallas_call x3 -> x6, Pallas kernels: 12.2 us -> 13.8 us  [the longest x1 5.09 us: dispatch(): call(functools.partial(dispatch_kernel, (expert_count, capacity)), (), [w...]
    unnamed x25 -> x26, local copies, waits for them, and re-layouts: 5.58 us -> 6.14 us
  transfers between devices with their start and end apart: 10 -> 10, of which waited for: 6 -> 6; matrix products, arithmetic and copies ran while one was open for 5% -> 3% of each run, Pallas kernels for 22% -> 22%
where the time goes in v3:
time: 221 us; the launch traced here: 220 us
  blocking collectives  72.8 us (33%)
  Pallas kernels  57.4 us (26%)
  waiting for transfers between devices  55.8 us (25%)
  starting transfers between devices  21.2 us (10%)
  local copies, waits for them, and re-layouts  6.39 us (3%)
  other arithmetic  4 us (2%)
    all_to_all x1, blocking collectives, exchange(): return lax.all_to_all(value, 'ep', split_axis=0, concat_axis=0, tiled=True)  72.8 us
    all_to_all x4, waiting for transfers between devices, exchange(): return lax.all_to_all(value, 'ep', split_axis=0, concat_axis=0, tiled=True)  35.7 us
    ppermute x5, waiting for transfers between devices, shifted(): return lax.ppermute(value, 'pp', pairs)  20.1 us
    all_to_all x4, starting transfers between devices, exchange(): return lax.all_to_all(value, 'ep', split_axis=0, concat_axis=0, tiled=True)  16.3 us
    pallas_call x1, Pallas kernels, backward_hidden(): call(backward_hidden_kernel, (count,), [pl.BlockSpec((slot_count, width),...  15 us
    pallas_call x1, Pallas kernels, row_gradient(): call(functools.partial(row_grad_kernel, block), (width // block,), [whole...  10.6 us
    pallas_call x1, Pallas kernels, forward_hidden(): call(forward_hidden_kernel, (count,), [pl.BlockSpec((slot_count, width),...  9.1 us
    pallas_call x2, Pallas kernels, produce(): call(produce_kernel, (columns // block,), [pl.BlockSpec((slot_count, unit...  8.91 us
  transfers between devices with their start and end apart: 10, of which 6 were waited for; matrix products, arithmetic and copies ran while one was open for 3% of the time, Pallas kernels for 22%

profile of v3, /device:TPU:0, one launch (start us, length us, event | category | flops | bytes accessed | tf_op | source)
XLA Modules:
  0.0 220.5 jit_solution(16316620820567533585)
XLA Ops:
  0.6 5.1 %shard_map.112 = (bf16[384,7168]{1,0:T(8,128)(2,1)S(1)}, bf16[384,3584]{1,0:T(8,128)(2,1)}, s32[4,128]{1,0:T(4,128)}) custom-call(s32[2,128]{1,0:T(2,128)} %bitcast.55, s32[2,128]{1,0:T(2,128)} %bitcast.73, bf16[128,3584]{1,0:T(8,128)(2,1)} %bitcast.68, bf16[128,3584]{1,0:T(8,128)(2,1)} %bitcast.48, bf16[128,3584]{1,0:T(8,128)(2,1)} %bitcast.69), custom_call_target="tpu_custom_call" | custom-call | flops 1000 | bytes 1000 | tf_op jit(solution)/shard_map/pallas_call | solution.py:123
  5.7 72.8 %all_to_all.53 = bf16[16,24,7168]{2,1,0:T(8,128)(2,1)} all-to-all(bf16[16,24,7168]{2,1,0:T(8,128)(2,1)S(1)} %bitcast.47), channel_id=1, replica_groups=mesh['pp'=8,'ep'=16] {'ep'}, dimensions={0} | all-to-all | bytes 11010048 | tf_op jit(solution)/shard_map/all_to_all | solution.py:22
  78.5 3.7 %all-to-all-start.1 = ((bf16[16,24,3584]{2,1,0:T(8,128)(2,1)}), bf16[16,24,3584]{2,1,0:T(8,128)(2,1)S(1)}, u32[]{:S(2)}, u32[]{:S(2)}) async-start(bf16[16,24,3584]{2,1,0:T(8,128)(2,1)} %bitcast.71), calls=%async_computation.1 | async-start | bytes 5505024 | tf_op jit(solution)/shard_map/all_to_all | solution.py:22
  82.2 15.0 %shard_map.115 = (bf16[384,1024]{1,0:T(8,128)(2,1)S(1)}, bf16[384,1024]{1,0:T(8,128)(2,1)S(1)}, f32[384,128]{1,0:T(8,128)S(1)}) custom-call(bf16[384,7168]{1,0:T(8,128)(2,1)} %bitcast.66, bf16[384,7168]{1,0:T(8,128)(2,1)} %bitcast.67, bf16[3584,2048]{1,0:T(8,128)(2,1)} %bitcast.58, bf16[3584,2048]{1,0:T(8,128)(2,1)} %bitcast.59, bf16[1024,3584]{1,0:T(8,128)(2,1)} %bitcast.63), custom_call_target="tpu_custom_call" | custom-call | flops 1000 | bytes 1000 | tf_op jit(solution)/shard_map/pallas_call | solution.py:175
  97.3 10.6 %shard_map.116 = bf16[384,3712]{1,0:T(8,128)(2,1)S(1)} custom-call(bf16[384,1024]{1,0:T(8,128)(2,1)S(1)} %get-tuple-element.24.gate_grad, bf16[384,1024]{1,0:T(8,128)(2,1)S(1)} %get-tuple-element.25.up_grad, bf16[3584,2048]{1,0:T(8,128)(2,1)} %bitcast.60, f32[384,128]{1,0:T(8,128)S(1)} %get-tuple-element.26.dots), custom_call_target="tpu_custom_call" | custom-call | flops 1000 | bytes 1000 | tf_op jit(solution)/shard_map/pallas_call | solution.py:220
  107.9 1.6 copy-done
  109.4 11.9 %all-to-all-done.1 = bf16[16,24,3584]{2,1,0:T(8,128)(2,1)S(1)} async-done(((bf16[16,24,3584]{2,1,0:T(8,128)(2,1)}), bf16[16,24,3584]{2,1,0:T(8,128)(2,1)S(1)}, u32[]{:S(2)}, u32[]{:S(2)}) %all-to-all-start.1) | async-done | bytes 2752544 | tf_op jit(solution)/shard_map/all_to_all | solution.py:22
  121.3 1.6 copy-done.1
  122.9 3.7 %all-to-all-start.2 = ((bf16[16,24,3712]{2,1,0:T(8,128)(2,1)}), bf16[16,24,3712]{2,1,0:T(8,128)(2,1)S(1)}, u32[]{:S(2)}, u32[]{:S(2)}) async-start(bf16[16,24,3712]{2,1,0:T(8,128)(2,1)} %bitcast.45), calls=%async_computation.2 | async-start | bytes 5701632 | tf_op jit(solution)/shard_map/all_to_all | solution.py:22
  126.6 1.8 copy-done.2
  128.4 9.1 %shard_map.113.hidden = bf16[384,1024]{1,0:T(8,128)(2,1)S(1)} custom-call(bf16[384,3584]{1,0:T(8,128)(2,1)S(1)} %bitcast.46, bf16[3584,2048]{1,0:T(8,128)(2,1)} %bitcast.61, bf16[3584,2048]{1,0:T(8,128)(2,1)} %bitcast.62), custom_call_target="tpu_custom_call" | custom-call | flops 1000 | bytes 1000 | tf_op jit(solution)/shard_map/pallas_call | solution.py:245
  137.5 0.0 copy-start.9
  137.5 0.0 copy-start.5
  137.5 0.0 copy-start.8
  137.5 4.5 %shard_map.118 = bf16[384,1792]{1,0:T(8,128)(2,1)} custom-call(bf16[384,1024]{1,0:T(8,128)(2,1)S(1)} %shard_map.113.hidden, bf16[1024,3584]{1,0:T(8,128)(2,1)} %bitcast.64), custom_call_target="tpu_custom_call" | custom-call | flops 1000 | bytes 1000 | tf_op jit(solution)/shard_map/pallas_call | solution.py:265
  142.1 0.0 collective-permute-start.4
  142.1 1.0 broadcast_select_fusion
  143.1 1.7 collective-permute-start.2
  144.8 0.3 fusion.8
  145.1 0.0 copy-start.7
  145.1 4.4 %shard_map.114 = bf16[384,1792]{1,0:T(8,128)(2,1)} custom-call(bf16[384,1024]{1,0:T(8,128)(2,1)S(1)} %shard_map.113.hidden, bf16[1024,3584]{1,0:T(8,128)(2,1)} %bitcast.65), custom_call_target="tpu_custom_call" | custom-call | flops 1000 | bytes 1000 | tf_op jit(solution)/shard_map/pallas_call | solution.py:265
  149.5 0.0 collective-permute-start.1
  149.6 17.5 %all-to-all-done.2 = bf16[16,24,3712]{2,1,0:T(8,128)(2,1)S(1)} async-done(((bf16[16,24,3712]{2,1,0:T(8,128)(2,1)}), bf16[16,24,3712]{2,1,0:T(8,128)(2,1)S(1)}, u32[]{:S(2)}, u32[]{:S(2)}) %all-to-all-start.2) | async-done | bytes 2850848 | tf_op jit(solution)/shard_map/all_to_all | solution.py:22
  167.0 0.3 shard_map.117.logit_pair
  167.3 0.0 collective-permute-done.4
  167.3 4.4 %all-to-all-start.4 = ((bf16[16,24,1792]{2,1,0:T(8,128)(2,1)}), bf16[16,24,1792]{2,1,0:T(8,128)(2,1)}, u32[]{:S(2)}, u32[]{:S(2)}) async-start(bf16[16,24,1792]{2,1,0:T(8,128)(2,1)} %bitcast.23), calls=%async_computation.4 | async-start | bytes 2752512 | tf_op jit(solution)/shard_map/all_to_all | solution.py:22
  171.7 1.4 fusion.6
  173.2 0.2 reshape.65
  173.4 12.5 %collective-permute-done.1 = bf16[384,1792]{1,0:T(8,128)(2,1)} collective-permute-done((bf16[384,1792]{1,0:T(8,128)(2,1)}, bf16[384,1792]{1,0:T(8,128)(2,1)}, u32[]{:S(2)}, u32[]{:S(2)}) %collective-permute-start.1) | collective-permute-done | bytes 1376288 | tf_op jit(solution)/shard_map/ppermute | solution.py:18
  185.9 2.7 %fusion.1 = bf16[16,24,2048]{2,1,0:T(8,128)(2,1)} fusion(bf16[16,16,224]{2,1,0:T(8,128)(2,1)S(1)} %bitcast.72, bf16[16,24,1792]{2,1,0:T(8,128)(2,1)} %bitcast.16), kind=kLoop, calls=%fused_computation.2 | loop fusion | flops 4718592 | bytes 3063808 | tf_op jit(solution)/shard_map/concatenate | solution.py:518
  188.6 2.9 %all-to-all-done.4 = bf16[16,24,1792]{2,1,0:T(8,128)(2,1)} async-done(((bf16[16,24,1792]{2,1,0:T(8,128)(2,1)}), bf16[16,24,1792]{2,1,0:T(8,128)(2,1)}, u32[]{:S(2)}, u32[]{:S(2)}) %all-to-all-start.4) | async-done | bytes 1376288 | tf_op jit(solution)/shard_map/all_to_all | solution.py:22
  191.5 4.4 %all-to-all-start.3 = ((bf16[16,24,2048]{2,1,0:T(8,128)(2,1)}), bf16[16,24,2048]{2,1,0:T(8,128)(2,1)}, u32[]{:S(2)}, u32[]{:S(2)}) async-start(bf16[16,24,2048]{2,1,0:T(8,128)(2,1)} %fusion.1), calls=%async_computation.3 | async-start | bytes 3145728 | tf_op jit(solution)/shard_map/all_to_all | solution.py:22
  196.0 0.0 copy-start.3
  196.0 1.2 copy-done.3
  197.2 2.1 shard_map.120
  199.3 0.2 collective-permute-start.5
  199.5 0.3 fusion.4
  200.0 0.1 select_reduce_fusion.1
  200.0 0.3 collective-permute-start
  200.3 2.7 %collective-permute-start.3 = (f32[224,16]{0,1:T(8,128)S(1)}, f32[224,16]{0,1:T(8,128)S(1)}, u32[]{:S(2)}, u32[]{:S(2)}) collective-permute-start(f32[224,16]{0,1:T(8,128)S(1)} %bitcast.75), channel_id=1, source_target_pairs={{0,112},{16,96},{32,80},{48,64},{64,48},{80,32},{96,16},{112,0},{1... | collective-permute-start | bytes 43016 | tf_op jit(solution)/shard_map/ppermute | solution.py:520
  203.0 7.6 %collective-permute-done.5.rows = bf16[128,3584]{1,0:T(8,128)(2,1)S(1)} collective-permute-done((bf16[128,3584]{1,0:T(8,128)(2,1)S(1)}, bf16[128,3584]{1,0:T(8,128)(2,1)S(1)}, u32[]{:S(2)}, u32[]{:S(2)}) %collective-permute-start.5) | collective-permute-done | bytes 917536 | tf_op jit(solution)/shard_map/ppermute | solution.py:18
  210.6 1.0 shard_map.121.grads
  211.7 0.0 collective-permute-done.mixer
  211.7 0.0 collective-permute-done.2.residual
  211.7 2.6 %shard_map.119.early = bf16[128,3584]{1,0:T(8,128)(2,1)} custom-call(bf16[384,128]{1,0:T(8,128)(2,1)S(1)} %collective-permute-done.mixer, bf16[384,1792]{1,0:T(8,128)(2,1)} %bitcast.24.rows, bf16[128,3584]{1,0:T(8,128)(2,1)} %collective-permute-done.2.residual), custom_call_target="tpu_custom_call" | custom-call | flops 1000 | bytes 1000 | tf_op jit(solution)/shard_map/pallas_call | solution.py:290
  214.3 0.0 collective-permute-done.3
  214.3 3.5 %all-to-all-done.3 = bf16[16,24,2048]{2,1,0:T(8,128)(2,1)} async-done(((bf16[16,24,2048]{2,1,0:T(8,128)(2,1)}), bf16[16,24,2048]{2,1,0:T(8,128)(2,1)}, u32[]{:S(2)}, u32[]{:S(2)}) %all-to-all-start.3) | async-done | bytes 1572896 | tf_op jit(solution)/shard_map/all_to_all | solution.py:22
  217.8 2.7 %shard_map.122 = (bf16[128,3584]{1,0:T(8,128)(2,1)}, f32[16,224]{1,0:T(8,128)}) custom-call(bf16[384,128]{1,0:T(8,128)(2,1)S(1)} %collective-permute-done.mixer, bf16[384,2048]{1,0:T(8,128)(2,1)} %bitcast.21.rows.parts, bf16[128,3584]{1,0:T(8,128)(2,1)} %collective-permute-done.2.residual, ...), custom_call_target="tpu_custom_call", output_to_operand_aliasing={{0}: (5, {})} | custom-call | flops 1000 | bytes 1000 | tf_op jit(solution)/shard_map/pallas_call | solution.py:330
  (27 shorter events, 0.3 us)
Async XLA Ops:
  78.5 42.8 %all-to-all-start.1 = ((bf16[16,24,3584]{2,1,0:T(8,128)(2,1)}), bf16[16,24,3584]{2,1,0:T(8,128)(2,1)S(1)}, u32[]{:S(2)}, u32[]{:S(2)}) async-start(bf16[16,24,3584]{2,1,0:T(8,128)(2,1)} %bitcast.71), calls=%async_computation.1 | async-start | bytes 5505024 | tf_op jit(solution)/shard_map/all_to_all | solution.py:22
  107.8 1.6 copy-start
  121.3 1.6 copy-start.1
  122.9 44.1 %all-to-all-start.2 = ((bf16[16,24,3712]{2,1,0:T(8,128)(2,1)}), bf16[16,24,3712]{2,1,0:T(8,128)(2,1)S(1)}, u32[]{:S(2)}, u32[]{:S(2)}) async-start(bf16[16,24,3712]{2,1,0:T(8,128)(2,1)} %bitcast.45), calls=%async_computation.2 | async-start | bytes 5701632 | tf_op jit(solution)/shard_map/all_to_all | solution.py:22
  126.6 1.8 copy-start.2
  137.5 4.6 %copy-start.9 = (bf16[1,128,3584]{2,1,0:T(8,128)(2,1)S(1)}, bf16[1,128,3584]{2,1,0:T(8,128)(2,1)}, u32[]{:S(2)}) copy-start(bf16[1,128,3584]{2,1,0:T(8,128)(2,1)} %param.9) | copy-start | bytes 2752516
  137.5 7.3 %copy-start.5 = (bf16[1,3584,16]{1,2,0:T(8,128)(2,1)S(1)}, bf16[1,3584,16]{1,2,0:T(8,128)(2,1)}, u32[]{:S(2)}) copy-start(bf16[1,3584,16]{1,2,0:T(8,128)(2,1)} %param.16) | copy-start | bytes 344068
  137.5 7.2 %copy-start.8 = (bf16[1,128,3584]{2,1,0:T(8,128)(2,1)S(1)}, bf16[1,128,3584]{2,1,0:T(8,128)(2,1)}, u32[]{:S(2)}) copy-start(bf16[1,128,3584]{2,1,0:T(8,128)(2,1)} %param.11) | copy-start | bytes 2752516
  142.1 3.0 %copy-start.6 = (s32[1,128,2]{1,2,0:T(2,128)S(1)}, s32[1,128,2]{1,2,0:T(2,128)}, u32[]{:S(2)}) copy-start(s32[1,128,2]{1,2,0:T(2,128)} %param.12) | copy-start | bytes 3076
  142.1 25.2 %collective-permute-start.4 = (bf16[384,1792]{1,0:T(8,128)(2,1)}, bf16[384,1792]{1,0:T(8,128)(2,1)}, u32[]{:S(2)}, u32[]{:S(2)}) collective-permute-start(bf16[384,1792]{1,0:T(8,128)(2,1)} %shard_map.118), channel_id=1, source_target_pairs={{0,16},{16,32},{32,48},{48,64},{64,80},{80,96},{96,112},{112,0},{1... | collective-permute-start | bytes 4128776 | tf_op jit(solution)/shard_map/ppermute | solution.py:18
  143.1 68.6 %collective-permute-start.2 = (bf16[128,3584]{1,0:T(8,128)(2,1)}, bf16[128,3584]{1,0:T(8,128)(2,1)}, u32[]{:S(2)}, u32[]{:S(2)}) collective-permute-start(bf16[128,3584]{1,0:T(8,128)(2,1)} %broadcast_select_fusion), channel_id=1, source_target_pairs={{0,16},{16,32},{32,48},{48,64},{64,80},{80,96},{96,112},{112,0},{1... | collective-permute-start | bytes 2752520 | tf_op jit(solution)/shard_map/ppermute | solution.py:18
  145.1 21.9 %copy-start.7 = (s32[4,128]{1,0:T(4,128)S(1)}, s32[4,128]{1,0:T(4,128)}, u32[]{:S(2)}) copy-start(s32[4,128]{1,0:T(4,128)} %get-tuple-element.20.slots) | copy-start | bytes 6148
  149.5 36.4 %collective-permute-start.1 = (bf16[384,1792]{1,0:T(8,128)(2,1)}, bf16[384,1792]{1,0:T(8,128)(2,1)}, u32[]{:S(2)}, u32[]{:S(2)}) collective-permute-start(bf16[384,1792]{1,0:T(8,128)(2,1)} %shard_map.114), channel_id=1, source_target_pairs={{0,16},{16,32},{32,48},{48,64},{64,80},{80,96},{96,112},{112,0},{1... | collective-permute-start | bytes 4128776 | tf_op jit(solution)/shard_map/ppermute | solution.py:18
  167.3 24.2 %all-to-all-start.4 = ((bf16[16,24,1792]{2,1,0:T(8,128)(2,1)}), bf16[16,24,1792]{2,1,0:T(8,128)(2,1)}, u32[]{:S(2)}, u32[]{:S(2)}) async-start(bf16[16,24,1792]{2,1,0:T(8,128)(2,1)} %bitcast.23), calls=%async_computation.4 | async-start | bytes 2752512 | tf_op jit(solution)/shard_map/all_to_all | solution.py:22
  191.5 26.2 %all-to-all-start.3 = ((bf16[16,24,2048]{2,1,0:T(8,128)(2,1)}), bf16[16,24,2048]{2,1,0:T(8,128)(2,1)}, u32[]{:S(2)}, u32[]{:S(2)}) async-start(bf16[16,24,2048]{2,1,0:T(8,128)(2,1)} %fusion.1), calls=%async_computation.3 | async-start | bytes 3145728 | tf_op jit(solution)/shard_map/all_to_all | solution.py:22
  196.0 1.2 copy-start.3
  197.2 2.3 %copy-start.10 = (bf16[1,128,3584]{2,1,0:T(8,128)(2,1)S(1)}, bf16[1,128,3584]{2,1,0:T(8,128)(2,1)}, u32[]{:S(2)}) copy-start(bf16[1,128,3584]{2,1,0:T(8,128)(2,1)} %param.9) | copy-start | bytes 2752516
  197.2 2.7 %copy-start.11 = (s32[1,128,2]{1,2,0:T(2,128)S(1)}, s32[1,128,2]{1,2,0:T(2,128)}, u32[]{:S(2)}) copy-start(s32[1,128,2]{1,2,0:T(2,128)} %param.10) | copy-start | bytes 3076
  197.2 3.1 %copy-start.12 = (f32[1,224,16]{1,2,0:T(8,128)S(1)}, f32[1,224,16]{1,2,0:T(8,128)}, u32[]{:S(2)}) copy-start(f32[1,224,16]{1,2,0:T(8,128)} %param.17) | copy-start | bytes 43012
  199.3 11.3 %collective-permute-start.5 = (bf16[128,3584]{1,0:T(8,128)(2,1)S(1)}, bf16[128,3584]{1,0:T(8,128)(2,1)S(1)}, u32[]{:S(2)}, u32[]{:S(2)}) collective-permute-start(bf16[128,3584]{1,0:T(8,128)(2,1)S(1)} %shard_map.120), channel_id=1, source_target_pairs={{0,112},{16,0},{32,16},{48,32},{64,48},{80,64},{96,80},{112,96},{1... | collective-permute-start | bytes 2752520 | tf_op jit(solution)/shard_map/ppermute | solution.py:18
  200.0 11.6 %collective-permute-start = (bf16[384,128]{1,0:T(8,128)(2,1)S(1)}, bf16[384,128]{1,0:T(8,128)(2,1)S(1)}, u32[]{:S(2)}, u32[]{:S(2)}) collective-permute-start(bf16[384,128]{1,0:T(8,128)(2,1)S(1)} %select_reduce_fusion.1), channel_id=1, source_target_pairs={{0,16},{16,32},{32,48},{48,64},{64,80},{80,96},{96,112},{112,0},{1... | collective-permute-start | bytes 294920 | tf_op jit(solution)/shard_map/ppermute | solution.py:18
  200.3 13.9 %collective-permute-start.3 = (f32[224,16]{0,1:T(8,128)S(1)}, f32[224,16]{0,1:T(8,128)S(1)}, u32[]{:S(2)}, u32[]{:S(2)}) collective-permute-start(f32[224,16]{0,1:T(8,128)S(1)} %bitcast.75), channel_id=1, source_target_pairs={{0,112},{16,96},{32,80},{48,64},{64,48},{80,32},{96,16},{112,0},{1... | collective-permute-start | bytes 43016 | tf_op jit(solution)/shard_map/ppermute | solution.py:520
  211.7 6.1 %copy-start.4 = (bf16[128,3584]{1,0:T(8,128)(2,1)S(1)}, bf16[128,3584]{1,0:T(8,128)(2,1)}, u32[]{:S(2)}) copy-start(bf16[128,3584]{1,0:T(8,128)(2,1)} %shard_map.121.grads) | copy-start | bytes 2752516

commit v4 on v3

--- a/solution.py
+++ b/solution.py
@@ -18,8 +18,23 @@
     return lax.ppermute(value, "pp", pairs)
 
 
+def diagonal(ranks):
+    side = int(ranks**0.5)
+    return [row * side + (row + turn) % side for turn in range(side) for row in range(side)]
+
+
+def place_of(rank, ranks):
+    side = int(ranks**0.5)
+    bits = side.bit_length() - 1
+    row, column = rank >> bits, rank & (side - 1)
+    return (((column - row) & (side - 1)) << bits) + row
+
+
 def exchange(value):
-    return lax.all_to_all(value, "ep", split_axis=0, concat_axis=0, tiled=True)
+    order = diagonal(lax.axis_size("ep"))
+    return lax.all_to_all(
+        value, "ep", split_axis=0, concat_axis=0, axis_index_groups=[order], tiled=True
+    )
 
 
 def split_two(value):
@@ -98,7 +113,8 @@
     ]
     for load in loads:
         load.start()
-    rows_bwd, rows_fwd = slot_rows([ids_bwd[...], ids_fwd[...]], expert_count, capacity)
+    places = [place_of(ids[...], expert_count) for ids in (ids_bwd, ids_fwd)]
+    rows_bwd, rows_fwd = slot_rows(places, expert_count, capacity)
     slots[...] = jnp.concatenate(rows_bwd + rows_fwd, axis=0)
     picker[0] = picker_of(rows_fwd, slot_count)
     picker[1] = picker_of(rows_bwd, slot_count)
@@ -195,7 +211,8 @@
     )(got, got, joined_weight, joined_weight, proj_weight)
 
 
-def row_grad_kernel(block, gate_grad, up_grad, weight, dots, out):
+def row_grad_kernel(block, gate_grad, up_grad, weight, dots, *refs):
+    out = refs[-1]
     step = pl.program_id(0)
     units = gate_grad.shape[1]
     contract = (((1,), (1,)), ((), ()))
@@ -212,7 +229,7 @@
         out[:, out.shape[1] - LANES :] = extra.astype(BF16)
 
 
-def row_gradient(gate_grad, up_grad, joined_weight, dots):
+def row_gradient(gate_grad, up_grad, joined_weight, dots, earlier):
     slot_count, units = gate_grad.shape
     width = joined_weight.shape[0]
     block = 512
@@ -225,10 +242,11 @@
             whole,
             pl.BlockSpec((block, 2 * units), lambda j: (j, 0)),
             pl.BlockSpec((slot_count, LANES), lambda j: (0, 0)),
+            pl.BlockSpec(memory_space=pl.ANY),
         ],
         pl.BlockSpec((slot_count, width + LANES), lambda j: (0, 0)),
         jax.ShapeDtypeStruct((slot_count, width + LANES), BF16),
-    )(gate_grad, up_grad, joined_weight, dots)
+    )(gate_grad, up_grad, joined_weight, dots, earlier)
 
 
 def forward_hidden_kernel(acts, gate_w, up_w, out):
@@ -255,23 +273,23 @@
     )(got, joined_weight, joined_weight)
 
 
-def produce_kernel(hidden, weight, out):
-    out[...] = jnp.dot(hidden[...], weight[...], preferred_element_type=F32).astype(BF16)
-
-
-def produce(hidden, proj_weight, first, columns):
+def produce_kernel(hidden, weight, *refs):
+    refs[-1][...] = jnp.dot(hidden[...], weight[...], preferred_element_type=F32).astype(BF16)
+
+
+def produce(hidden, proj_weight, first, columns, block, earlier=()):
     slot_count, units = hidden.shape
-    block = 896
     return call(
         produce_kernel,
         (columns // block,),
         [
             pl.BlockSpec((slot_count, units), lambda j: (0, 0)),
             pl.BlockSpec((units, block), lambda j: (0, first // block + j)),
-        ],
+        ]
+        + [pl.BlockSpec(memory_space=pl.ANY)] * len(earlier),
         pl.BlockSpec((slot_count, block), lambda j: (0, j)),
         jax.ShapeDtypeStruct((slot_count, columns), BF16),
-    )(hidden, proj_weight)
+    )(hidden, proj_weight, *earlier)
 
 
 def mix_rows(mixer, rows, residual):
@@ -285,7 +303,7 @@
     out[...] = mix_rows(mixer, rows, residual).astype(BF16)
 
 
-def mix_early(mixer, rows, residual, block=896):
+def mix_early(mixer, rows, residual, block):
     slot_count, tokens = mixer.shape
     return call(
         mix_early_kernel,
@@ -321,7 +339,7 @@
         summed[...] = total[:, : mirrored.shape[1]] + mirrored[...]
 
 
-def mix_late(mixer, returned, residual, mirrored, early, grads, capacity, wide, block=896):
+def mix_late(mixer, returned, residual, mirrored, early, grads, capacity, wide, block):
     slot_count, tokens = mixer.shape
     columns = returned.shape[1] - wide
     first = residual.shape[1] - columns
@@ -464,17 +482,17 @@
     tokens_fwd = forward_acts[0]
     tokens_bwd = backward_acts[0]
     upstream = upstream_grad[0]
+    ranks = lax.axis_size("ep")
     ids_fwd = forward_ids[0].T
     ids_bwd = backward_ids[0].T
     mirrored = mirror_grads[0]
     row_count, width = tokens_fwd.shape
     top_count = ids_fwd.shape[0]
     expert_count = router_section.shape[1]
-    ranks = lax.axis_size("ep")
     capacity = 3 * row_count * top_count // (2 * ranks)
     slot_count = expert_count * capacity
     shard = width // ranks
-    early = width // 2
+    early = 3 * width // 7
 
     sent_bwd, sent_fwd, slots = dispatch(
         ids_bwd, ids_fwd, tokens_bwd, upstream, tokens_fwd, expert_count, capacity
@@ -486,19 +504,22 @@
     got_fwd = exchange(sent_fwd)
 
     gate_part, up_part, dots = backward_hidden(got_bwd, joined_weight, proj_weight)
-    back = exchange(row_gradient(gate_part, up_part, joined_weight, dots))
+    residual = shifted(jnp.where(here, tokens_fwd, 0), 1)
+    back = exchange(row_gradient(gate_part, up_part, joined_weight, dots, residual))
 
     hidden = forward_hidden(got_fwd, joined_weight)
-    produced_early = shifted(produce(hidden, proj_weight, 0, early), 1)
-    produced_late = shifted(produce(hidden, proj_weight, early, width - early), 1)
-    residual = shifted(jnp.where(here, tokens_fwd, 0), 1)
+    rows_early = produce(hidden, proj_weight, 0, early, early // 2)
+    rows_late = produce(hidden, proj_weight, early, width - early, early // 3, (rows_early,))
+    produced_early = shifted(rows_early, 1)
+    produced_late = shifted(rows_late, 1)
     _, gates_fwd = gating(tokens_fwd, ids_fwd, router_section)
     hot_fwd = slot_hot(slots[top_count:], slot_count)
     mixer_fwd = shifted(weighted(hot_fwd, gates_fwd).astype(BF16), 1)
     returned_early = exchange(produced_early)
-    next_early = mix_early(mixer_fwd, returned_early, residual)
-
-    affinity, gates_bwd = gating(tokens_bwd, ids_bwd, router_section)
+    next_early = mix_early(mixer_fwd, returned_early, residual, early // 2)
+
+    router_bwd = lax.optimization_barrier((router_section, rows_late))[0]
+    affinity, gates_bwd = gating(tokens_bwd, ids_bwd, router_bwd)
     hot_bwd = slot_hot(slots[:top_count], slot_count)
     mixer_bwd = weighted(hot_bwd, gates_bwd).astype(BF16)
     logit_pair = logit_gradient(back, slots, ids_bwd, affinity, expert_count)
@@ -510,16 +531,25 @@
     router_part = ((router_pair[:expert_count] + router_pair[expert_count:]) / row_count).astype(
         BF16
     )
+    by_rank = router_part.reshape(expert_count, ranks, shard).transpose(1, 0, 2)
     wide = -(-shard // LANES) * LANES
     router_blocks = jnp.pad(
-        router_part.reshape(expert_count, ranks, shard).transpose(1, 0, 2),
+        jnp.stack([by_rank[rank] for rank in diagonal(ranks)]),
         ((0, 0), (0, capacity - expert_count), (0, wide - shard)),
     ).reshape(slot_count, wide)
     returned_late = exchange(jnp.concatenate([produced_late, router_blocks], axis=1))
     count = lax.axis_size("pp")
     mirrored = lax.ppermute(mirrored, "pp", [(i, count - 1 - i) for i in range(count)])
     next_acts, router_grads = mix_late(
-        mixer_fwd, returned_late, residual, mirrored.T, next_early, next_grads, capacity, wide
+        mixer_fwd,
+        returned_late,
+        residual,
+        mirrored.T,
+        next_early,
+        next_grads,
+        capacity,
+        wide,
+        early // 3,
     )
     return (next_acts[None], next_grads[None], router_grads.T[None])
 

time: 221 us -> 220 us (level)
  waiting for transfers between devices: 55.8 us -> 45.7 us
  starting transfers between devices: 21.2 us -> 26.6 us
    all_to_all x4, waiting for transfers between devices: 35.7 us -> 28.6 us  [exchange(): lax.all_to_all(value, 'ep', split_axis=0, concat_axis=0, axis_index_group...]
    all_to_all x4, starting transfers between devices: 16.3 us -> 22 us  [exchange(): lax.all_to_all(value, 'ep', split_axis=0, concat_axis=0, axis_index_group...]
    ppermute x5, waiting for transfers between devices: 20.1 us -> 17.2 us  [shifted(): return lax.ppermute(value, 'pp', pairs)]
    unnamed x26 -> x44, local copies, waits for them, and re-layouts: 6.14 us -> 8.09 us
  transfers between devices with their start and end apart: 10 -> 10, of which waited for: 6 -> 6; matrix products, arithmetic and copies ran while one was open for 3% -> 3% of each run, Pallas kernels for 22% -> 23%
where the time goes in v4:
time: 220 us; the launch traced here: 218 us
  blocking collectives  72.4 us (33%)
  Pallas kernels  58.9 us (27%)
  waiting for transfers between devices  45.7 us (21%)
  starting transfers between devices  26.6 us (12%)
  local copies, waits for them, and re-layouts  8.34 us (4%)
  other arithmetic  4.34 us (2%)
    all_to_all x1, blocking collectives, exchange(): lax.all_to_all(value, 'ep', split_axis=0, concat_axis=0, axis_index_group...  72.4 us
    all_to_all x4, waiting for transfers between devices, exchange(): lax.all_to_all(value, 'ep', split_axis=0, concat_axis=0, axis_index_group...  28.6 us
    all_to_all x4, starting transfers between devices, exchange(): lax.all_to_all(value, 'ep', split_axis=0, concat_axis=0, axis_index_group...  22 us
    ppermute x5, waiting for transfers between devices, shifted(): return lax.ppermute(value, 'pp', pairs)  17.2 us
    pallas_call x1, Pallas kernels, backward_hidden(): call(backward_hidden_kernel, (count,), [pl.BlockSpec((slot_count, width),...  15 us
    pallas_call x1, Pallas kernels, row_gradient(): call(functools.partial(row_grad_kernel, block), (width // block,), [whole...  10.6 us
    pallas_call x2, Pallas kernels, produce(): call(produce_kernel, (columns // block,), [pl.BlockSpec((slot_count, unit...  9.21 us
    pallas_call x1, Pallas kernels, forward_hidden(): call(forward_hidden_kernel, (count,), [pl.BlockSpec((slot_count, width),...  9.11 us
  transfers between devices with their start and end apart: 10, of which 6 were waited for; matrix products, arithmetic and copies ran while one was open for 3% of the time, Pallas kernels for 23%

profile of v4, /device:TPU:0, one launch (start us, length us, event | category | flops | bytes accessed | tf_op | source)
XLA Modules:
  0.0 218.2 jit_solution(11824429934583332934)
XLA Ops:
  0.6 5.1 %shard_map.112 = (bf16[384,7168]{1,0:T(8,128)(2,1)S(1)}, bf16[384,3584]{1,0:T(8,128)(2,1)}, s32[4,128]{1,0:T(4,128)}) custom-call(s32[2,128]{1,0:T(2,128)} %bitcast.55, s32[2,128]{1,0:T(2,128)} %bitcast.85, bf16[128,3584]{1,0:T(8,128)(2,1)} %bitcast.68, bf16[128,3584]{1,0:T(8,128)(2,1)} %bitcast.49, bf16[128,3584]{1,0:T(8,128)(2,1)} %bitcast.69), custom_call_target="tpu_custom_call" | custom-call | flops 1000 | bytes 1000 | tf_op jit(solution)/shard_map/pallas_call | solution.py:139
  5.7 72.4 %all_to_all.53 = bf16[16,24,7168]{2,1,0:T(8,128)(2,1)} all-to-all(bf16[16,24,7168]{2,1,0:T(8,128)(2,1)S(1)} %bitcast.47), channel_id=1, replica_groups={{0,5,10,15,1,6,11,12,2,7,8,13,3,4,9,14},{16,21,26,31,17,22,27,28,18,23,..., dimensions={0} | all-to-all | bytes 11010048 | tf_op jit(solution)/shard_map/all_to_all | solution.py:35
  78.2 3.7 %all-to-all-start.1 = ((bf16[16,24,3584]{2,1,0:T(8,128)(2,1)}), bf16[16,24,3584]{2,1,0:T(8,128)(2,1)S(1)}, u32[]{:S(2)}, u32[]{:S(2)}) async-start(bf16[16,24,3584]{2,1,0:T(8,128)(2,1)} %bitcast.71), calls=%async_computation.1 | async-start | bytes 5505024 | tf_op jit(solution)/shard_map/all_to_all | solution.py:35
  81.9 1.2 broadcast_select_fusion
  83.2 0.0 collective-permute-start.2
  83.2 15.0 %shard_map.116 = (bf16[384,1024]{1,0:T(8,128)(2,1)S(1)}, bf16[384,1024]{1,0:T(8,128)(2,1)S(1)}, f32[384,128]{1,0:T(8,128)S(1)}) custom-call(bf16[384,7168]{1,0:T(8,128)(2,1)} %bitcast.66, bf16[384,7168]{1,0:T(8,128)(2,1)} %bitcast.67, bf16[3584,2048]{1,0:T(8,128)(2,1)} %bitcast.58, bf16[3584,2048]{1,0:T(8,128)(2,1)} %bitcast.59, bf16[1024,3584]{1,0:T(8,128)(2,1)} %bitcast.63), custom_call_target="tpu_custom_call" | custom-call | flops 1000 | bytes 1000 | tf_op jit(solution)/shard_map/pallas_call | solution.py:191
  98.2 0.0 collective-permute-done.2.refs_0_.residual
  98.2 10.6 %shard_map.117 = bf16[384,3712]{1,0:T(8,128)(2,1)S(1)} custom-call(bf16[384,1024]{1,0:T(8,128)(2,1)S(1)} %get-tuple-element.25.gate_grad, bf16[384,1024]{1,0:T(8,128)(2,1)S(1)} %get-tuple-element.26.up_grad, bf16[3584,2048]{1,0:T(8,128)(2,1)} %bitcast.60, f32[384,128]{1,0:T(8,128)S(1)} %get-tuple-element.27.dots, ...), custom_call_target="tpu_custom_call" | custom-call | flops 1000 | bytes 1000 | tf_op jit(solution)/shard_map/pallas_call | solution.py:237
  108.8 1.6 copy-done
  110.4 1.0 copy-done.3
  111.4 5.8 %all-to-all-done.1 = bf16[16,24,3584]{2,1,0:T(8,128)(2,1)S(1)} async-done(((bf16[16,24,3584]{2,1,0:T(8,128)(2,1)}), bf16[16,24,3584]{2,1,0:T(8,128)(2,1)S(1)}, u32[]{:S(2)}, u32[]{:S(2)}) %all-to-all-start.1) | async-done | bytes 2752544 | tf_op jit(solution)/shard_map/all_to_all | solution.py:35
  117.2 1.6 copy-done.1
  118.8 6.5 %all-to-all-start.2 = ((bf16[16,24,3712]{2,1,0:T(8,128)(2,1)}), bf16[16,24,3712]{2,1,0:T(8,128)(2,1)S(1)}, u32[]{:S(2)}, u32[]{:S(2)}) async-start(bf16[16,24,3712]{2,1,0:T(8,128)(2,1)} %bitcast.45), calls=%async_computation.2 | async-start | bytes 5701632 | tf_op jit(solution)/shard_map/all_to_all | solution.py:35
  125.3 1.8 copy-done.2
  127.1 9.1 %shard_map.113.hidden = bf16[384,1024]{1,0:T(8,128)(2,1)S(1)} custom-call(bf16[384,3584]{1,0:T(8,128)(2,1)S(1)} %bitcast.46, bf16[3584,2048]{1,0:T(8,128)(2,1)} %bitcast.61, bf16[3584,2048]{1,0:T(8,128)(2,1)} %bitcast.62), custom_call_target="tpu_custom_call" | custom-call | flops 1000 | bytes 1000 | tf_op jit(solution)/shard_map/pallas_call | solution.py:263
  136.2 3.9 %shard_map.114.refs_0_ = bf16[384,1536]{1,0:T(8,128)(2,1)} custom-call(bf16[384,1024]{1,0:T(8,128)(2,1)S(1)} %shard_map.113.hidden, bf16[1024,3584]{1,0:T(8,128)(2,1)} %bitcast.64), custom_call_target="tpu_custom_call" | custom-call | flops 1000 | bytes 1000 | tf_op jit(solution)/shard_map/pallas_call | solution.py:282
  140.1 5.3 %shard_map.115 = bf16[384,2048]{1,0:T(8,128)(2,1)} custom-call(bf16[384,1024]{1,0:T(8,128)(2,1)S(1)} %shard_map.113.hidden, bf16[1024,3584]{1,0:T(8,128)(2,1)} %bitcast.65, bf16[384,1536]{1,0:T(8,128)(2,1)} %shard_map.114.refs_0_), custom_call_target="tpu_custom_call" | custom-call | flops 1000 | bytes 1000 | tf_op jit(solution)/shard_map/pallas_call | solution.py:282
  145.4 0.0 collective-permute-start.4
  145.4 1.6 collective-permute-start.1
  147.0 0.0 copy-done.8
  147.0 0.3 fusion.8
  147.3 0.0 copy-done.9
  147.4 13.3 %all-to-all-done.2 = bf16[16,24,3712]{2,1,0:T(8,128)(2,1)S(1)} async-done(((bf16[16,24,3712]{2,1,0:T(8,128)(2,1)}), bf16[16,24,3712]{2,1,0:T(8,128)(2,1)S(1)}, u32[]{:S(2)}, u32[]{:S(2)}) %all-to-all-start.2) | async-done | bytes 2850848 | tf_op jit(solution)/shard_map/all_to_all | solution.py:35
  160.8 0.3 shard_map.118.logit_pair
  161.0 0.9 copy-done.12
  161.9 0.3 fusion.6
  162.2 0.2 reshape.65
  162.6 0.0 collective-permute-done.4
  162.6 7.2 %all-to-all-start.4 = ((bf16[16,24,1536]{2,1,0:T(8,128)(2,1)}), bf16[16,24,1536]{2,1,0:T(8,128)(2,1)}, u32[]{:S(2)}, u32[]{:S(2)}) async-start(bf16[16,24,1536]{2,1,0:T(8,128)(2,1)} %bitcast.23), calls=%async_computation.4 | async-start | bytes 2359296 | tf_op jit(solution)/shard_map/all_to_all | solution.py:35
  169.9 9.5 %collective-permute-done.1 = bf16[384,2048]{1,0:T(8,128)(2,1)} collective-permute-done((bf16[384,2048]{1,0:T(8,128)(2,1)}, bf16[384,2048]{1,0:T(8,128)(2,1)}, u32[]{:S(2)}, u32[]{:S(2)}) %collective-permute-start.1) | collective-permute-done | bytes 1572896 | tf_op jit(solution)/shard_map/ppermute | solution.py:18
  179.4 2.8 %fusion.1 = bf16[16,24,2304]{2,1,0:T(8,128)(2,1)} fusion(bf16[16,16,224]{2,1,0:T(8,128)(2,1)S(1)} %constant_dynamic-update-slice_fusion, bf16[16,24,2048]{2,1,0:T(8,128)(2,1)} %bitcast.16), kind=kLoop, calls=%fused_computation.2 | loop fusion | flops 5308416 | bytes 3457024 | tf_op jit(solution)/shard_map/concatenate | solution.py:540
  182.2 4.1 %all-to-all-done.4 = bf16[16,24,1536]{2,1,0:T(8,128)(2,1)} async-done(((bf16[16,24,1536]{2,1,0:T(8,128)(2,1)}), bf16[16,24,1536]{2,1,0:T(8,128)(2,1)}, u32[]{:S(2)}, u32[]{:S(2)}) %all-to-all-start.4) | async-done | bytes 1179680 | tf_op jit(solution)/shard_map/all_to_all | solution.py:35
  186.4 4.4 %all-to-all-start.3 = ((bf16[16,24,2304]{2,1,0:T(8,128)(2,1)}), bf16[16,24,2304]{2,1,0:T(8,128)(2,1)}, u32[]{:S(2)}, u32[]{:S(2)}) async-start(bf16[16,24,2304]{2,1,0:T(8,128)(2,1)} %fusion.1), calls=%async_computation.3 | async-start | bytes 3538944 | tf_op jit(solution)/shard_map/all_to_all | solution.py:35
  190.9 0.0 copy-start.7
  190.9 1.2 copy-done.7
  192.1 2.1 shard_map.120
  194.2 0.0 collective-permute-start.5
  194.2 0.3 fusion.4
  194.7 0.1 select_reduce_fusion.1
  194.7 0.5 collective-permute-start
  195.2 2.5 %collective-permute-start.3 = (f32[224,16]{0,1:T(8,128)S(1)}, f32[224,16]{0,1:T(8,128)S(1)}, u32[]{:S(2)}, u32[]{:S(2)}) collective-permute-start(f32[224,16]{0,1:T(8,128)S(1)} %bitcast.87), channel_id=1, source_target_pairs={{0,112},{16,96},{32,80},{48,64},{64,48},{80,32},{96,16},{112,0},{1... | collective-permute-start | bytes 43016 | tf_op jit(solution)/shard_map/ppermute | solution.py:542
  197.7 7.6 %collective-permute-done.5.rows = bf16[128,3584]{1,0:T(8,128)(2,1)S(1)} collective-permute-done((bf16[128,3584]{1,0:T(8,128)(2,1)S(1)}, bf16[128,3584]{1,0:T(8,128)(2,1)S(1)}, u32[]{:S(2)}, u32[]{:S(2)}) %collective-permute-start.5) | collective-permute-done | bytes 917536 | tf_op jit(solution)/shard_map/ppermute | solution.py:18
  205.3 1.0 shard_map.121.grads
  206.4 0.0 collective-permute-done.mixer
  206.4 2.5 %shard_map.119.early = bf16[128,3584]{1,0:T(8,128)(2,1)} custom-call(bf16[384,128]{1,0:T(8,128)(2,1)S(1)} %collective-permute-done.mixer, bf16[384,1536]{1,0:T(8,128)(2,1)} %bitcast.24.rows, bf16[128,3584]{1,0:T(8,128)(2,1)S(1)} %copy-done.4), custom_call_target="tpu_custom_call" | custom-call | flops 1000 | bytes 1000 | tf_op jit(solution)/shard_map/pallas_call | solution.py:308
  208.8 0.0 collective-permute-done.3
  208.8 5.3 %all-to-all-done.3 = bf16[16,24,2304]{2,1,0:T(8,128)(2,1)} async-done(((bf16[16,24,2304]{2,1,0:T(8,128)(2,1)}), bf16[16,24,2304]{2,1,0:T(8,128)(2,1)}, u32[]{:S(2)}, u32[]{:S(2)}) %all-to-all-start.3) | async-done | bytes 1769504 | tf_op jit(solution)/shard_map/all_to_all | solution.py:35
  214.1 4.0 %shard_map.122 = (bf16[128,3584]{1,0:T(8,128)(2,1)}, f32[16,224]{1,0:T(8,128)}) custom-call(bf16[384,128]{1,0:T(8,128)(2,1)S(1)} %collective-permute-done.mixer, bf16[384,2304]{1,0:T(8,128)(2,1)} %bitcast.21.rows.parts, bf16[128,3584]{1,0:T(8,128)(2,1)S(1)} %copy-done.5, bf16[384,2304]{1,0:T(8,128)(2,1)} %bitcast.21.rows.parts, ...), custom_call_target="tpu_custom_call", output_to_operand_aliasing={{0}: (5, {})} | custom-call | flops 1000 | bytes 1000 | tf_op jit(solution)/shard_map/pallas_call | solution.py:348
  (46 shorter events, 0.4 us)
Async XLA Ops:
  78.2 39.0 %all-to-all-start.1 = ((bf16[16,24,3584]{2,1,0:T(8,128)(2,1)}), bf16[16,24,3584]{2,1,0:T(8,128)(2,1)S(1)}, u32[]{:S(2)}, u32[]{:S(2)}) async-start(bf16[16,24,3584]{2,1,0:T(8,128)(2,1)} %bitcast.71), calls=%async_computation.1 | async-start | bytes 5505024 | tf_op jit(solution)/shard_map/all_to_all | solution.py:35
  83.2 15.1 %collective-permute-start.2 = (bf16[128,3584]{1,0:T(8,128)(2,1)S(1)}, bf16[128,3584]{1,0:T(8,128)(2,1)S(1)}, u32[]{:S(2)}, u32[]{:S(2)}) collective-permute-start(bf16[128,3584]{1,0:T(8,128)(2,1)S(1)} %broadcast_select_fusion), channel_id=1, source_target_pairs={{0,16},{16,32},{32,48},{48,64},{64,80},{80,96},{96,112},{112,0},{1... | collective-permute-start | bytes 2752520 | tf_op jit(solution)/shard_map/ppermute | solution.py:18
  108.8 1.6 copy-start
  110.4 1.0 copy-start.3
  117.2 1.6 copy-start.1
  118.8 42.0 %all-to-all-start.2 = ((bf16[16,24,3712]{2,1,0:T(8,128)(2,1)}), bf16[16,24,3712]{2,1,0:T(8,128)(2,1)S(1)}, u32[]{:S(2)}, u32[]{:S(2)}) async-start(bf16[16,24,3712]{2,1,0:T(8,128)(2,1)} %bitcast.45), calls=%async_computation.2 | async-start | bytes 5701632 | tf_op jit(solution)/shard_map/all_to_all | solution.py:35
  125.3 1.8 copy-start.2
  140.1 6.9 %copy-start.8 = (bf16[1,3584,16]{1,2,0:T(8,128)(2,1)S(1)}, bf16[1,3584,16]{1,2,0:T(8,128)(2,1)}, u32[]{:S(2)}) copy-start(bf16[1,3584,16]{1,2,0:T(8,128)(2,1)} %param.16) | copy-start | bytes 344068
  140.1 6.9 %copy-start.11 = (bf16[1,128,3584]{2,1,0:T(8,128)(2,1)S(1)}, bf16[1,128,3584]{2,1,0:T(8,128)(2,1)}, u32[]{:S(2)}) copy-start(bf16[1,128,3584]{2,1,0:T(8,128)(2,1)} %param.11) | copy-start | bytes 2752516
  140.1 7.3 %copy-start.9 = (s32[1,128,2]{1,2,0:T(2,128)S(1)}, s32[1,128,2]{1,2,0:T(2,128)}, u32[]{:S(2)}) copy-start(s32[1,128,2]{1,2,0:T(2,128)} %param.12) | copy-start | bytes 3076
  140.1 20.7 %copy-start.10 = (s32[4,128]{1,0:T(4,128)S(1)}, s32[4,128]{1,0:T(4,128)}, u32[]{:S(2)}) copy-start(s32[4,128]{1,0:T(4,128)} %get-tuple-element.21.slots) | copy-start | bytes 6148
  145.4 17.2 %collective-permute-start.4 = (bf16[384,1536]{1,0:T(8,128)(2,1)}, bf16[384,1536]{1,0:T(8,128)(2,1)}, u32[]{:S(2)}, u32[]{:S(2)}) collective-permute-start(bf16[384,1536]{1,0:T(8,128)(2,1)} %shard_map.114.refs_0_), channel_id=1, source_target_pairs={{0,16},{16,32},{32,48},{48,64},{64,80},{80,96},{96,112},{112,0},{1... | collective-permute-start | bytes 3538952 | tf_op jit(solution)/shard_map/ppermute | solution.py:18
  145.4 34.0 %collective-permute-start.1 = (bf16[384,2048]{1,0:T(8,128)(2,1)}, bf16[384,2048]{1,0:T(8,128)(2,1)}, u32[]{:S(2)}, u32[]{:S(2)}) collective-permute-start(bf16[384,2048]{1,0:T(8,128)(2,1)} %shard_map.115), channel_id=1, source_target_pairs={{0,16},{16,32},{32,48},{48,64},{64,80},{80,96},{96,112},{112,0},{1... | collective-permute-start | bytes 4718600 | tf_op jit(solution)/shard_map/ppermute | solution.py:18
  160.8 1.2 copy-start.12
  162.6 23.8 %all-to-all-start.4 = ((bf16[16,24,1536]{2,1,0:T(8,128)(2,1)}), bf16[16,24,1536]{2,1,0:T(8,128)(2,1)}, u32[]{:S(2)}, u32[]{:S(2)}) async-start(bf16[16,24,1536]{2,1,0:T(8,128)(2,1)} %bitcast.23), calls=%async_computation.4 | async-start | bytes 2359296 | tf_op jit(solution)/shard_map/all_to_all | solution.py:35
  186.4 27.7 %all-to-all-start.3 = ((bf16[16,24,2304]{2,1,0:T(8,128)(2,1)}), bf16[16,24,2304]{2,1,0:T(8,128)(2,1)}, u32[]{:S(2)}, u32[]{:S(2)}) async-start(bf16[16,24,2304]{2,1,0:T(8,128)(2,1)} %fusion.1), calls=%async_computation.3 | async-start | bytes 3538944 | tf_op jit(solution)/shard_map/all_to_all | solution.py:35
  190.9 1.2 copy-start.7
  192.1 2.2 copy-start.13
  192.1 2.5 %copy-start.14 = (s32[1,128,2]{1,2,0:T(2,128)S(1)}, s32[1,128,2]{1,2,0:T(2,128)}, u32[]{:S(2)}) copy-start(s32[1,128,2]{1,2,0:T(2,128)} %param.10) | copy-start | bytes 3076
  192.1 3.2 %copy-start.15 = (f32[1,224,16]{1,2,0:T(8,128)S(1)}, f32[1,224,16]{1,2,0:T(8,128)}, u32[]{:S(2)}) copy-start(f32[1,224,16]{1,2,0:T(8,128)} %param.17) | copy-start | bytes 43012
  192.1 14.3 %copy-start.4 = (bf16[128,3584]{1,0:T(8,128)(2,1)S(1)}, bf16[128,3584]{1,0:T(8,128)(2,1)}, u32[]{:S(2)}) copy-start(bf16[128,3584]{1,0:T(8,128)(2,1)} %copy-done.3) | copy-start | bytes 2752516
  194.2 11.1 %collective-permute-start.5 = (bf16[128,3584]{1,0:T(8,128)(2,1)S(1)}, bf16[128,3584]{1,0:T(8,128)(2,1)S(1)}, u32[]{:S(2)}, u32[]{:S(2)}) collective-permute-start(bf16[128,3584]{1,0:T(8,128)(2,1)S(1)} %shard_map.120), channel_id=1, source_target_pairs={{0,112},{16,0},{32,16},{48,32},{64,48},{80,64},{96,80},{112,96},{1... | collective-permute-start | bytes 2752520 | tf_op jit(solution)/shard_map/ppermute | solution.py:18
  194.6 19.5 %copy-start.5 = (bf16[128,3584]{1,0:T(8,128)(2,1)S(1)}, bf16[128,3584]{1,0:T(8,128)(2,1)}, u32[]{:S(2)}) copy-start(bf16[128,3584]{1,0:T(8,128)(2,1)} %copy-done.3) | copy-start | bytes 2752516
  194.7 11.6 %collective-permute-start = (bf16[384,128]{1,0:T(8,128)(2,1)S(1)}, bf16[384,128]{1,0:T(8,128)(2,1)S(1)}, u32[]{:S(2)}, u32[]{:S(2)}) collective-permute-start(bf16[384,128]{1,0:T(8,128)(2,1)S(1)} %select_reduce_fusion.1), channel_id=1, source_target_pairs={{0,16},{16,32},{32,48},{48,64},{64,80},{80,96},{96,112},{112,0},{1... | collective-permute-start | bytes 294920 | tf_op jit(solution)/shard_map/ppermute | solution.py:18
  195.2 13.6 %collective-permute-start.3 = (f32[224,16]{0,1:T(8,128)S(1)}, f32[224,16]{0,1:T(8,128)S(1)}, u32[]{:S(2)}, u32[]{:S(2)}) collective-permute-start(f32[224,16]{0,1:T(8,128)S(1)} %bitcast.87), channel_id=1, source_target_pairs={{0,112},{16,96},{32,80},{48,64},{64,48},{80,32},{96,16},{112,0},{1... | collective-permute-start | bytes 43016 | tf_op jit(solution)/shard_map/ppermute | solution.py:542
  206.3 7.8 %copy-start.6 = (bf16[128,3584]{1,0:T(8,128)(2,1)S(1)}, bf16[128,3584]{1,0:T(8,128)(2,1)}, u32[]{:S(2)}) copy-start(bf16[128,3584]{1,0:T(8,128)(2,1)} %shard_map.121.grads) | copy-start | bytes 2752516

commit v5 on v4

--- a/solution.py
+++ b/solution.py
@@ -305,15 +305,16 @@
 
 def mix_early(mixer, rows, residual, block):
     slot_count, tokens = mixer.shape
+    first = residual.shape[1] - rows.shape[1]
     return call(
         mix_early_kernel,
         (rows.shape[1] // block,),
         [
             pl.BlockSpec((slot_count, tokens), lambda j: (0, 0)),
             pl.BlockSpec((slot_count, block), lambda j: (0, j)),
-            pl.BlockSpec((tokens, block), lambda j: (0, j)),
-        ],
-        pl.BlockSpec((tokens, block), lambda j: (0, j)),
+            pl.BlockSpec((tokens, block), lambda j: (0, first // block + j)),
+        ],
+        pl.BlockSpec((tokens, block), lambda j: (0, first // block + j)),
         jax.ShapeDtypeStruct(residual.shape, BF16),
     )(mixer, rows, residual)
 
@@ -342,7 +343,6 @@
 def mix_late(mixer, returned, residual, mirrored, early, grads, capacity, wide, block):
     slot_count, tokens = mixer.shape
     columns = returned.shape[1] - wide
-    first = residual.shape[1] - columns
     stays = pl.BlockSpec(memory_space=pl.ANY)
     whole = pl.BlockSpec(mirrored.shape, lambda j: (0, 0))
     return call(
@@ -351,13 +351,13 @@
         [
             pl.BlockSpec((slot_count, tokens), lambda j: (0, 0)),
             pl.BlockSpec((slot_count, block), lambda j: (0, j)),
-            pl.BlockSpec((tokens, block), lambda j: (0, first // block + j)),
+            pl.BlockSpec((tokens, block), lambda j: (0, j)),
             pl.BlockSpec((slot_count, wide), lambda j: (0, columns // wide)),
             whole,
             stays,
             stays,
         ],
-        [pl.BlockSpec((tokens, block), lambda j: (0, first // block + j)), whole],
+        [pl.BlockSpec((tokens, block), lambda j: (0, j)), whole],
         [
             jax.ShapeDtypeStruct(residual.shape, BF16),
             jax.ShapeDtypeStruct(mirrored.shape, F32),
@@ -508,15 +508,17 @@
     back = exchange(row_gradient(gate_part, up_part, joined_weight, dots, residual))
 
     hidden = forward_hidden(got_fwd, joined_weight)
-    rows_early = produce(hidden, proj_weight, 0, early, early // 2)
-    rows_late = produce(hidden, proj_weight, early, width - early, early // 3, (rows_early,))
+    rows_early = produce(hidden, proj_weight, width - early, early, early // 3)
+    rows_late = produce(
+        hidden, proj_weight, 0, width - early, (width - early) // 2, (rows_early,)
+    )
     produced_early = shifted(rows_early, 1)
     produced_late = shifted(rows_late, 1)
     _, gates_fwd = gating(tokens_fwd, ids_fwd, router_section)
     hot_fwd = slot_hot(slots[top_count:], slot_count)
     mixer_fwd = shifted(weighted(hot_fwd, gates_fwd).astype(BF16), 1)
     returned_early = exchange(produced_early)
-    next_early = mix_early(mixer_fwd, returned_early, residual, early // 2)
+    next_early = mix_early(mixer_fwd, returned_early, residual, early // 3)
 
     router_bwd = lax.optimization_barrier((router_section, rows_late))[0]
     affinity, gates_bwd = gating(tokens_bwd, ids_bwd, router_bwd)
@@ -549,7 +551,7 @@
         next_grads,
         capacity,
         wide,
-        early // 3,
+        (width - early) // 2,
     )
     return (next_acts[None], next_grads[None], router_grads.T[None])
 

time: 220 us -> 218 us (level)
  no operation moved by 1% of the time
where the time goes in v5:
time: 218 us; the launch traced here: 217 us
  blocking collectives  72.4 us (33%)
  Pallas kernels  58.4 us (27%)
  waiting for transfers between devices  44.9 us (21%)
  starting transfers between devices  26.5 us (12%)
  local copies, waits for them, and re-layouts  8.34 us (4%)
  other arithmetic  4.34 us (2%)
    all_to_all x1, blocking collectives, exchange(): lax.all_to_all(value, 'ep', split_axis=0, concat_axis=0, axis_index_group...  72.4 us
    all_to_all x4, waiting for transfers between devices, exchange(): lax.all_to_all(value, 'ep', split_axis=0, concat_axis=0, axis_index_group...  27.7 us
    all_to_all x4, starting transfers between devices, exchange(): lax.all_to_all(value, 'ep', split_axis=0, concat_axis=0, axis_index_group...  21.9 us
    ppermute x5, waiting for transfers between devices, shifted(): return lax.ppermute(value, 'pp', pairs)  17.2 us
    pallas_call x1, Pallas kernels, backward_hidden(): call(backward_hidden_kernel, (count,), [pl.BlockSpec((slot_count, width),...  15 us
    pallas_call x1, Pallas kernels, row_gradient(): call(functools.partial(row_grad_kernel, block), (width // block,), [whole...  10.6 us
    pallas_call x2, Pallas kernels, produce(): call(produce_kernel, (columns // block,), [pl.BlockSpec((slot_count, unit...  9.15 us
    pallas_call x1, Pallas kernels, forward_hidden(): call(forward_hidden_kernel, (count,), [pl.BlockSpec((slot_count, width),...  9.11 us
  transfers between devices with their start and end apart: 10, of which 6 were waited for; matrix products, arithmetic and copies ran while one was open for 3% of the time, Pallas kernels for 23%

profile of v5, /device:TPU:0, one launch (start us, length us, event | category | flops | bytes accessed | tf_op | source)
XLA Modules:
  0.0 216.7 jit_solution(1331193857876612133)
XLA Ops:
  0.6 5.1 %shard_map.112 = (bf16[384,7168]{1,0:T(8,128)(2,1)S(1)}, bf16[384,3584]{1,0:T(8,128)(2,1)}, s32[4,128]{1,0:T(4,128)}) custom-call(s32[2,128]{1,0:T(2,128)} %bitcast.55, s32[2,128]{1,0:T(2,128)} %bitcast.85, bf16[128,3584]{1,0:T(8,128)(2,1)} %bitcast.68, bf16[128,3584]{1,0:T(8,128)(2,1)} %bitcast.49, bf16[128,3584]{1,0:T(8,128)(2,1)} %bitcast.69), custom_call_target="tpu_custom_call" | custom-call | flops 1000 | bytes 1000 | tf_op jit(solution)/shard_map/pallas_call | solution.py:139
  5.7 72.4 %all_to_all.53 = bf16[16,24,7168]{2,1,0:T(8,128)(2,1)} all-to-all(bf16[16,24,7168]{2,1,0:T(8,128)(2,1)S(1)} %bitcast.47), channel_id=1, replica_groups={{0,5,10,15,1,6,11,12,2,7,8,13,3,4,9,14},{16,21,26,31,17,22,27,28,18,23,..., dimensions={0} | all-to-all | bytes 11010048 | tf_op jit(solution)/shard_map/all_to_all | solution.py:35
  78.2 3.7 %all-to-all-start.1 = ((bf16[16,24,3584]{2,1,0:T(8,128)(2,1)}), bf16[16,24,3584]{2,1,0:T(8,128)(2,1)S(1)}, u32[]{:S(2)}, u32[]{:S(2)}) async-start(bf16[16,24,3584]{2,1,0:T(8,128)(2,1)} %bitcast.71), calls=%async_computation.1 | async-start | bytes 5505024 | tf_op jit(solution)/shard_map/all_to_all | solution.py:35
  81.9 1.2 broadcast_select_fusion
  83.2 0.0 collective-permute-start.2
  83.2 15.0 %shard_map.116 = (bf16[384,1024]{1,0:T(8,128)(2,1)S(1)}, bf16[384,1024]{1,0:T(8,128)(2,1)S(1)}, f32[384,128]{1,0:T(8,128)S(1)}) custom-call(bf16[384,7168]{1,0:T(8,128)(2,1)} %bitcast.66, bf16[384,7168]{1,0:T(8,128)(2,1)} %bitcast.67, bf16[3584,2048]{1,0:T(8,128)(2,1)} %bitcast.58, bf16[3584,2048]{1,0:T(8,128)(2,1)} %bitcast.59, bf16[1024,3584]{1,0:T(8,128)(2,1)} %bitcast.63), custom_call_target="tpu_custom_call" | custom-call | flops 1000 | bytes 1000 | tf_op jit(solution)/shard_map/pallas_call | solution.py:191
  98.2 0.0 collective-permute-done.2.refs_0_.residual
  98.2 10.6 %shard_map.117 = bf16[384,3712]{1,0:T(8,128)(2,1)S(1)} custom-call(bf16[384,1024]{1,0:T(8,128)(2,1)S(1)} %get-tuple-element.25.gate_grad, bf16[384,1024]{1,0:T(8,128)(2,1)S(1)} %get-tuple-element.26.up_grad, bf16[3584,2048]{1,0:T(8,128)(2,1)} %bitcast.60, f32[384,128]{1,0:T(8,128)S(1)} %get-tuple-element.27.dots, ...), custom_call_target="tpu_custom_call" | custom-call | flops 1000 | bytes 1000 | tf_op jit(solution)/shard_map/pallas_call | solution.py:237
  108.8 0.0 copy-start
  108.8 1.6 copy-done
  110.4 1.0 copy-done.3
  111.4 5.8 %all-to-all-done.1 = bf16[16,24,3584]{2,1,0:T(8,128)(2,1)S(1)} async-done(((bf16[16,24,3584]{2,1,0:T(8,128)(2,1)}), bf16[16,24,3584]{2,1,0:T(8,128)(2,1)S(1)}, u32[]{:S(2)}, u32[]{:S(2)}) %all-to-all-start.1) | async-done | bytes 2752544 | tf_op jit(solution)/shard_map/all_to_all | solution.py:35
  117.2 1.6 copy-done.1
  118.8 6.5 %all-to-all-start.2 = ((bf16[16,24,3712]{2,1,0:T(8,128)(2,1)}), bf16[16,24,3712]{2,1,0:T(8,128)(2,1)S(1)}, u32[]{:S(2)}, u32[]{:S(2)}) async-start(bf16[16,24,3712]{2,1,0:T(8,128)(2,1)} %bitcast.45), calls=%async_computation.2 | async-start | bytes 5701632 | tf_op jit(solution)/shard_map/all_to_all | solution.py:35
  125.3 1.8 copy-done.2
  127.1 9.1 %shard_map.113.hidden = bf16[384,1024]{1,0:T(8,128)(2,1)S(1)} custom-call(bf16[384,3584]{1,0:T(8,128)(2,1)S(1)} %bitcast.46, bf16[3584,2048]{1,0:T(8,128)(2,1)} %bitcast.61, bf16[3584,2048]{1,0:T(8,128)(2,1)} %bitcast.62), custom_call_target="tpu_custom_call" | custom-call | flops 1000 | bytes 1000 | tf_op jit(solution)/shard_map/pallas_call | solution.py:263
  136.2 4.5 %shard_map.114.refs_0_ = bf16[384,1536]{1,0:T(8,128)(2,1)} custom-call(bf16[384,1024]{1,0:T(8,128)(2,1)S(1)} %shard_map.113.hidden, bf16[1024,3584]{1,0:T(8,128)(2,1)} %bitcast.64), custom_call_target="tpu_custom_call" | custom-call | flops 1000 | bytes 1000 | tf_op jit(solution)/shard_map/pallas_call | solution.py:282
  140.8 4.6 %shard_map.115 = bf16[384,2048]{1,0:T(8,128)(2,1)} custom-call(bf16[384,1024]{1,0:T(8,128)(2,1)S(1)} %shard_map.113.hidden, bf16[1024,3584]{1,0:T(8,128)(2,1)} %bitcast.65, bf16[384,1536]{1,0:T(8,128)(2,1)} %shard_map.114.refs_0_), custom_call_target="tpu_custom_call" | custom-call | flops 1000 | bytes 1000 | tf_op jit(solution)/shard_map/pallas_call | solution.py:282
  145.4 0.0 collective-permute-start.4
  145.4 1.6 collective-permute-start.1
  147.0 0.0 copy-done.8
  147.0 0.3 fusion.8
  147.4 13.4 %all-to-all-done.2 = bf16[16,24,3712]{2,1,0:T(8,128)(2,1)S(1)} async-done(((bf16[16,24,3712]{2,1,0:T(8,128)(2,1)}), bf16[16,24,3712]{2,1,0:T(8,128)(2,1)S(1)}, u32[]{:S(2)}, u32[]{:S(2)}) %all-to-all-start.2) | async-done | bytes 2850848 | tf_op jit(solution)/shard_map/all_to_all | solution.py:35
  160.8 0.3 shard_map.118.logit_pair
  161.0 0.9 copy-done.12
  161.9 0.3 fusion.6
  162.2 0.2 reshape.65
  162.6 0.0 collective-permute-done.4
  162.6 7.2 %all-to-all-start.4 = ((bf16[16,24,1536]{2,1,0:T(8,128)(2,1)}), bf16[16,24,1536]{2,1,0:T(8,128)(2,1)}, u32[]{:S(2)}, u32[]{:S(2)}) async-start(bf16[16,24,1536]{2,1,0:T(8,128)(2,1)} %bitcast.23), calls=%async_computation.4 | async-start | bytes 2359296 | tf_op jit(solution)/shard_map/all_to_all | solution.py:35
  169.8 9.5 %collective-permute-done.1 = bf16[384,2048]{1,0:T(8,128)(2,1)} collective-permute-done((bf16[384,2048]{1,0:T(8,128)(2,1)}, bf16[384,2048]{1,0:T(8,128)(2,1)}, u32[]{:S(2)}, u32[]{:S(2)}) %collective-permute-start.1) | collective-permute-done | bytes 1572896 | tf_op jit(solution)/shard_map/ppermute | solution.py:18
  179.4 2.8 %fusion.1 = bf16[16,24,2304]{2,1,0:T(8,128)(2,1)} fusion(bf16[16,16,224]{2,1,0:T(8,128)(2,1)S(1)} %constant_dynamic-update-slice_fusion, bf16[16,24,2048]{2,1,0:T(8,128)(2,1)} %bitcast.16), kind=kLoop, calls=%fused_computation.2 | loop fusion | flops 5308416 | bytes 3457024 | tf_op jit(solution)/shard_map/concatenate | solution.py:542
  182.2 4.1 %all-to-all-done.4 = bf16[16,24,1536]{2,1,0:T(8,128)(2,1)} async-done(((bf16[16,24,1536]{2,1,0:T(8,128)(2,1)}), bf16[16,24,1536]{2,1,0:T(8,128)(2,1)}, u32[]{:S(2)}, u32[]{:S(2)}) %all-to-all-start.4) | async-done | bytes 1179680 | tf_op jit(solution)/shard_map/all_to_all | solution.py:35
  186.3 4.4 %all-to-all-start.3 = ((bf16[16,24,2304]{2,1,0:T(8,128)(2,1)}), bf16[16,24,2304]{2,1,0:T(8,128)(2,1)}, u32[]{:S(2)}, u32[]{:S(2)}) async-start(bf16[16,24,2304]{2,1,0:T(8,128)(2,1)} %fusion.1), calls=%async_computation.3 | async-start | bytes 3538944 | tf_op jit(solution)/shard_map/all_to_all | solution.py:35
  190.8 0.0 copy-start.7
  190.8 1.2 copy-done.7
  192.0 2.2 shard_map.120
  194.2 0.0 collective-permute-start.5
  194.2 0.3 fusion.4
  194.6 0.1 select_reduce_fusion.1
  194.7 0.5 collective-permute-start
  195.2 2.5 %collective-permute-start.3 = (f32[224,16]{0,1:T(8,128)S(1)}, f32[224,16]{0,1:T(8,128)S(1)}, u32[]{:S(2)}, u32[]{:S(2)}) collective-permute-start(f32[224,16]{0,1:T(8,128)S(1)} %bitcast.87), channel_id=1, source_target_pairs={{0,112},{16,96},{32,80},{48,64},{64,48},{80,32},{96,16},{112,0},{1... | collective-permute-start | bytes 43016 | tf_op jit(solution)/shard_map/ppermute | solution.py:544
  197.7 7.6 %collective-permute-done.5.rows = bf16[128,3584]{1,0:T(8,128)(2,1)S(1)} collective-permute-done((bf16[128,3584]{1,0:T(8,128)(2,1)S(1)}, bf16[128,3584]{1,0:T(8,128)(2,1)S(1)}, u32[]{:S(2)}, u32[]{:S(2)}) %collective-permute-start.5) | collective-permute-done | bytes 917536 | tf_op jit(solution)/shard_map/ppermute | solution.py:18
  205.3 1.0 shard_map.121.grads
  206.3 0.0 collective-permute-done.mixer
  206.3 3.3 %shard_map.119.early = bf16[128,3584]{1,0:T(8,128)(2,1)} custom-call(bf16[384,128]{1,0:T(8,128)(2,1)S(1)} %collective-permute-done.mixer, bf16[384,1536]{1,0:T(8,128)(2,1)} %bitcast.24.rows, bf16[128,3584]{1,0:T(8,128)(2,1)S(1)} %copy-done.4), custom_call_target="tpu_custom_call" | custom-call | flops 1000 | bytes 1000 | tf_op jit(solution)/shard_map/pallas_call | solution.py:309
  209.6 0.0 collective-permute-done.3
  209.6 4.4 %all-to-all-done.3 = bf16[16,24,2304]{2,1,0:T(8,128)(2,1)} async-done(((bf16[16,24,2304]{2,1,0:T(8,128)(2,1)}), bf16[16,24,2304]{2,1,0:T(8,128)(2,1)}, u32[]{:S(2)}, u32[]{:S(2)}) %all-to-all-start.3) | async-done | bytes 1769504 | tf_op jit(solution)/shard_map/all_to_all | solution.py:35
  214.0 2.7 %shard_map.122 = (bf16[128,3584]{1,0:T(8,128)(2,1)}, f32[16,224]{1,0:T(8,128)}) custom-call(bf16[384,128]{1,0:T(8,128)(2,1)S(1)} %collective-permute-done.mixer, bf16[384,2304]{1,0:T(8,128)(2,1)} %bitcast.21.rows.parts, bf16[128,3584]{1,0:T(8,128)(2,1)S(1)} %copy-done.5, bf16[384,2304]{1,0:T(8,128)(2,1)} %bitcast.21.rows.parts, ...), custom_call_target="tpu_custom_call", output_to_operand_aliasing={{0}: (5, {})} | custom-call | flops 1000 | bytes 1000 | tf_op jit(solution)/shard_map/pallas_call | solution.py:348
  (46 shorter events, 0.4 us)
Async XLA Ops:
  78.2 39.0 %all-to-all-start.1 = ((bf16[16,24,3584]{2,1,0:T(8,128)(2,1)}), bf16[16,24,3584]{2,1,0:T(8,128)(2,1)S(1)}, u32[]{:S(2)}, u32[]{:S(2)}) async-start(bf16[16,24,3584]{2,1,0:T(8,128)(2,1)} %bitcast.71), calls=%async_computation.1 | async-start | bytes 5505024 | tf_op jit(solution)/shard_map/all_to_all | solution.py:35
  83.2 15.1 %collective-permute-start.2 = (bf16[128,3584]{1,0:T(8,128)(2,1)S(1)}, bf16[128,3584]{1,0:T(8,128)(2,1)S(1)}, u32[]{:S(2)}, u32[]{:S(2)}) collective-permute-start(bf16[128,3584]{1,0:T(8,128)(2,1)S(1)} %broadcast_select_fusion), channel_id=1, source_target_pairs={{0,16},{16,32},{32,48},{48,64},{64,80},{80,96},{96,112},{112,0},{1... | collective-permute-start | bytes 2752520 | tf_op jit(solution)/shard_map/ppermute | solution.py:18
  108.8 1.6 copy-start
  110.4 1.0 copy-start.3
  117.2 1.6 copy-start.1
  118.8 42.0 %all-to-all-start.2 = ((bf16[16,24,3712]{2,1,0:T(8,128)(2,1)}), bf16[16,24,3712]{2,1,0:T(8,128)(2,1)S(1)}, u32[]{:S(2)}, u32[]{:S(2)}) async-start(bf16[16,24,3712]{2,1,0:T(8,128)(2,1)} %bitcast.45), calls=%async_computation.2 | async-start | bytes 5701632 | tf_op jit(solution)/shard_map/all_to_all | solution.py:35
  125.3 1.8 copy-start.2
  140.7 6.2 %copy-start.8 = (bf16[1,3584,16]{1,2,0:T(8,128)(2,1)S(1)}, bf16[1,3584,16]{1,2,0:T(8,128)(2,1)}, u32[]{:S(2)}) copy-start(bf16[1,3584,16]{1,2,0:T(8,128)(2,1)} %param.16) | copy-start | bytes 344068
  140.7 6.2 %copy-start.11 = (bf16[1,128,3584]{2,1,0:T(8,128)(2,1)S(1)}, bf16[1,128,3584]{2,1,0:T(8,128)(2,1)}, u32[]{:S(2)}) copy-start(bf16[1,128,3584]{2,1,0:T(8,128)(2,1)} %param.11) | copy-start | bytes 2752516
  140.7 6.5 %copy-start.9 = (s32[1,128,2]{1,2,0:T(2,128)S(1)}, s32[1,128,2]{1,2,0:T(2,128)}, u32[]{:S(2)}) copy-start(s32[1,128,2]{1,2,0:T(2,128)} %param.12) | copy-start | bytes 3076
  140.7 20.0 %copy-start.10 = (s32[4,128]{1,0:T(4,128)S(1)}, s32[4,128]{1,0:T(4,128)}, u32[]{:S(2)}) copy-start(s32[4,128]{1,0:T(4,128)} %get-tuple-element.21.slots) | copy-start | bytes 6148
  145.4 17.2 %collective-permute-start.4 = (bf16[384,1536]{1,0:T(8,128)(2,1)}, bf16[384,1536]{1,0:T(8,128)(2,1)}, u32[]{:S(2)}, u32[]{:S(2)}) collective-permute-start(bf16[384,1536]{1,0:T(8,128)(2,1)} %shard_map.114.refs_0_), channel_id=1, source_target_pairs={{0,16},{16,32},{32,48},{48,64},{64,80},{80,96},{96,112},{112,0},{1... | collective-permute-start | bytes 3538952 | tf_op jit(solution)/shard_map/ppermute | solution.py:18
  145.4 34.0 %collective-permute-start.1 = (bf16[384,2048]{1,0:T(8,128)(2,1)}, bf16[384,2048]{1,0:T(8,128)(2,1)}, u32[]{:S(2)}, u32[]{:S(2)}) collective-permute-start(bf16[384,2048]{1,0:T(8,128)(2,1)} %shard_map.115), channel_id=1, source_target_pairs={{0,16},{16,32},{32,48},{48,64},{64,80},{80,96},{96,112},{112,0},{1... | collective-permute-start | bytes 4718600 | tf_op jit(solution)/shard_map/ppermute | solution.py:18
  160.8 1.2 copy-start.12
  162.6 23.7 %all-to-all-start.4 = ((bf16[16,24,1536]{2,1,0:T(8,128)(2,1)}), bf16[16,24,1536]{2,1,0:T(8,128)(2,1)}, u32[]{:S(2)}, u32[]{:S(2)}) async-start(bf16[16,24,1536]{2,1,0:T(8,128)(2,1)} %bitcast.23), calls=%async_computation.4 | async-start | bytes 2359296 | tf_op jit(solution)/shard_map/all_to_all | solution.py:35
  186.3 27.7 %all-to-all-start.3 = ((bf16[16,24,2304]{2,1,0:T(8,128)(2,1)}), bf16[16,24,2304]{2,1,0:T(8,128)(2,1)}, u32[]{:S(2)}, u32[]{:S(2)}) async-start(bf16[16,24,2304]{2,1,0:T(8,128)(2,1)} %fusion.1), calls=%async_computation.3 | async-start | bytes 3538944 | tf_op jit(solution)/shard_map/all_to_all | solution.py:35
  190.8 1.2 copy-start.7
  192.0 2.2 %copy-start.13 = (bf16[1,128,3584]{2,1,0:T(8,128)(2,1)S(1)}, bf16[1,128,3584]{2,1,0:T(8,128)(2,1)}, u32[]{:S(2)}) copy-start(bf16[1,128,3584]{2,1,0:T(8,128)(2,1)} %param.9) | copy-start | bytes 2752516
  192.0 2.5 %copy-start.14 = (s32[1,128,2]{1,2,0:T(2,128)S(1)}, s32[1,128,2]{1,2,0:T(2,128)}, u32[]{:S(2)}) copy-start(s32[1,128,2]{1,2,0:T(2,128)} %param.10) | copy-start | bytes 3076
  192.0 3.2 %copy-start.15 = (f32[1,224,16]{1,2,0:T(8,128)S(1)}, f32[1,224,16]{1,2,0:T(8,128)}, u32[]{:S(2)}) copy-start(f32[1,224,16]{1,2,0:T(8,128)} %param.17) | copy-start | bytes 43012
  192.0 14.3 %copy-start.4 = (bf16[128,3584]{1,0:T(8,128)(2,1)S(1)}, bf16[128,3584]{1,0:T(8,128)(2,1)}, u32[]{:S(2)}) copy-start(bf16[128,3584]{1,0:T(8,128)(2,1)} %copy-done.3) | copy-start | bytes 2752516
  194.2 11.1 %collective-permute-start.5 = (bf16[128,3584]{1,0:T(8,128)(2,1)S(1)}, bf16[128,3584]{1,0:T(8,128)(2,1)S(1)}, u32[]{:S(2)}, u32[]{:S(2)}) collective-permute-start(bf16[128,3584]{1,0:T(8,128)(2,1)S(1)} %shard_map.120), channel_id=1, source_target_pairs={{0,112},{16,0},{32,16},{48,32},{64,48},{80,64},{96,80},{112,96},{1... | collective-permute-start | bytes 2752520 | tf_op jit(solution)/shard_map/ppermute | solution.py:18
  194.5 19.5 %copy-start.5 = (bf16[128,3584]{1,0:T(8,128)(2,1)S(1)}, bf16[128,3584]{1,0:T(8,128)(2,1)}, u32[]{:S(2)}) copy-start(bf16[128,3584]{1,0:T(8,128)(2,1)} %copy-done.3) | copy-start | bytes 2752516
  194.7 11.6 %collective-permute-start = (bf16[384,128]{1,0:T(8,128)(2,1)S(1)}, bf16[384,128]{1,0:T(8,128)(2,1)S(1)}, u32[]{:S(2)}, u32[]{:S(2)}) collective-permute-start(bf16[384,128]{1,0:T(8,128)(2,1)S(1)} %select_reduce_fusion.1), channel_id=1, source_target_pairs={{0,16},{16,32},{32,48},{48,64},{64,80},{80,96},{96,112},{112,0},{1... | collective-permute-start | bytes 294920 | tf_op jit(solution)/shard_map/ppermute | solution.py:18
  195.2 14.4 %collective-permute-start.3 = (f32[224,16]{0,1:T(8,128)S(1)}, f32[224,16]{0,1:T(8,128)S(1)}, u32[]{:S(2)}, u32[]{:S(2)}) collective-permute-start(f32[224,16]{0,1:T(8,128)S(1)} %bitcast.87), channel_id=1, source_target_pairs={{0,112},{16,96},{32,80},{48,64},{64,48},{80,32},{96,16},{112,0},{1... | collective-permute-start | bytes 43016 | tf_op jit(solution)/shard_map/ppermute | solution.py:544
  206.3 7.7 %copy-start.6 = (bf16[128,3584]{1,0:T(8,128)(2,1)S(1)}, bf16[128,3584]{1,0:T(8,128)(2,1)}, u32[]{:S(2)}) copy-start(bf16[128,3584]{1,0:T(8,128)(2,1)} %shard_map.121.grads) | copy-start | bytes 2752516
